TPU v7x, 32 devices: a whole 2x2x4 slice. The times are simulated.
32 devices in a mesh: ctx: 8 (over z, x), fsdp: 4 (over y, core).
Axes of the slice: x: 2, y: 2, z: 4, core: 2. Of those that a mesh axis runs over, the one named last changes fastest.
Arguments:
- inputs: bfloat16 [4, 2048, 2048], P('fsdp', 'ctx'), may hold values from -6 to 6
- norm_gain: float32 [2048], replicated, may hold values from 0.1 to 1.9
- norm_shift: float32 [2048], replicated, may hold values from -2 to 2
- qkv_weight: bfloat16 [2048, 6144], P('fsdp'), may hold values from -0.125 to 0.125
- qkv_bias: float32 [6144], replicated, may hold values from -2 to 2
- out_weight: bfloat16 [2048, 2048], P('fsdp'), may hold values from -0.25 to 0.25
- out_bias: float32 [2048], replicated, may hold values from -2 to 2
- up_weight: bfloat16 [2048, 8192], P('fsdp'), may hold values from -0.125 to 0.125
- up_bias: float32 [8192], replicated, may hold values from -2 to 2
- down_weight: bfloat16 [8192, 2048], P('fsdp'), may hold values from -0.0625 to 0.0625
- down_bias: float32 [2048], replicated, may hold values from -2 to 2
- cotangent: bfloat16 [4, 2048, 2048], P('fsdp', 'ctx'), may hold values from -6 to 6
Outputs:
- output: bfloat16 [4, 2048, 2048], P('fsdp', 'ctx')
- input_grad: bfloat16 [4, 2048, 2048], P('fsdp', 'ctx')
- gain_grad: float32 [2048], replicated
- shift_grad: float32 [2048], replicated
- qkv_weight_grad: float32 [2048, 6144], P(('fsdp', 'ctx'))
- qkv_bias_grad: float32 [6144], replicated
- out_weight_grad: float32 [2048, 2048], P(('fsdp', 'ctx'))
- out_bias_grad: float32 [2048], replicated
- up_weight_grad: float32 [2048, 8192], P(('fsdp', 'ctx'))
- up_bias_grad: float32 [8192], replicated
- down_weight_grad: float32 [8192, 2048], P(('fsdp', 'ctx'))
- down_bias_grad: float32 [2048], replicated
All inputs are finite; a program needn't handle non-finite values.
Results may differ from a plain program's by a relative error of at most 0.012.
Values may be sent and summed in bfloat16 or wider, within the bound.
A program may use at most 704 MiB of HBM per device.

v0:
```python
from functools import partial

import jax
import jax.numpy as jnp
from jax import lax
from jax.sharding import PartitionSpec as P

HD = 64
ROT = 32


EPS = 1e-05
ROOT = 0.7978845608028654
CUBIC = 0.044715


def tables(positions):
    quarter = ROT // 2
    inverse = 10000.0 ** (-jnp.arange(quarter, dtype=jnp.float32) * 2.0 / ROT)
    angle = positions.astype(jnp.float32)[:, None] * inverse[None, :]
    return (jnp.cos(angle)[:, None, :], jnp.sin(angle)[:, None, :])


def rotate(heads, cosine, sine):
    quarter = ROT // 2
    first = heads[..., :quarter]
    second = heads[..., quarter:ROT]
    return jnp.concatenate(
        [first * cosine - second * sine, second * cosine + first * sine, heads[..., ROT:]], axis=-1
    )


def unrotate(grads, cosine, sine):
    quarter = ROT // 2
    first = grads[..., :quarter]
    second = grads[..., quarter:ROT]
    return jnp.concatenate(
        [first * cosine + second * sine, second * cosine - first * sine, grads[..., ROT:]], axis=-1
    )


def gelu_value(value):
    return 0.5 * value * (1.0 + jnp.tanh(ROOT * (value + CUBIC * value * value * value)))


def gelu_slope(value):
    tangent = jnp.tanh(ROOT * (value + CUBIC * value * value * value))
    return 0.5 * (1.0 + tangent) + 0.5 * value * (1.0 - tangent * tangent) * ROOT * (
        1.0 + 3.0 * CUBIC * value * value
    )


def keep_state(state):
    return state


def sweep(step, carry, place, shards, half):

    def sweep_per_shard(shard, state):
        for upper in range(2):
            key_index = shard if upper == 0 else 2 * shards - 1 - shard
            key_start = shard * 2 * half + upper * half
            key_pos = key_index * half + jnp.arange(half, dtype=jnp.int32)
            for lower in range(2):
                query_index = place if lower == 0 else 2 * shards - 1 - place
                query_pos = query_index * half + jnp.arange(half, dtype=jnp.int32)
                allowed = key_pos[None, :] <= query_pos[:, None]
                state = lax.cond(
                    key_index <= query_index,
                    partial(step, which=lower, start=key_start, allowed=allowed),
                    keep_state,
                    state,
                )
        return state

    return lax.fori_loop(0, shards, sweep_per_shard, carry)


def owner_sweep(step, carry, place, shards, half):

    def owner_per_shard(shard, state):
        for lower in range(2):
            query_index = shard if lower == 0 else 2 * shards - 1 - shard
            query_pos = query_index * half + jnp.arange(half, dtype=jnp.int32)
            for upper in range(2):
                key_index = place if upper == 0 else 2 * shards - 1 - place
                key_pos = key_index * half + jnp.arange(half, dtype=jnp.int32)
                allowed = key_pos[None, :] <= query_pos[:, None]
                state = lax.cond(
                    key_index <= query_index,
                    partial(step, shard=shard, lower=lower, upper=upper, allowed=allowed),
                    keep_state,
                    state,
                )
        return state

    return lax.fori_loop(0, shards, owner_per_shard, carry)


def contract_rows(left, right):
    return lax.dot_general(
        left, right, (((0,), (0,)), ((), ())), preferred_element_type=jnp.float32
    )


def contract_cols(left, right):
    return lax.dot_general(
        left, right, (((1,), (1,)), ((), ())), preferred_element_type=jnp.float32
    )


def on_device(
    inputs,
    norm_gain,
    norm_shift,
    qkv_weight,
    qkv_bias,
    out_weight,
    out_bias,
    up_weight,
    up_bias,
    down_weight,
    down_bias,
    cotangent,
):
    rows = inputs.shape[1]
    width = inputs.shape[2]
    hidden_width = up_weight.shape[1]
    half = rows // 2
    heads = width // HD
    scale = HD ** (-0.5)
    shards = lax.axis_size("ctx")
    groups = lax.axis_size("fsdp")
    place = lax.axis_index("ctx")
    tokens = inputs[0].astype(jnp.float32)
    mean = jnp.mean(tokens, axis=-1, keepdims=True)
    centred = tokens - mean
    inv_scale = lax.rsqrt(jnp.mean(centred * centred, axis=-1, keepdims=True) + EPS)
    normal = centred * inv_scale
    flat = (normal * norm_gain + norm_shift).astype(jnp.bfloat16)
    pieces = (
        lax.all_gather(qkv_weight, "fsdp", axis=0, tiled=True),
        lax.all_gather(up_weight, "fsdp", axis=0, tiled=True),
    )
    left = flat
    qkv_sum = jnp.dot(left, pieces[0], preferred_element_type=jnp.float32)
    up_sum = jnp.dot(left, pieces[1], preferred_element_type=jnp.float32)
    up_rows = up_sum + up_bias
    local = jnp.arange(rows, dtype=jnp.int32)
    blocks = jnp.where(local < half, place, 2 * shards - 1 - place)
    positions = blocks * half + local % half
    cosine, sine = tables(positions)
    split = (qkv_sum + qkv_bias).reshape(rows, 3, heads, HD)
    queries = rotate(split[:, 0], cosine, sine).astype(jnp.bfloat16)
    keys = rotate(split[:, 1], cosine, sine).astype(jnp.bfloat16)
    values = split[:, 2].astype(jnp.bfloat16)
    query_halves = queries.reshape(2, half, heads, HD)
    all_keys, all_values = (
        lax.all_gather(keys.reshape(rows, width), "ctx", axis=0, tiled=True),
        lax.all_gather(values.reshape(rows, width), "ctx", axis=0, tiled=True),
    )

    def block_scores(which, start, allowed, key_source):
        key_block = lax.dynamic_slice_in_dim(key_source, start, half, 0).reshape(half, heads, HD)
        raw = (
            jnp.einsum(
                "qhd,khd->hqk", query_halves[which], key_block, preferred_element_type=jnp.float32
            )
            * scale
        )
        return (jnp.where(allowed[None], raw, -1e30), key_block)

    def stats_step(state, which, start, allowed):
        top, total = state
        scores, _ = block_scores(which, start, allowed, all_keys)
        new_top = jnp.maximum(top[which], jnp.max(scores, axis=-1))
        new_total = total[which] * jnp.exp(top[which] - new_top) + jnp.sum(
            jnp.exp(scores - new_top[..., None]), axis=-1
        )
        return (top.at[which].set(new_top), total.at[which].set(new_total))

    top_init = jnp.full((2, heads, half), -1e30, jnp.float32)
    total_init = jnp.zeros((2, heads, half), jnp.float32)
    top, total = sweep(stats_step, (top_init, total_init), place, shards, half)
    log_total = top + jnp.log(total)

    def value_step(state, which, start, allowed):
        scores, _ = block_scores(which, start, allowed, all_keys)
        probs = jnp.exp(scores - log_total[which][..., None]).astype(jnp.bfloat16)
        value_block = lax.dynamic_slice_in_dim(all_values, start, half, 0).reshape(half, heads, HD)
        return state.at[which].add(
            jnp.einsum("hqk,khd->qhd", probs, value_block, preferred_element_type=jnp.float32)
        )

    mixed = sweep(value_step, jnp.zeros((2, half, heads, HD), jnp.float32), place, shards, half)
    attended = mixed.reshape(rows, width).astype(jnp.bfloat16)
    left = attended
    attn_sum = jnp.dot(
        left,
        lax.all_gather(out_weight, "fsdp", axis=0, tiled=True),
        preferred_element_type=jnp.float32,
    )
    hidden = gelu_value(up_rows).astype(jnp.bfloat16)
    left = hidden
    mlp_sum = jnp.dot(
        left,
        lax.all_gather(down_weight, "fsdp", axis=0, tiled=True),
        preferred_element_type=jnp.float32,
    )
    result = tokens + attn_sum + out_bias + mlp_sum + down_bias
    grad_low = cotangent[0]
    grad_full = grad_low.astype(jnp.float32)
    out_full, down_full = (
        lax.all_gather(out_weight, "fsdp", axis=0, tiled=True),
        lax.all_gather(down_weight, "fsdp", axis=0, tiled=True),
    )
    grad_attended = contract_cols(grad_low, out_full).astype(jnp.bfloat16)
    grad_hidden = contract_cols(grad_low, down_full)
    grad_up = (grad_hidden * gelu_slope(up_rows)).astype(jnp.bfloat16)
    out_grads = grad_attended.reshape(2, half, heads, HD)
    delta = jnp.transpose(jnp.sum(out_grads.astype(jnp.float32) * mixed, axis=-1), (0, 2, 1))
    back_keys, back_values = (
        lax.all_gather(keys.reshape(rows, width), "ctx", axis=0, tiled=True),
        lax.all_gather(values.reshape(rows, width), "ctx", axis=0, tiled=True),
    )
    grad_q_init = jnp.zeros((2, half, heads, HD), jnp.float32)

    def query_step(grad_q, which, start, allowed):
        scores, key_block = block_scores(which, start, allowed, back_keys)
        value_block = lax.dynamic_slice_in_dim(back_values, start, half, 0).reshape(half, heads, HD)
        probs = jnp.exp(scores - log_total[which][..., None])
        grad_probs = jnp.einsum(
            "qhd,khd->hqk", out_grads[which], value_block, preferred_element_type=jnp.float32
        )
        grad_scores = (probs * (grad_probs - delta[which][..., None])).astype(jnp.bfloat16)
        return grad_q.at[which].add(
            jnp.einsum("hqk,khd->qhd", grad_scores, key_block, preferred_element_type=jnp.float32)
            * scale
        )

    grad_q = sweep(query_step, grad_q_init, place, shards, half)
    far_queries, far_grads = (
        lax.all_gather(queries.reshape(rows, width), "ctx", axis=0, tiled=True),
        lax.all_gather(grad_attended, "ctx", axis=0, tiled=True),
    )
    far_log, far_delta = (
        lax.all_gather(log_total, "ctx", axis=0, tiled=True),
        lax.all_gather(delta, "ctx", axis=0, tiled=True),
    )
    key_halves = keys.reshape(2, half, heads, HD)
    value_halves = values.reshape(2, half, heads, HD)

    def owner_step(state, shard, lower, upper, allowed):
        row_start = shard * rows + lower * half
        slot = shard * 2 + lower
        query_block = lax.dynamic_slice_in_dim(far_queries, row_start, half, 0).reshape(
            half, heads, HD
        )
        grad_block = lax.dynamic_slice_in_dim(far_grads, row_start, half, 0).reshape(
            half, heads, HD
        )
        log_block = lax.dynamic_index_in_dim(far_log, slot, 0, keepdims=False)
        delta_block = lax.dynamic_index_in_dim(far_delta, slot, 0, keepdims=False)
        raw = (
            jnp.einsum(
                "qhd,khd->hqk", query_block, key_halves[upper], preferred_element_type=jnp.float32
            )
            * scale
        )
        scores = jnp.where(allowed[None], raw, -1e30)
        probs = jnp.exp(scores - log_block[..., None])
        grad_probs = jnp.einsum(
            "qhd,khd->hqk", grad_block, value_halves[upper], preferred_element_type=jnp.float32
        )
        grad_scores = (probs * (grad_probs - delta_block[..., None])).astype(jnp.bfloat16)
        grad_k = (
            jnp.einsum("hqk,qhd->khd", grad_scores, query_block, preferred_element_type=jnp.float32)
            * scale
        )
        grad_v = jnp.einsum(
            "hqk,qhd->khd",
            probs.astype(jnp.bfloat16),
            grad_block,
            preferred_element_type=jnp.float32,
        )
        addition = jnp.concatenate(
            [grad_k.reshape(half, width), grad_v.reshape(half, width)], axis=1
        )
        return state.at[upper].add(addition)

    own_init = jnp.zeros((2, half, 2 * width), jnp.float32)
    own_kv = owner_sweep(owner_step, own_init, place, shards, half).reshape(rows, 2 * width)
    grad_queries = unrotate(grad_q.reshape(rows, heads, HD), cosine, sine)
    grad_keys = unrotate(own_kv[:, :width].reshape(rows, heads, HD), cosine, sine)
    grad_qkv = jnp.concatenate(
        [grad_queries.reshape(rows, width), grad_keys.reshape(rows, width), own_kv[:, width:]],
        axis=1,
    ).astype(jnp.bfloat16)
    pieces = lax.all_gather((qkv_weight, up_weight), "fsdp", axis=0, tiled=True)
    grad_normed = contract_cols(grad_qkv, pieces[0]) + contract_cols(grad_up, pieces[1])
    grad_normal = grad_normed * norm_gain
    grad_tokens = inv_scale * (
        grad_normal
        - jnp.mean(grad_normal, axis=-1, keepdims=True)
        - normal * jnp.mean(grad_normal * normal, axis=-1, keepdims=True)
    )
    input_grad = (grad_full + grad_tokens).astype(jnp.bfloat16)
    gain_grad, shift_grad, qkv_bias_grad, out_bias_grad, up_bias_grad = lax.psum(
        (
            jnp.sum(grad_normed * normal, axis=0),
            jnp.sum(grad_normed, axis=0),
            jnp.sum(grad_qkv.astype(jnp.float32), axis=0),
            jnp.sum(grad_full, axis=0),
            jnp.sum(grad_up.astype(jnp.float32), axis=0),
        ),
        ("ctx", "fsdp"),
    )
    both_in = jnp.concatenate([grad_qkv, grad_up], axis=1)
    both_out = jnp.concatenate([attended, hidden], axis=1)
    width_group = width // groups
    hidden_group = hidden_width // groups
    out_rows = width_group + hidden_group
    in_part = lax.psum_scatter(
        contract_rows(flat, both_in), "fsdp", scatter_dimension=0, tiled=True
    )
    virtual = jnp.arange(out_rows * lax.axis_size("fsdp"), dtype=jnp.int32)
    owner = virtual // out_rows
    inner = virtual % out_rows
    column = jnp.where(
        inner < width_group,
        owner * width_group + inner,
        width + owner * hidden_group + inner - width_group,
    )
    out_part = lax.psum_scatter(
        contract_rows(jnp.take(both_out, column, axis=1), grad_low),
        "fsdp",
        scatter_dimension=0,
        tiled=True,
    )
    pieces = (
        lax.psum_scatter(in_part[:, : 3 * width], "ctx", scatter_dimension=0, tiled=True),
        lax.psum_scatter(in_part[:, 3 * width :], "ctx", scatter_dimension=0, tiled=True),
        lax.psum_scatter(out_part[:width_group], "ctx", scatter_dimension=0, tiled=True),
        lax.psum_scatter(out_part[width_group:], "ctx", scatter_dimension=0, tiled=True),
    )
    qkv_weight_grad, up_weight_grad, out_weight_grad, down_weight_grad = pieces
    return (
        result.astype(jnp.bfloat16)[None],
        input_grad[None],
        gain_grad,
        shift_grad,
        qkv_weight_grad,
        qkv_bias_grad,
        out_weight_grad,
        out_bias_grad,
        up_weight_grad,
        up_bias_grad,
        down_weight_grad,
        out_bias_grad,
    )


def solution(mesh):
    in_specs = (
        P("fsdp", "ctx", None),
        P(),
        P(),
        P("fsdp", None),
        P(),
        P("fsdp", None),
        P(),
        P("fsdp", None),
        P(),
        P("fsdp", None),
        P(),
        P("fsdp", "ctx", None),
    )
    out_specs = (
        P("fsdp", "ctx", None),
        P("fsdp", "ctx", None),
        P(),
        P(),
        P(("fsdp", "ctx"), None),
        P(),
        P(("fsdp", "ctx"), None),
        P(),
        P(("fsdp", "ctx"), None),
        P(),
        P(("fsdp", "ctx"), None),
        P(),
    )
    return jax.shard_map(
        on_device, mesh=mesh, in_specs=in_specs, out_specs=out_specs, check_vma=False
    )
```

profile of v0, /device:TPU:0, one launch (start us, length us, event | category | flops | bytes accessed | tf_op | source)
XLA Modules:
  0.0 4318.4 jit_solution(12765744746342240059)
XLA Ops:
  10.7 156.4 %all-gather.9.cloned.1.call-done = bf16[2048,6144]{1,0:T(8,128)(2,1)} async-done(((bf16[512,6144]{1,0:T(8,128)(2,1)}), bf16[2048,6144]{1,0:T(8,128)(2,1)}) %all-gather.9.cloned.1.call-update) | async-done | bytes 25165840 | tf_op jit(solution)/shard_map/all_gather | solution.py:142
  167.1 13.7 convolution_add_fusion.1
  196.1 30.9 all-gather.15.cloned.1.call-done
  237.1 193.0 %all-gather.17.cloned.1.call-done = bf16[2048,8192]{1,0:T(8,128)(2,1)} async-done(((bf16[512,8192]{1,0:T(8,128)(2,1)}), bf16[2048,8192]{1,0:T(8,128)(2,1)}) %all-gather.17.cloned.1.call-update) | async-done | bytes 33554448 | tf_op jit(solution)/shard_map/all_gather | solution.py:143
  430.2 19.8 multiply_convert_fusion.4
  449.9 108.1 %all-gather.13.cloned.1.call-done = bf16[2048,2048]{0,1:T(8,128)(2,1)} async-done(((bf16[256,2048]{0,1:T(8,128)(2,1)}), bf16[2048,2048]{0,1:T(8,128)(2,1)}) %all-gather.13.cloned.1.call-update) | async-done | bytes 8388624 | tf_op jit(solution)/shard_map/all_gather | solution.py:159
  558.0 40.0 while.90
  598.1 86.0 %all-gather.11.cloned.1.call-done = bf16[2048,2048]{0,1:T(8,128)(2,1)} async-done(((bf16[256,2048]{0,1:T(8,128)(2,1)}), bf16[2048,2048]{0,1:T(8,128)(2,1)}) %all-gather.11.cloned.1.call-update) | async-done | bytes 8388624 | tf_op jit(solution)/shard_map/all_gather | solution.py:160
  684.4 80.7 %while.91 = (s32[]{:T(128)}, f32[2,128,32,64]{1,3,2,0:T(8,128)S(1)}, s32[]{:T(128)}, s32[]{:T(128)}, s32[]{:T(128)}, /*index=5*/bf16[2048,2048]{0,1:T(8,128)(2,1...) while((s32[]{:T(128)}, ...), condition=%wide.region_29.30_spmd, body=%wide.region_20.29_spmd.sunk | while | flops 546374144 | bytes 23795400 | solution.py:76
  782.9 41.9 gather_fusion
  824.8 35.4 fusion.238
  887.5 123.6 %all-gather.19.cloned.1.call-done = bf16[8192,2048]{1,0:T(8,128)(2,1)} async-done(((bf16[2048,2048]{1,0:T(8,128)(2,1)}), bf16[8192,2048]{1,0:T(8,128)(2,1)}) %all-gather.19.cloned.1.call-update) | async-done | bytes 33554448 | tf_op jit(solution)/shard_map/all_gather | solution.py:207
  1011.1 22.3 convert_reduce_fusion
  1038.1 35.9 all_gather.43
  1074.0 34.0 all_gather.45
  1108.0 37.6 all-gather.21.cloned.1.call-done
  1147.9 218.1 %while.93 = (s32[]{:T(128)}, f32[2,128,4096]{1,2,0:T(8,128)}, s32[]{:T(128)}, s32[]{:T(128)}, s32[]{:T(128)}, /*index=5*/bf16[2048,2048]{0,1:T(8,128)(2,1)}, bf1...) while((s32[]{:T(128)}, f32[2,128,4096]{1,2,0:T(8,128)}, ...), condition=%wide.region_50.51_spmd, body=%wide.region_41.50_spmd.sunk | while | flops 1093730816 | bytes 122558832 | solution.py:97
  1212.3 13.0 conditional.44
  1263.6 12.9 conditional.44
  1379.1 126.6 %while.92 = (s32[]{:T(128)}, f32[2,128,32,64]{1,3,2,0:T(8,128)}, s32[]{:T(128)}, s32[]{:T(128)}, s32[]{:T(128)}, /*index=5*/bf16[2048,2048]{0,1:T(8,128)(2,1)}, ...) while((s32[]{:T(128)}, f32[2,128,32,64]{1,3,2,0:T(8,128)}, ...), condition=%wide.region_40.41_spmd, body=%wide.region_31.40_spmd.sunk | while | flops 820052480 | bytes 53352328 | solution.py:76
  1521.4 43.2 fusion.230
  1566.5 13.9 fusion.263
  1580.4 19.4 fusion.259
  1605.0 909.6 %all-reduce.5.cloned.1.call-done = f32[10240,2048]{1,0:T(8,128)} async-done(((f32[10240,2048]{1,0:T(8,128)}), f32[10240,2048]{1,0:T(8,128)}) %all-reduce.5.cloned.1.call-update) | async-done | bytes 83886096
  2519.3 14.4 constant_dynamic-slice_fusion.29
  2533.8 760.8 %reduce-scatter.6.cloned.1.call-done = f32[512,14336]{1,0:T(8,128)} async-done(((f32[2048,14336]{1,0:T(8,128)}), f32[512,14336]{1,0:T(8,128)}) %reduce-scatter.6.cloned.1.call-update) | async-done | bytes 29360144 | tf_op jit(solution)/shard_map/reduce_scatter | solution.py:323
  3324.4 16.5 fusion.253
  3340.9 84.8 %all-reduce.7.cloned.1.call-done = (f32[2048]{0:T(1024)}, f32[2048]{0:T(1024)}, f32[6144]{0:T(1024)}, f32[2048]{0:T(1024)}, f32[8192]{0:T(1024)}) async-done(((f32[2048]{0:T(1024)}, f32[2048]{0:T(1024)}, f32[6144]{0:T(1024)}, f32[2048]{0:T(1024)}, f32[8192]{0:T(1024)}), (f32[2048]{0:T(1024)}, f32[2048]{0:T(1024)}, f32[6144]{0:T(1024)}, f32[2048]{0:T(1024)}, f32[8192]{0:T(1024)})) %all-reduce.7.cloned.1.call-update) | async-done | bytes 81936 | tf_op jit(solution)/shard_map/psum | solution.py:308
  3425.7 93.9 %reduce-scatter.10.cloned.1.call-done = f32[64,2048]{1,0:T(8,128)} async-done(((f32[512,2048]{1,0:T(8,128)}), f32[64,2048]{1,0:T(8,128)}) %reduce-scatter.10.cloned.1.call-update) | async-done | bytes 524304 | tf_op jit(solution)/shard_map/reduce_scatter | solution.py:343
  3519.6 286.8 %reduce-scatter.14.cloned.1.call-done = f32[256,2048]{1,0:T(8,128)} async-done(((f32[2048,2048]{1,0:T(8,128)}), f32[256,2048]{1,0:T(8,128)}) %reduce-scatter.14.cloned.1.call-update) | async-done | bytes 2097168 | tf_op jit(solution)/shard_map/reduce_scatter | solution.py:344
  3806.4 210.8 %reduce-scatter.8.cloned.1.call-done = f32[64,6144]{1,0:T(8,128)} async-done(((f32[512,6144]{1,0:T(8,128)}), f32[64,6144]{1,0:T(8,128)}) %reduce-scatter.8.cloned.1.call-update) | async-done | bytes 1572880 | tf_op jit(solution)/shard_map/reduce_scatter | solution.py:341
  4017.3 286.5 %reduce-scatter.12.cloned.1.call-done = f32[64,8192]{1,0:T(8,128)} async-done(((f32[512,8192]{1,0:T(8,128)}), f32[64,8192]{1,0:T(8,128)}) %reduce-scatter.12.cloned.1.call-update) | async-done | bytes 2097168 | tf_op jit(solution)/shard_map/reduce_scatter | solution.py:342
  (965 shorter events, 1051.3 us)
Async XLA Ops:
  7.2 160.0 %all-gather.9.cloned.1.call-start = ((), (), s32[]{:S(2)}) async-start(), calls=%async_computation.5 | async-start | bytes 31457280 | tf_op jit(solution)/shard_map/all_gather | solution.py:142
  7.9 219.1 %all-gather.15.cloned.1.call-start = ((), (), s32[]{:S(2)}) async-start(), calls=%async_computation.8 | async-start | bytes 10485760 | tf_op jit(solution)/shard_map/all_gather | solution.py:200
  8.7 421.5 %all-gather.17.cloned.1.call-start = ((), (), s32[]{:S(2)}) async-start(), calls=%async_computation.9 | async-start | bytes 41943040 | tf_op jit(solution)/shard_map/all_gather | solution.py:143
  9.4 157.7 %copy-start.40 = (f32[2048]{0:T(1024)S(1)}, f32[2048]{0:T(1024)}, u32[]{:S(2)}) copy-start(f32[2048]{0:T(1024)} %param.93) | copy-start | bytes 24580
  9.4 157.7 %copy-start.42 = (f32[2048]{0:T(1024)S(1)}, f32[2048]{0:T(1024)}, u32[]{:S(2)}) copy-start(f32[2048]{0:T(1024)} %param.94) | copy-start | bytes 24580
  9.4 157.7 %copy-start.54 = (f32[6144]{0:T(1024)S(1)}, f32[6144]{0:T(1024)}, u32[]{:S(2)}) copy-start(f32[6144]{0:T(1024)} %param.96) | copy-start | bytes 73732
  9.4 548.6 %all-gather.13.cloned.1.call-start = ((), (), s32[]{:S(2)}) async-start(), calls=%async_computation.7 | async-start | bytes 9437184 | tf_op jit(solution)/shard_map/all_gather | solution.py:159
  10.1 420.0 %copy-start.44 = (f32[256]{0:T(256)}, f32[256]{0:T(256)S(1)}, u32[]{:S(2)}) copy-start(f32[256]{0:T(256)S(1)} %broadcast_multiply_fusion.2) | copy-start | bytes 3076
  10.6 419.6 %copy-start.46 = (f32[256]{0:T(256)}, f32[256]{0:T(256)S(1)}, u32[]{:S(2)}) copy-start(f32[256]{0:T(256)S(1)} %add_rsqrt_fusion) | copy-start | bytes 3076
  10.7 179.6 %copy-start.48 = (f32[256,16]{0,1:T(8,128)}, f32[256,16]{0,1:T(8,128)S(1)}, u32[]{:S(2)}) copy-start(f32[256,16]{0,1:T(8,128)S(1)} %get-tuple-element.1902) | copy-start | bytes 49156
  10.7 179.6 %copy-start.50 = (f32[256,16]{0,1:T(8,128)}, f32[256,16]{0,1:T(8,128)S(1)}, u32[]{:S(2)}) copy-start(f32[256,16]{0,1:T(8,128)S(1)} %get-tuple-element.1903) | copy-start | bytes 49156
  193.1 33.9 copy-start.25
  193.2 490.9 %all-gather.11.cloned.1.call-start = ((), (), s32[]{:S(2)}) async-start(), calls=%async_computation.6 | async-start | bytes 9437184 | tf_op jit(solution)/shard_map/all_gather | solution.py:160
  196.0 669.5 %all-gather.23.cloned.1.call-start = ((), (), s32[]{:S(2)}) async-start(), calls=%async_computation.12 | async-start | bytes 9437184 | tf_op jit(solution)/shard_map/all_gather | solution.py:244
  233.8 777.3 %all-gather.19.cloned.1.call-start = ((), (), s32[]{:S(2)}) async-start(), calls=%async_computation.10 | async-start | bytes 41943040 | tf_op jit(solution)/shard_map/all_gather | solution.py:207
  234.5 195.6 %copy-start.53 = (f32[8192]{0:T(1024)S(1)}, f32[8192]{0:T(1024)}, u32[]{:S(2)}) copy-start(f32[8192]{0:T(1024)} %param.100) | copy-start | bytes 98308
  234.5 911.0 %all-gather.21.cloned.1.call-start = ((), (), s32[]{:S(2)}) async-start(), calls=%async_computation.11 | async-start | bytes 9437184 | tf_op jit(solution)/shard_map/all_gather | solution.py:243
  235.3 2279.4 %all-reduce.5.cloned.1.call-start = ((), (), s32[]{:S(2)}) async-start(), calls=%async_computation.18 | async-start | bytes 167772160
  782.9 41.9 copy-start.26
  860.2 2434.4 %reduce-scatter.6.cloned.1.call-start = ((), (), s32[]{:S(2)}) async-start(), calls=%async_computation.13 | async-start | bytes 146800640 | tf_op jit(solution)/shard_map/reduce_scatter | solution.py:323
  864.2 13.7 copy-start.19
  865.5 14.1 copy-start.32
  1516.7 4.7 copy-start.15
  1516.7 4.7 copy-start.18
  1516.7 4.7 copy-start.41
  1564.6 1861.0 %all-reduce.7.cloned.1.call-start = ((), (), s32[]{:S(2)}) async-start(), calls=%async_computation.19 | async-start | bytes 163840 | tf_op jit(solution)/shard_map/psum | solution.py:308
  1604.9 1914.7 %reduce-scatter.10.cloned.1.call-start = ((), (), s32[]{:S(2)}) async-start(), calls=%async_computation.15 | async-start | bytes 4718592 | tf_op jit(solution)/shard_map/reduce_scatter | solution.py:343
  2519.3 1287.2 %reduce-scatter.14.cloned.1.call-start = ((), (), s32[]{:S(2)}) async-start(), calls=%async_computation.17 | async-start | bytes 18874368 | tf_op jit(solution)/shard_map/reduce_scatter | solution.py:344
  2533.7 1483.5 %reduce-scatter.8.cloned.1.call-start = ((), (), s32[]{:S(2)}) async-start(), calls=%async_computation.14 | async-start | bytes 14155776 | tf_op jit(solution)/shard_map/reduce_scatter | solution.py:341
  3305.3 998.5 %reduce-scatter.12.cloned.1.call-start = ((), (), s32[]{:S(2)}) async-start(), calls=%async_computation.16 | async-start | bytes 18874368 | tf_op jit(solution)/shard_map/reduce_scatter | solution.py:342
  3318.4 5.9 copy-start.28
  3318.4 5.9 copy-start.55
  (92 other events, 173.4 us)
Sparse Core Ops, SparseCore 0:
  9.6 157.4 all-gather.8
  168.7 58.2 all-gather.14
  228.6 201.5 all-gather.16
  432.6 125.3 all-gather.12
  560.5 123.5 all-gather.10
  686.7 123.0 all-gather.22
  811.3 199.7 all-gather.18
  1013.7 131.8 all-gather.20
  1148.1 1366.5 all-reduce.4
  2517.1 777.4 reduce-scatter.5
  3303.3 122.3 all-reduce.6
  3430.2 89.3 reduce-scatter.9
  3524.0 282.4 reduce-scatter.13
  3810.9 206.3 reduce-scatter.7
  4021.9 281.7 reduce-scatter.11
where the time goes:
time: 4330 us; the launch traced here: 4320 us
  waiting for transfers between devices  3370 us (78%)
  matrix products  415 us (10%)
  local copies, waits for them, and re-layouts  344 us (8%)
  other arithmetic  94.8 us (2%)
  blocking collectives  69.9 us (2%)
    unnamed x16, waiting for transfers between devices  913 us
    reduce_scatter x1, waiting for transfers between devices, on_device(): lax.psum_scatter(contract_rows(flat, both_in), 'fsdp', scatter_dimension=...  761 us
    reduce_scatter x1, waiting for transfers between devices, on_device(): lax.psum_scatter(out_part[width_group:], 'ctx', scatter_dimension=0, tile...  287 us
    reduce_scatter x1, waiting for transfers between devices, on_device(): lax.psum_scatter(in_part[:, 3 * width:], 'ctx', scatter_dimension=0, tile...  287 us
    reduce_scatter x1, waiting for transfers between devices, on_device(): lax.psum_scatter(in_part[:, :3 * width], 'ctx', scatter_dimension=0, tile...  211 us
    all_gather x1, waiting for transfers between devices, on_device(): lax.all_gather(up_weight, 'fsdp', axis=0, tiled=True)  193 us
    all_gather x1, waiting for transfers between devices, on_device(): lax.all_gather(qkv_weight, 'fsdp', axis=0, tiled=True)  156 us
    all_gather x1, waiting for transfers between devices, on_device(): lax.all_gather(down_weight, 'fsdp', axis=0, tiled=True)  124 us
  transfers between devices with their start and end apart: 15, of which 14 were waited for; matrix products, arithmetic and copies ran while one was open for 19% of the time, Pallas kernels for 0%

commit v1 on v0

v1 whole, which is shorter than its diff:
```python
from functools import partial

import jax
import jax.numpy as jnp
from jax import lax
from jax.experimental import pallas as pl
from jax.experimental.pallas import tpu as pltpu
from jax.sharding import PartitionSpec as P

HD = 64
ROT = 32
LANES = 128

EPS = 1e-05
ROOT = 0.7978845608028654
CUBIC = 0.044715
F32 = jnp.float32
BF16 = jnp.bfloat16


def gelu_value(value):
    return 0.5 * value * (1.0 + jnp.tanh(ROOT * (value + CUBIC * value * value * value)))


def gelu_slope(value):
    tangent = jnp.tanh(ROOT * (value + CUBIC * value * value * value))
    return 0.5 * (1.0 + tangent) + 0.5 * value * (1.0 - tangent * tangent) * ROOT * (
        1.0 + 3.0 * CUBIC * value * value
    )


def contract_rows(left, right):
    return lax.dot_general(left, right, (((0,), (0,)), ((), ())), preferred_element_type=F32)


def contract_cols(left, right):
    return lax.dot_general(left, right, (((1,), (1,)), ((), ())), preferred_element_type=F32)


def matmul(left, right):
    return jnp.dot(left, right, preferred_element_type=F32)


def swap(value, axis, bit):
    size = lax.axis_size(axis)
    return lax.ppermute(value, axis, [(i, i ^ bit) for i in range(size)])


def rotary(positions):
    quarter = ROT // 2
    inverse = 10000.0 ** (-jnp.arange(quarter, dtype=F32) * 2.0 / ROT)
    angle = positions.astype(F32)[:, None] * inverse[None, :]
    cosine, sine = jnp.cos(angle), jnp.sin(angle)
    rest = positions.shape[0], HD - ROT
    one = jnp.concatenate([cosine, cosine, jnp.ones(rest, F32)], axis=1)
    two = jnp.concatenate([-sine, sine, jnp.zeros(rest, F32)], axis=1)
    return jnp.tile(one, (1, LANES // HD)), jnp.tile(two, (1, LANES // HD))


def turn(rows, cosine, sine):
    lane = lax.broadcasted_iota(jnp.int32, rows.shape, 1) % HD
    quarter = ROT // 2
    other = jnp.where(
        lane < quarter,
        pltpu.roll(rows, LANES - quarter, 1),
        pltpu.roll(rows, quarter, 1),
    )
    return rows * cosine + other * sine


def qkv_kernel(pieces, rows_ref, *refs):
    weights = refs[:pieces]
    bias_ref, cos_ref, sin_ref, out_ref = refs[pieces:]
    part = pl.program_id(0)
    depth = weights[0].shape[0]
    acc = bias_ref[0]
    for j in range(pieces):
        acc = acc + jnp.dot(
            rows_ref[:, j * depth : (j + 1) * depth],
            weights[j][...],
            preferred_element_type=F32,
        )
    cosine, sine = cos_ref[...], sin_ref[...]
    for h in range(out_ref.shape[0]):
        cols = acc[:, h * LANES : (h + 1) * LANES]
        turned = turn(cols, cosine, sine)
        out_ref[h, 0, 0, 0] = jnp.where(part < 2, turned, cols).astype(out_ref.dtype)


def project(rows, weights, bias, cosine, sine, groups, per_group):
    tokens = cosine.shape[0]
    slots = rows.shape[0] // tokens
    width = rows.shape[1]
    part_cols = bias.shape[1]
    pairs = part_cols // LANES
    pieces = len(weights)
    depth = width // pieces
    return pl.pallas_call(
        partial(qkv_kernel, pieces),
        grid=(3, slots),
        out_shape=jax.ShapeDtypeStruct((pairs, groups, per_group, 3, tokens, LANES), BF16),
        in_specs=[pl.BlockSpec((tokens, width), lambda p, s: (s, 0))]
        + [pl.BlockSpec((depth, part_cols), lambda p, s: (0, p))] * pieces
        + [
            pl.BlockSpec((1, 1, part_cols), lambda p, s: (p, 0, 0)),
            pl.BlockSpec((tokens, LANES), lambda p, s: (0, 0)),
            pl.BlockSpec((tokens, LANES), lambda p, s: (0, 0)),
        ],
        out_specs=pl.BlockSpec(
            (pairs, 1, 1, 1, tokens, LANES),
            lambda p, s: (0, s // per_group, s % per_group, p, 0, 0),
        ),
        compiler_params=pltpu.CompilerParams(vmem_limit_bytes=40 * 2**20),
        cost_estimate=pl.CostEstimate(
            flops=2 * rows.shape[0] * width * part_cols * 3,
            bytes_accessed=30 * 2**20,
            transcendentals=0,
        ),
    )(rows, *weights, bias.reshape(3, 1, part_cols), cosine, sine)


def attend_kernel(
    shards, heads, dup, qkv_ref, do_ref, cos_ref, sin_ref, out_ref, s_buf, dp_buf, dk_buf, dv_buf
):
    half = qkv_ref.shape[-2]
    block = 2 * half
    count = shards
    base = lax.axis_index("ctx") % dup
    lane = lax.broadcasted_iota(jnp.int32, (block, LANES), 1) // HD
    own = [lane == (base + h) for h in range(heads)]
    scale = HD**-0.5

    def where_is(item):
        low = item < count // 2
        first = jnp.where(low, 2 * item, 2 * count - 1 - 2 * item)
        second = jnp.where(low, 2 * item + 1, 2 * count - 2 - 2 * item)
        return first, second, jnp.where(low, 0, 1)

    def load(part, item):
        first, second, side = where_is(item)
        return jnp.concatenate(
            [qkv_ref[first, 0, part, side], qkv_ref[second, 0, part, side]], axis=0
        )

    def load_do(item):
        first, second, side = where_is(item)
        return jnp.concatenate([do_ref[first, 0, side], do_ref[second, 0, side]], axis=0)

    def store(part, item, value):
        first, second, side = where_is(item)
        out_ref[first, 0, part, side] = value[:half].astype(out_ref.dtype)
        out_ref[second, 0, part, side] = value[half:].astype(out_ref.dtype)

    dk_buf[...] = jnp.zeros_like(dk_buf)
    dv_buf[...] = jnp.zeros_like(dv_buf)
    nothing = jnp.zeros((block, LANES), BF16)
    key_at = lax.broadcasted_iota(jnp.int32, (block, block), 0)
    query_at = lax.broadcasted_iota(jnp.int32, (block, block), 1)

    def per_query(item, _):
        query = load(0, item) * jnp.asarray(scale, BF16)
        grad = load_do(item)
        queries = [jnp.where(own[h], query, nothing) for h in range(heads)]
        grads = [jnp.where(own[h], grad, nothing) for h in range(heads)]

        def measure(key_item, state, diagonal):
            keys, values = load(1, key_item), load(2, key_item)
            new = []
            for h in range(heads):
                top, total, dot = state[h]
                s = contract_cols(keys, queries[h])
                if diagonal:
                    s = jnp.where(key_at <= query_at, s, -1e30)
                dp = contract_cols(values, grads[h])
                s_buf[h, key_item] = s
                dp_buf[h, key_item] = dp
                new_top = jnp.maximum(top, jnp.max(s, axis=0, keepdims=True))
                e = jnp.exp(s - new_top)
                fade = jnp.exp(top - new_top)
                new.append(
                    (
                        new_top,
                        total * fade + jnp.sum(e, axis=0, keepdims=True),
                        dot * fade + jnp.sum(e * dp, axis=0, keepdims=True),
                    )
                )
            return tuple(new)

        zero = jnp.zeros((1, block), F32)
        start = tuple((zero - 1e30, zero, zero) for _ in range(heads))
        state = lax.fori_loop(0, item, lambda k, st: measure(k, st, False), start)
        state = measure(item, state, True)
        logs = [top + jnp.log(total) for top, total, _ in state]
        deltas = [dot / total for _, total, dot in state]

        def apply(key_item, state):
            keys, values = load(1, key_item), load(2, key_item)
            out, dq = state
            dk, dv = dk_buf[key_item], dv_buf[key_item]
            for h in range(heads):
                p = jnp.exp(s_buf[h, key_item] - logs[h])
                ds = (p * (dp_buf[h, key_item] - deltas[h])).astype(BF16)
                p = p.astype(BF16)
                dv = dv + matmul(p, grads[h])
                dk = dk + matmul(ds, queries[h])
                out = out + jnp.where(own[h], contract_rows(p, values), 0.0)
                dq = dq + jnp.where(own[h], contract_rows(ds, keys), 0.0)
            dk_buf[key_item] = dk
            dv_buf[key_item] = dv
            return out, dq

        empty = jnp.zeros((block, LANES), F32)
        out, dq = lax.fori_loop(0, item + 1, apply, (empty, empty))
        store(0, item, out)
        rows = pl.ds(pl.multiple_of(item * block, block), block)
        store(1, item, turn(dq * scale, cos_ref[rows, :], -sin_ref[rows, :]))
        return 0

    lax.fori_loop(0, count, per_query, 0)

    def finish(item, _):
        rows = pl.ds(pl.multiple_of(item * block, block), block)
        store(2, item, turn(dk_buf[item], cos_ref[rows, :], -sin_ref[rows, :]))
        store(3, item, dv_buf[item])
        return 0

    lax.fori_loop(0, count, finish, 0)


def attend(qkv, grads, cosine, sine, heads, dup):
    shards, items = qkv.shape[:2]
    half = qkv.shape[-2]
    tokens = shards * 2 * half
    block = 2 * half
    once = pl.Buffered(1)
    pairs = shards * (shards + 1) // 2 * items * heads
    return pl.pallas_call(
        partial(attend_kernel, shards, heads, dup),
        grid=(items,),
        out_shape=jax.ShapeDtypeStruct((shards, items, 4, 2, half, LANES), BF16),
        in_specs=[
            pl.BlockSpec(
                (shards, 1, 3, 2, half, LANES), lambda i: (0, i, 0, 0, 0, 0), pipeline_mode=once
            ),
            pl.BlockSpec((shards, 1, 2, half, LANES), lambda i: (0, i, 0, 0, 0), pipeline_mode=once),
            pl.BlockSpec((tokens, LANES), lambda i: (0, 0), pipeline_mode=once),
            pl.BlockSpec((tokens, LANES), lambda i: (0, 0), pipeline_mode=once),
        ],
        out_specs=pl.BlockSpec(
            (shards, 1, 4, 2, half, LANES), lambda i: (0, i, 0, 0, 0, 0), pipeline_mode=once
        ),
        scratch_shapes=[
            pltpu.VMEM((heads, shards, block, block), F32),
            pltpu.VMEM((heads, shards, block, block), F32),
            pltpu.VMEM((shards, block, LANES), F32),
            pltpu.VMEM((shards, block, LANES), F32),
        ],
        compiler_params=pltpu.CompilerParams(vmem_limit_bytes=58 * 2**20),
        cost_estimate=pl.CostEstimate(
            flops=pairs * 5 * 2 * block * block * 256,
            bytes_accessed=16 * 2**20,
            transcendentals=2 * pairs * block * block,
        ),
    )(qkv, grads, cosine, sine)


def scatter_sum(parts, axis_at, place, bits):
    lead, tail = parts.shape[:axis_at], parts.shape[axis_at + 1 :]
    total = len(bits)
    left = list(range(total - 1, -1, -1))
    value = parts.reshape(lead + (2,) * total + tail)
    for bit in bits:
        at = axis_at + left.index(bit)
        left.remove(bit)
        mine = (place >> bit) & 1
        send = lax.dynamic_index_in_dim(value, 1 - mine, at, keepdims=False)
        keep = lax.dynamic_index_in_dim(value, mine, at, keepdims=False)
        got = swap(send.astype(BF16), "ctx", 1 << bit)
        value = keep.astype(F32) + got.astype(F32)
    return value


def gather_rows(own):
    far = swap(own, "fsdp", 2)
    pair = swap(jnp.stack([own, far]), "fsdp", 1)
    return [own, pair[0], far, pair[1]]


def scatter_rows(parts):
    near = swap(jnp.stack([parts[1], parts[3]]).astype(BF16), "fsdp", 1).astype(F32)
    mine = parts[0] + near[0]
    far = swap((parts[2] + near[1]).astype(BF16), "fsdp", 2)
    return mine + far.astype(F32)


def total_sum(value):
    for axis in ("fsdp", "ctx"):
        bit = 1
        while bit < lax.axis_size(axis):
            value = value + swap(value, axis, bit)
            bit *= 2
    return value


def on_device(
    inputs,
    norm_gain,
    norm_shift,
    qkv_weight,
    qkv_bias,
    out_weight,
    out_bias,
    up_weight,
    up_bias,
    down_weight,
    down_bias,
    cotangent,
):
    rows = inputs.shape[1]
    width = inputs.shape[2]
    hidden_width = up_weight.shape[1]
    half = rows // 2
    shards = lax.axis_size("ctx")
    groups = lax.axis_size("fsdp")
    place = lax.axis_index("ctx")
    member = lax.axis_index("fsdp")
    wide = width // groups
    deep = hidden_width // groups
    bits = shards.bit_length() - 1

    tokens = inputs[0].astype(F32)
    mean = jnp.mean(tokens, axis=-1, keepdims=True)
    centred = tokens - mean
    inv_scale = lax.rsqrt(jnp.mean(centred * centred, axis=-1, keepdims=True) + EPS)
    normal = centred * inv_scale
    flat = (normal * norm_gain + norm_shift).astype(BF16)

    def relative(value, axis):
        return [
            lax.dynamic_index_in_dim(value, member ^ j, axis, keepdims=False) for j in range(groups)
        ]

    flat_rel = jnp.stack(relative(flat.reshape(rows, groups, wide), 1))
    got = gather_rows(flat_rel)
    normed = jnp.concatenate(
        [
            jnp.concatenate([got[j][i ^ j] for i in range(groups)], axis=1)
            for j in range(groups)
        ],
        axis=0,
    )
    grad_low = cotangent[0]
    grads = jnp.concatenate(gather_rows(grad_low), axis=0)

    qkv_cols = qkv_weight.reshape(wide, 3, groups, wide)
    up_cols = up_weight.reshape(wide, groups, deep)
    qkv_pieces, up_pieces = [], []
    for j in range(groups):
        piece = lax.dynamic_index_in_dim(qkv_cols, member ^ j, 2, keepdims=False).reshape(
            wide, 3 * wide
        )
        qkv_pieces.append(swap(piece, "fsdp", j) if j else piece)
    for j in range(groups):
        piece = lax.dynamic_index_in_dim(up_cols, member ^ j, 1, keepdims=False)
        up_pieces.append(swap(piece, "fsdp", j) if j else piece)
    qkv_bias_own = lax.dynamic_index_in_dim(
        qkv_bias.reshape(3, groups, wide), member, 1, keepdims=False
    )
    up_bias_own = lax.dynamic_index_in_dim(up_bias.reshape(groups, deep), member, 0, keepdims=False)

    pairs = wide // LANES
    heads_in_pair = LANES // HD
    units = pairs * groups
    dup = max(1, shards // units)
    slot_groups = shards // (pairs * dup)
    per_group = groups // slot_groups
    heads = heads_in_pair // dup

    def spread(value):
        shape = value.shape
        if dup > 1:
            value = jnp.broadcast_to(
                value[:, :, None], shape[:2] + (dup,) + shape[2:]
            )
        return value.reshape((shards,) + shape[2:])

    local = jnp.arange(rows, dtype=jnp.int32)
    blocks = jnp.where(local < half, place, 2 * shards - 1 - place)
    cosine, sine = rotary(blocks * half + local % half)
    qkv_out = project(normed, qkv_pieces, qkv_bias_own, cosine, sine, slot_groups, per_group)
    qkv_in = lax.all_to_all(spread(qkv_out), "ctx", 0, 0)

    grad_att = contract_cols(grads, out_weight).astype(BF16)
    grad_att = grad_att.reshape(slot_groups, per_group, rows, pairs, LANES).transpose(3, 0, 1, 2, 4)
    grad_in = lax.all_to_all(spread(grad_att), "ctx", 0, 0)

    up_own = jnp.concatenate(up_pieces, axis=0)
    up_rows = matmul(normed, up_own) + up_bias_own
    hidden = gelu_value(up_rows).astype(BF16)
    grad_hidden = contract_cols(grads, down_weight)
    grad_up = (grad_hidden * gelu_slope(up_rows)).astype(BF16)
    down_grad = contract_rows(hidden, grads).astype(BF16)
    up_grad = contract_rows(normed, grad_up).astype(BF16)
    hw = deep // shards
    down_weight_grad = scatter_sum(
        down_grad.reshape(shards, hw, width), 0, place, list(range(bits))
    )
    up_part = scatter_sum(
        up_grad.reshape(groups, shards, wide // shards, deep), 1, place, list(range(bits))
    )

    full = jnp.arange(shards * rows, dtype=jnp.int32)
    cos_full, sin_full = rotary(full)
    back = attend(
        qkv_in.reshape(shards, per_group, 3, 2, half, LANES),
        grad_in.reshape(shards, per_group, 2, half, LANES),
        cos_full,
        sin_full,
        heads,
        dup,
    )
    back = lax.all_to_all(back, "ctx", 0, 0)
    back = back.reshape(pairs, slot_groups, dup, per_group, 4, rows, LANES)
    back = jnp.sum(back, axis=2) if dup > 1 else back[:, :, 0]
    back = back.transpose(3, 1, 2, 4, 0, 5).reshape(4, groups * rows, wide)
    attended = back[0]
    grad_qkv = jnp.concatenate([back[1], back[2], back[3]], axis=1)

    share = matmul(hidden, down_weight) + matmul(attended, out_weight)
    result = tokens + scatter_rows(list(share.reshape(groups, rows, width))) + out_bias + down_bias

    qkv_own = jnp.concatenate(qkv_pieces, axis=0)
    grad_share = contract_cols(grad_up, up_own) + contract_cols(grad_qkv, qkv_own)
    grad_share = grad_share.reshape(groups, rows, groups, wide)
    grad_share = [
        jnp.stack([grad_share[j, :, i ^ j] for i in range(groups)]) for j in range(groups)
    ]
    grad_normed = scatter_rows(grad_share)
    grad_normed = jnp.concatenate(relative(grad_normed, 0), axis=1)
    grad_full = grad_low.astype(F32)
    grad_normal = grad_normed * norm_gain
    grad_tokens = inv_scale * (
        grad_normal
        - jnp.mean(grad_normal, axis=-1, keepdims=True)
        - normal * jnp.mean(grad_normal * normal, axis=-1, keepdims=True)
    )
    input_grad = (grad_full + grad_tokens).astype(BF16)

    qkv_grad = contract_rows(normed, grad_qkv).astype(BF16)
    out_grad = contract_rows(attended, grads).astype(BF16)
    ow = wide // shards
    out_weight_grad = scatter_sum(out_grad.reshape(shards, ow, width), 0, place, list(range(bits)))
    qkv_part = scatter_sum(
        qkv_grad.reshape(groups, shards, ow, 3 * wide), 1, place, list(range(bits))
    )

    def exchange(part):
        part = part.astype(BF16)
        got = [part[0]] + [swap(part[j], "fsdp", j) for j in range(1, groups)]
        return relative(jnp.stack(got), 0)

    up_weight_grad = jnp.concatenate(exchange(up_part), axis=1).astype(F32)
    qkv_weight_grad = jnp.concatenate(
        [item.reshape(ow, 3, 1, wide) for item in exchange(qkv_part)], axis=2
    ).reshape(ow, 3 * width).astype(F32)

    qkv_bias_cols = jnp.sum(grad_qkv.astype(F32), axis=0).reshape(3, 1, wide)
    up_bias_cols = jnp.sum(grad_up.astype(F32), axis=0).reshape(1, deep)
    qkv_bias_all = lax.dynamic_update_slice(
        jnp.zeros((3, groups, wide), F32), qkv_bias_cols, (0, member, 0)
    ).reshape(-1)
    up_bias_all = lax.dynamic_update_slice(
        jnp.zeros((groups, deep), F32), up_bias_cols, (member, 0)
    ).reshape(-1)
    sums = total_sum(
        jnp.concatenate(
            [
                jnp.sum(grad_normed * normal, axis=0),
                jnp.sum(grad_normed, axis=0),
                jnp.sum(grad_full, axis=0),
                qkv_bias_all,
                up_bias_all,
            ]
        )
    )
    gain_grad = sums[:width]
    shift_grad = sums[width : 2 * width]
    out_bias_grad = sums[2 * width : 3 * width]
    qkv_bias_grad = sums[3 * width : 6 * width]
    up_bias_grad = sums[6 * width :]
    return (
        result.astype(BF16)[None],
        input_grad[None],
        gain_grad,
        shift_grad,
        qkv_weight_grad,
        qkv_bias_grad,
        out_weight_grad,
        out_bias_grad,
        up_weight_grad,
        up_bias_grad,
        down_weight_grad,
        out_bias_grad,
    )


def solution(mesh):
    in_specs = (
        P("fsdp", "ctx", None),
        P(),
        P(),
        P("fsdp", None),
        P(),
        P("fsdp", None),
        P(),
        P("fsdp", None),
        P(),
        P("fsdp", None),
        P(),
        P("fsdp", "ctx", None),
    )
    out_specs = (
        P("fsdp", "ctx", None),
        P("fsdp", "ctx", None),
        P(),
        P(),
        P(("fsdp", "ctx"), None),
        P(),
        P(("fsdp", "ctx"), None),
        P(),
        P(("fsdp", "ctx"), None),
        P(),
        P(("fsdp", "ctx"), None),
        P(),
    )
    return jax.shard_map(
        on_device, mesh=mesh, in_specs=in_specs, out_specs=out_specs, check_vma=False
    )
```

time: 4330 us -> 999 us (0.23)
  waiting for transfers between devices: 3370 us -> 407 us
  matrix products: 415 us -> 130 us
  local copies, waits for them, and re-layouts: 344 us -> 174 us
  Pallas kernels: 0 us -> 87.6 us
  blocking collectives: 69.9 us -> 0 us
  starting transfers between devices: 0.82 us -> 62.6 us
    reduce_scatter x5 -> x0, waiting for transfers between devices: 1640 us -> none  [the longest x1 761 us: on_device(): lax.psum_scatter(contract_rows(flat, both_in), 'fsdp', scatter_dimension=...]
    unnamed x16 -> x0, waiting for transfers between devices: 913 us -> none
    all_gather x8 -> x0, waiting for transfers between devices: 736 us -> none  [the longest x1 193 us: on_device(): lax.all_gather(up_weight, 'fsdp', axis=0, tiled=True)]
    ppermute x0 -> x37, waiting for transfers between devices: none -> 407 us  [swap(): return lax.ppermute(value, axis, [(i, i ^ bit) for i in range(size)])]
    dot_general x123 -> x3, matrix products: 275 us -> 32 us  [matmul(): return jnp.dot(left, right, preferred_element_type=F32)]
    pallas_call x0 -> x2, Pallas kernels: none -> 87.6 us  [the longest x1 72.8 us: attend(): pl.pallas_call(partial(attend_kernel, shards, heads, dup), grid=(items,),...]
    dynamic_slice x68 -> x16, local copies, waits for them, and re-layouts: 129 us -> 43.9 us  [the longest x5 22.8 us: on_device(): piece = lax.dynamic_index_in_dim(up_cols, member ^ j, 1, keepdims=False)]
    psum x1 -> x0, waiting for transfers between devices: 84.8 us -> none  [on_device(): lax.psum((jnp.sum(grad_normed * normal, axis=0), jnp.sum(grad_normed, axi...]
  transfers between devices with their start and end apart: 15 -> 40, of which waited for: 14 -> 14; matrix products, arithmetic and copies ran while one was open for 19% -> 34% of each run, Pallas kernels for 0% -> 9%
where the time goes in v1:
time: 999 us; the launch traced here: 988 us
  waiting for transfers between devices  407 us (41%)
  local copies, waits for them, and re-layouts  174 us (17%)
  matrix products  130 us (13%)
  other arithmetic  124 us (12%)
  Pallas kernels  87.6 us (9%)
  starting transfers between devices  62.6 us (6%)
    ppermute x37, waiting for transfers between devices, swap(): return lax.ppermute(value, axis, [(i, i ^ bit) for i in range(size)])  407 us
    pallas_call x1, Pallas kernels, attend(): pl.pallas_call(partial(attend_kernel, shards, heads, dup), grid=(items,),...  72.8 us
    concatenate x1, other arithmetic, on_device(): jnp.concatenate([jnp.concatenate([got[j][i ^ j] for i in range(groups)],...  57.1 us
    dot_general x4, matrix products, contract_cols(): lax.dot_general(left, right, (((1,), (1,)), ((), ())), preferred_element_...  54.3 us
    ppermute x37, starting transfers between devices, swap(): return lax.ppermute(value, axis, [(i, i ^ bit) for i in range(size)])  45.6 us
    dot_general x4, matrix products, contract_rows(): lax.dot_general(left, right, (((0,), (0,)), ((), ())), preferred_element_...  43.4 us
    unnamed x141, local copies, waits for them, and re-layouts  38 us
    dot_general x3, matrix products, matmul(): return jnp.dot(left, right, preferred_element_type=F32)  32 us
  transfers between devices with their start and end apart: 40, of which 14 were waited for; matrix products, arithmetic and copies ran while one was open for 34% of the time, Pallas kernels for 9%

profile of v1, /device:TPU:0, one launch (start us, length us, event | category | flops | bytes accessed | tf_op | source)
XLA Modules:
  0.0 987.8 jit_solution(13716892463059116808)
XLA Ops:
  15.1 8.7 copy.101
  39.5 12.0 %copy.96 = bf16[512,8192]{0,1:T(8,128)(2,1)} copy(bf16[512,8192]{1,0:T(8,128)(2,1)} %param.19) | data formatting | bytes 16777216 | tf_op args[7]
  51.5 6.9 constant_dynamic-slice_fusion.23
  106.7 6.5 all-to-all-start.1
  116.5 57.1 %maximum_maximum_fusion.rows_ref = bf16[1024,2048]{1,0:T(8,128)(2,1)S(1)} fusion(bf16[256,512]{1,0:T(8,128)(2,1)S(1)} %get-tuple-element.59, bf16[256,512]{1,0:T(8,128)(2,1)S(1)} %get-tuple-element.60, bf16[256,512]{1,0:T(8,128)(2,1)S(1)} %get-tuple-element.61, bf16[256,512]{1,0:T(8,128)(2,1)S(1)} %get-tuple-element.62, bf16[256,512]{1,0:T(8,128)(2,1)S(1)} %copy-done.37, ...), kind=kLoop, calls=%fused_computation.27 | loop fusion | flops 67108864 | bytes 8388608 | tf_op jit(solution)/shard_map/concatenate | solution.py:345
  173.8 14.4 %fusion.42 = f32[1024,2048]{1,0:T(8,128)} fusion(bf16[1024,2048]{1,0:T(8,128)(2,1)S(1)} %maximum_maximum_fusion.rows_ref, bf16[512,2048]{1,0:T(8,128)(2,1)} %collective-permute-done.4, bf16[512,2048]{1,0:T(8,128)(2,1)} %collective-permute-done.3, bf16[512,2048]{1,0:T(8,128)(2,1)} %collective-permute-done.2, bf16[512,2048]{1,0:T(8,128)(2,1)S(1)} %bitcast.337), kind=kOutput, calls=%fused_computation.97 | convolution fusion | flops 8623489024 | bytes 20971520 | tf_op jit(solution)/shard_map/dot_general | solution.py:41
  188.1 21.4 %convert_reduce_fusion = (f32[2048]{0:T(1024)S(1)}, bf16[1024,2048]{1,0:T(8,128)(2,1)}) fusion(f32[1024,2048]{1,0:T(8,128)} %fusion.42, f32[2048]{0:T(1024)S(1)} %bitcast.354, bf16[2048,2048]{1,0:T(8,128)(2,1)} %param.21, bf16[256,2048]{1,0:T(8,128)(2,1)} %copy-done.30, bf16[256,2048]{1,0:T(8,128)(2,1)} %collective-permute-done.8, ...), kind=kOutput, calls=%fused_computation.12 | convolution fusion | flops 8652847104 | bytes 25182208 | tf_op jit(solution)/shard_map/dot_general | solution.py:37
  209.6 12.0 %convolution_convert_fusion.1 = bf16[2048,2048]{1,0:T(8,128)(2,1)S(1)} fusion(bf16[1024,2048]{1,0:T(8,128)(2,1)} %copy-done.1, bf16[1024,2048]{1,0:T(8,128)(2,1)} %get-tuple-element.109), kind=kOutput, calls=%fused_computation.15 | convolution fusion | flops 8594128896 | bytes 16777216 | tf_op jit(solution)/shard_map/dot_general | solution.py:33
  229.8 14.7 %shard_map.211 = bf16[4,2,2,3,256,128]{5,4,3,2,1,0:T(8,128)(2,1)S(1)} custom-call(bf16[1024,2048]{1,0:T(8,128)(2,1)S(1)} %copy-done.2, bf16[512,1536]{1,0:T(8,128)(2,1)S(1)} %copy-done.5, bf16[512,1536]{1,0:T(8,128)(2,1)} %collective-permute-done.5.refs_1_, bf16[512,1536]{1,0:T(8,128)(2,1)} %collective-permute-done.6.refs_2_, ...), custom_call_target="tpu_custom_call" | custom-call | flops 6442450944 | bytes 31457280 | tf_op jit(solution)/shard_map/pallas_call | solution.py:98
  251.0 18.9 %convolution_convert_fusion = bf16[2048,2048]{1,0:T(8,128)(2,1)} fusion(f32[1024,2048]{1,0:T(8,128)} %fusion.42, f32[2048]{0:T(1024)S(1)} %bitcast.355, bf16[256,2048]{1,0:T(8,128)(2,1)} %copy-done.30, bf16[256,2048]{1,0:T(8,128)(2,1)} %collective-permute-done.8, bf16[256,2048]{1,0:T(8,128)(2,1)} %copy-done.28, bf16[256,2048]{1,0:T(8,128)(2,1)S(1)} %bitcast.310), kind=kOutput, calls=%fused_computation.14 | convolution fusion | flops 8631877632 | bytes 20979712 | tf_op jit(solution)/shard_map/dot_general | solution.py:33
  269.9 6.7 constant_dynamic-slice_fusion.1
  290.6 56.2 %collective-permute-done.28 = bf16[4,2,2,64,2048]{4,3,2,1,0:T(8,128)(2,1)} collective-permute-done((bf16[4,2,2,64,2048]{4,3,2,1,0:T(8,128)(2,1)}, bf16[4,2,2,64,2048]{4,3,2,1,0:T(8,128)(2,1)}, u32[]{:S(2)}, u32[]{:S(2)}) %collective-permute-start.28) | collective-permute-done | bytes 4194336 | tf_op jit(solution)/shard_map/ppermute | solution.py:46
  359.2 84.5 %collective-permute-done.34 = bf16[2,2,256,2048]{3,2,0,1:T(8,128)(2,1)} collective-permute-done((bf16[2,2,256,2048]{3,2,0,1:T(8,128)(2,1)}, bf16[2,2,256,2048]{3,2,0,1:T(8,128)(2,1)}, u32[]{:S(2)}, u32[]{:S(2)}) %collective-permute-start.34) | collective-permute-done | bytes 4194336 | tf_op jit(solution)/shard_map/ppermute | solution.py:46
  443.7 7.3 convert_add_fusion
  451.0 72.8 %shard_map.212 = bf16[8,2,4,2,128,128]{5,4,3,2,1,0:T(8,128)(2,1)} custom-call(bf16[8,2,3,2,128,128]{5,4,3,2,1,0:T(8,128)(2,1)} %bitcast.37.qkv_ref, bf16[8,2,2,128,128]{4,3,2,1,0:T(8,128)(2,1)} %bitcast.44.do_ref, f32[2048,128]{1,0:T(8,128)} %copy.109.cos_ref, f32[2048,128]{1,0:T(8,128)} %copy.110.sin_ref), custom_call_target="tpu_custom_call" | custom-call | flops 24159191040 | bytes 16777216 | tf_op jit(solution)/shard_map/pallas_call | solution.py:237
  543.2 122.1 %collective-permute-done.35 = bf16[2,256,2048]{2,1,0:T(8,128)(2,1)} collective-permute-done((bf16[2,256,2048]{2,1,0:T(8,128)(2,1)}, bf16[2,256,2048]{2,1,0:T(8,128)(2,1)}, u32[]{:S(2)}, u32[]{:S(2)}) %collective-permute-start.35) | collective-permute-done | bytes 2097184 | tf_op jit(solution)/shard_map/ppermute | solution.py:46
  671.9 11.9 %fusion.63 = f32[1024,2048]{1,0:T(8,128)} fusion(bf16[2048,2048]{1,0:T(8,128)(2,1)S(1)} %bitcast.359, f32[1024,2048]{1,0:T(8,128)S(1)} %bitcast.361, f32[2048]{0:T(1024)S(1)} %bitcast.356), kind=kOutput, calls=%fused_computation.230 | convolution fusion | flops 8610906112 | bytes 25174016 | tf_op jit(solution)/shard_map/dot_general | solution.py:41
  689.1 28.6 %collective-permute-done.36 = bf16[256,2048]{1,0:T(8,128)(2,1)} collective-permute-done((bf16[256,2048]{1,0:T(8,128)(2,1)}, bf16[256,2048]{1,0:T(8,128)(2,1)}, u32[]{:S(2)}, u32[]{:S(2)}) %collective-permute-start.36) | collective-permute-done | bytes 1048608 | tf_op jit(solution)/shard_map/ppermute | solution.py:46
  721.8 5.7 copy.180
  732.4 8.7 convolution_convert_fusion.2
  741.1 11.6 %fusion.7 = f32[1024,2048]{1,0:T(8,128)} fusion(bf16[1024,1536]{1,0:T(8,128)(2,1)S(1)} %bitcast_dynamic-update-slice_fusion, bf16[512,1536]{1,0:T(8,128)(2,1)} %collective-permute-done.7.refs_3_, bf16[512,1536]{1,0:T(8,128)(2,1)} %collective-permute-done.6.refs_2_, bf16[512,1536]{1,0:T(8,128)(2,1)} %collective-permute-done.5.refs_1_, ...), kind=kOutput, calls=%fused_computation.17 | convolution fusion | flops 6467616768 | bytes 17825792 | tf_op jit(solution)/shard_map/dot_general | solution.py:37
  752.7 16.7 %convolution_add_fusion.1 = f32[1024,2048]{1,0:T(8,128)} fusion(f32[1024,2048]{1,0:T(8,128)} %fusion.7, bf16[1024,2048]{1,0:T(8,128)(2,1)} %get-tuple-element.109, bf16[512,2048]{1,0:T(8,128)(2,1)} %collective-permute-done.4, bf16[512,2048]{1,0:T(8,128)(2,1)} %collective-permute-done.3, bf16[512,2048]{1,0:T(8,128)(2,1)} %collective-permute-done.2, ...), kind=kOutput, calls=%fused_computation.38 | convolution fusion | flops 8625586176 | bytes 29360128 | tf_op jit(solution)/shard_map/dot_general | solution.py:37
  769.4 11.0 %reshape.376 = f32[4,256,4,512]{3,2,1,0:T(4,128)} reshape(f32[1024,2048]{1,0:T(8,128)} %convolution_add_fusion.1) | data formatting | bytes 16777216 | tf_op jit(solution)/shard_map/reshape | solution.py:434
  780.4 5.8 copy.176
  786.3 5.9 copy.113
  805.5 5.8 fusion.68
  813.0 9.5 collective-permute-done.25
  830.1 6.4 collective-permute-done.26
  851.7 37.0 %collective-permute-done.19 = bf16[4,2,2,64,1536]{4,3,0,1,2:T(8,128)(2,1)} collective-permute-done((bf16[4,2,2,64,1536]{4,3,0,1,2:T(8,128)(2,1)}, bf16[4,2,2,64,1536]{4,3,0,1,2:T(8,128)(2,1)}, u32[]{:S(2)}, u32[]{:S(2)}) %collective-permute-start.19) | collective-permute-done | bytes 3145760 | tf_op jit(solution)/shard_map/ppermute | solution.py:46
  908.0 18.9 %collective-permute-done.20 = bf16[4,2,64,1536]{3,2,0,1:T(8,128)(2,1)S(1)} collective-permute-done((bf16[4,2,64,1536]{3,2,0,1:T(8,128)(2,1)S(1)}, bf16[4,2,64,1536]{3,2,0,1:T(8,128)(2,1)S(1)}, u32[]{:S(2)}, u32[]{:S(2)}) %collective-permute-start.20) | collective-permute-done | bytes 1572896 | tf_op jit(solution)/shard_map/ppermute | solution.py:46
  932.5 15.5 %collective-permute-done.17 = f32[20480]{0:T(1024)S(1)} collective-permute-done((f32[20480]{0:T(1024)S(1)}, f32[20480]{0:T(1024)S(1)}, u32[]{:S(2)}, u32[]{:S(2)}) %collective-permute-start.17) | collective-permute-done | bytes 81952 | tf_op jit(solution)/shard_map/ppermute | solution.py:46
  952.2 15.1 %collective-permute-done.18 = f32[20480]{0:T(1024)S(1)} collective-permute-done((f32[20480]{0:T(1024)S(1)}, f32[20480]{0:T(1024)S(1)}, u32[]{:S(2)}, u32[]{:S(2)}) %collective-permute-start.18) | collective-permute-done | bytes 81952 | tf_op jit(solution)/shard_map/ppermute | solution.py:46
  (342 shorter events, 249.1 us)
Async XLA Ops:
  0.7 27.3 %collective-permute-start.8 = (bf16[256,2048]{1,0:T(8,128)(2,1)}, bf16[256,2048]{1,0:T(8,128)(2,1)}, u32[]{:S(2)}, u32[]{:S(2)}) collective-permute-start(bf16[256,2048]{1,0:T(8,128)(2,1)} %bitcast.307), channel_id=1, source_target_pairs={{0,2},{1,3},{2,0},{3,1},{4,6},{5,7},{6,4},{7,5},{8,10},{9,11},{10,... | collective-permute-start | bytes 3145736 | tf_op jit(solution)/shard_map/ppermute | solution.py:46
  14.9 55.1 %collective-permute-start = (bf16[4,256,512]{2,1,0:T(8,128)(2,1)}, bf16[4,256,512]{2,1,0:T(8,128)(2,1)}, u32[]{:S(2)}, u32[]{:S(2)}) collective-permute-start(bf16[4,256,512]{2,1,0:T(8,128)(2,1)} %get-tuple-element.88), channel_id=1, source_target_pairs={{0,2},{1,3},{2,0},{3,1},{4,6},{5,7},{6,4},{7,5},{8,10},{9,11},{10,... | collective-permute-start | bytes 3145736 | tf_op jit(solution)/shard_map/ppermute | solution.py:46
  30.8 63.8 %collective-permute-start.9 = (bf16[2,256,2048]{2,1,0:T(8,128)(2,1)}, bf16[2,256,2048]{2,1,0:T(8,128)(2,1)}, u32[]{:S(2)}, u32[]{:S(2)}) collective-permute-start(bf16[2,256,2048]{2,1,0:T(8,128)(2,1)} %pad_maximum_fusion.3), channel_id=1, source_target_pairs={{0,1},{1,0},{2,3},{3,2},{4,5},{5,4},{6,7},{7,6},{8,9},{9,8},{10,11... | collective-permute-start | bytes 6291464 | tf_op jit(solution)/shard_map/ppermute | solution.py:46
  39.0 190.7 %collective-permute-start.5 = (bf16[512,1536]{1,0:T(8,128)(2,1)}, bf16[512,1536]{1,0:T(8,128)(2,1)}, u32[]{:S(2)}, u32[]{:S(2)}) collective-permute-start(bf16[512,1536]{1,0:T(8,128)(2,1)} %copy.102), channel_id=1, source_target_pairs={{0,1},{1,0},{2,3},{3,2},{4,5},{5,4},{6,7},{7,6},{8,9},{9,8},{10,11... | collective-permute-start | bytes 4718600 | tf_op jit(solution)/shard_map/ppermute | solution.py:46
  62.4 111.2 %collective-permute-start.2 = (bf16[512,2048]{1,0:T(8,128)(2,1)}, bf16[512,2048]{1,0:T(8,128)(2,1)}, u32[]{:S(2)}, u32[]{:S(2)}) collective-permute-start(bf16[512,2048]{1,0:T(8,128)(2,1)} %bitcast.339), channel_id=1, source_target_pairs={{0,1},{1,0},{2,3},{3,2},{4,5},{5,4},{6,7},{7,6},{8,9},{9,8},{10,11... | collective-permute-start | bytes 6291464 | tf_op jit(solution)/shard_map/ppermute | solution.py:46
  66.4 107.3 %collective-permute-start.3 = (bf16[512,2048]{1,0:T(8,128)(2,1)}, bf16[512,2048]{1,0:T(8,128)(2,1)}, u32[]{:S(2)}, u32[]{:S(2)}) collective-permute-start(bf16[512,2048]{1,0:T(8,128)(2,1)} %bitcast.338), channel_id=1, source_target_pairs={{0,2},{1,3},{2,0},{3,1},{4,6},{5,7},{6,4},{7,5},{8,10},{9,11},{10,... | collective-permute-start | bytes 6291464 | tf_op jit(solution)/shard_map/ppermute | solution.py:46
  73.1 40.1 %collective-permute-start.1 = (bf16[2,4,256,512]{3,2,1,0:T(8,128)(2,1)}, bf16[2,4,256,512]{3,2,1,0:T(8,128)(2,1)}, u32[]{:S(2)}, u32[]{:S(2)}) collective-permute-start(bf16[2,4,256,512]{3,2,1,0:T(8,128)(2,1)} %pad_maximum_fusion.2), channel_id=1, source_target_pairs={{0,1},{1,0},{2,3},{3,2},{4,5},{5,4},{6,7},{7,6},{8,9},{9,8},{10,11... | collective-permute-start | bytes 6291464 | tf_op jit(solution)/shard_map/ppermute | solution.py:46
  94.5 79.2 %collective-permute-start.4 = (bf16[512,2048]{1,0:T(8,128)(2,1)}, bf16[512,2048]{1,0:T(8,128)(2,1)}, u32[]{:S(2)}, u32[]{:S(2)}) collective-permute-start(bf16[512,2048]{1,0:T(8,128)(2,1)} %bitcast.340), channel_id=1, source_target_pairs={{0,3},{1,2},{2,1},{3,0},{4,7},{5,6},{6,5},{7,4},{8,11},{9,10},{10,... | collective-permute-start | bytes 6291464 | tf_op jit(solution)/shard_map/ppermute | solution.py:46
  106.7 139.5 %all-to-all-start.1 = ((bf16[8,2,256,128]{3,2,1,0:T(8,128)(2,1)}), bf16[8,2,256,128]{3,2,1,0:T(8,128)(2,1)}, u32[]{:S(2)}, u32[]{:S(2)}) async-start(bf16[8,2,256,128]{3,2,1,0:T(8,128)(2,1)} %bitcast.328), calls=%async_computation.1 | async-start | bytes 2097152 | tf_op jit(solution)/shard_map/all_to_all | solution.py:395
  113.2 116.5 %collective-permute-start.6 = (bf16[512,1536]{1,0:T(8,128)(2,1)}, bf16[512,1536]{1,0:T(8,128)(2,1)}, u32[]{:S(2)}, u32[]{:S(2)}) collective-permute-start(bf16[512,1536]{1,0:T(8,128)(2,1)} %copy.103), channel_id=1, source_target_pairs={{0,2},{1,3},{2,0},{3,1},{4,6},{5,7},{6,4},{7,5},{8,10},{9,11},{10,... | collective-permute-start | bytes 4718600 | tf_op jit(solution)/shard_map/ppermute | solution.py:46
  173.7 56.1 %collective-permute-start.7 = (bf16[512,1536]{1,0:T(8,128)(2,1)}, bf16[512,1536]{1,0:T(8,128)(2,1)}, u32[]{:S(2)}, u32[]{:S(2)}) collective-permute-start(bf16[512,1536]{1,0:T(8,128)(2,1)} %copy.104), channel_id=1, source_target_pairs={{0,3},{1,2},{2,1},{3,0},{4,7},{5,6},{6,5},{7,4},{8,11},{9,10},{10,... | collective-permute-start | bytes 4718600 | tf_op jit(solution)/shard_map/ppermute | solution.py:46
  227.7 119.1 %collective-permute-start.28 = (bf16[4,2,2,64,2048]{4,3,2,1,0:T(8,128)(2,1)}, bf16[4,2,2,64,2048]{4,3,2,1,0:T(8,128)(2,1)}, u32[]{:S(2)}, u32[]{:S(2)}) collective-permute-start(bf16[4,2,2,64,2048]{4,3,2,1,0:T(8,128)(2,1)} %dynamic-slice_bitcast_fusion), channel_id=1, source_target_pairs={{0,4},{4,0},{8,12},{12,8},{16,20},{20,16},{24,28},{28,24},{1,5},{5... | collective-permute-start | bytes 12582920 | tf_op jit(solution)/shard_map/ppermute | solution.py:46
  246.2 204.8 %all-to-all-start = ((bf16[8,2,3,256,128]{4,3,2,1,0:T(8,128)(2,1)}), bf16[8,2,3,256,128]{4,3,2,1,0:T(8,128)(2,1)}, u32[]{:S(2)}, u32[]{:S(2)}) async-start(bf16[8,2,3,256,128]{4,3,2,1,0:T(8,128)(2,1)} %bitcast.299), calls=%async_computation | async-start | bytes 6291456 | tf_op jit(solution)/shard_map/all_to_all | solution.py:391
  278.9 164.7 %collective-permute-start.34 = (bf16[2,2,256,2048]{3,2,0,1:T(8,128)(2,1)}, bf16[2,2,256,2048]{3,2,0,1:T(8,128)(2,1)}, u32[]{:S(2)}, u32[]{:S(2)}) collective-permute-start(bf16[2,2,256,2048]{3,2,0,1:T(8,128)(2,1)} %bitcast.295), channel_id=1, source_target_pairs={{0,4},{4,0},{8,12},{12,8},{16,20},{20,16},{24,28},{28,24},{1,5},{5... | collective-permute-start | bytes 12582920 | tf_op jit(solution)/shard_map/ppermute | solution.py:46
  357.1 179.0 %collective-permute-start.29 = (bf16[4,2,64,2048]{3,2,1,0:T(8,128)(2,1)}, bf16[4,2,64,2048]{3,2,1,0:T(8,128)(2,1)}, u32[]{:S(2)}, u32[]{:S(2)}) collective-permute-start(bf16[4,2,64,2048]{3,2,1,0:T(8,128)(2,1)} %fusion.15), channel_id=1, source_target_pairs={{0,8},{4,12},{8,0},{12,4},{16,24},{20,28},{24,16},{28,20},{1,9},{5... | collective-permute-start | bytes 6291464 | tf_op jit(solution)/shard_map/ppermute | solution.py:46
  523.8 198.0 %all-to-all-start.2 = ((bf16[8,2,4,2,128,128]{5,4,3,2,1,0:T(8,128)(2,1)}), bf16[8,2,4,2,128,128]{5,4,3,2,1,0:T(8,128)(2,1)}, u32[]{:S(2)}, u32[]{:S(2)}) async-start(bf16[8,2,4,2,128,128]{5,4,3,2,1,0:T(8,128)(2,1)} %shard_map.212), calls=%async_computation.2 | async-start | bytes 8388608 | tf_op jit(solution)/shard_map/all_to_all | solution.py:422
  533.3 132.0 %collective-permute-start.35 = (bf16[2,256,2048]{2,1,0:T(8,128)(2,1)}, bf16[2,256,2048]{2,1,0:T(8,128)(2,1)}, u32[]{:S(2)}, u32[]{:S(2)}) collective-permute-start(bf16[2,256,2048]{2,1,0:T(8,128)(2,1)} %fusion.16), channel_id=1, source_target_pairs={{0,8},{4,12},{8,0},{12,4},{16,24},{20,28},{24,16},{28,20},{1,9},{5... | collective-permute-start | bytes 6291464 | tf_op jit(solution)/shard_map/ppermute | solution.py:46
  540.8 143.1 %collective-permute-start.30 = (bf16[4,64,2048]{2,1,0:T(8,128)(2,1)}, bf16[4,64,2048]{2,1,0:T(8,128)(2,1)}, u32[]{:S(2)}, u32[]{:S(2)}) collective-permute-start(bf16[4,64,2048]{2,1,0:T(8,128)(2,1)} %fusion.43), channel_id=1, source_target_pairs={{0,16},{4,20},{8,24},{12,28},{16,0},{20,4},{24,8},{28,12},{1,17},{... | collective-permute-start | bytes 3145736 | tf_op jit(solution)/shard_map/ppermute | solution.py:46
  671.8 45.9 %collective-permute-start.36 = (bf16[256,2048]{1,0:T(8,128)(2,1)}, bf16[256,2048]{1,0:T(8,128)(2,1)}, u32[]{:S(2)}, u32[]{:S(2)}) collective-permute-start(bf16[256,2048]{1,0:T(8,128)(2,1)} %fusion.44), channel_id=1, source_target_pairs={{0,16},{4,20},{8,24},{12,28},{16,0},{20,4},{24,8},{28,12},{1,17},{... | collective-permute-start | bytes 3145736 | tf_op jit(solution)/shard_map/ppermute | solution.py:46
  686.4 34.2 %collective-permute-start.33 = (bf16[64,2048]{1,0:T(8,128)(2,1)S(1)}, bf16[64,2048]{1,0:T(8,128)(2,1)S(1)}, u32[]{:S(2)}, u32[]{:S(2)}) collective-permute-start(bf16[64,2048]{1,0:T(8,128)(2,1)S(1)} %get-tuple-element.72), channel_id=1, source_target_pairs={{0,3},{1,2},{2,1},{3,0},{4,7},{5,6},{6,5},{7,4},{8,11},{9,10},{10,... | collective-permute-start | bytes 786440 | tf_op jit(solution)/shard_map/ppermute | solution.py:46
  688.3 32.2 %collective-permute-start.32 = (bf16[64,2048]{1,0:T(8,128)(2,1)S(1)}, bf16[64,2048]{1,0:T(8,128)(2,1)S(1)}, u32[]{:S(2)}, u32[]{:S(2)}) collective-permute-start(bf16[64,2048]{1,0:T(8,128)(2,1)S(1)} %get-tuple-element.73), channel_id=1, source_target_pairs={{0,2},{1,3},{2,0},{3,1},{4,6},{5,7},{6,4},{7,5},{8,10},{9,11},{10,... | collective-permute-start | bytes 786440 | tf_op jit(solution)/shard_map/ppermute | solution.py:46
  689.1 31.5 %collective-permute-start.31 = (bf16[64,2048]{1,0:T(8,128)(2,1)S(1)}, bf16[64,2048]{1,0:T(8,128)(2,1)S(1)}, u32[]{:S(2)}, u32[]{:S(2)}) collective-permute-start(bf16[64,2048]{1,0:T(8,128)(2,1)S(1)} %get-tuple-element.74), channel_id=1, source_target_pairs={{0,1},{1,0},{2,3},{3,2},{4,5},{5,4},{6,7},{7,6},{8,9},{9,8},{10,11... | collective-permute-start | bytes 786440 | tf_op jit(solution)/shard_map/ppermute | solution.py:46
  796.4 26.1 %collective-permute-start.25 = (bf16[2,2,64,2048]{3,2,0,1:T(8,128)(2,1)S(1)}, bf16[2,2,64,2048]{3,2,0,1:T(8,128)(2,1)S(1)}, u32[]{:S(2)}, u32[]{:S(2)}) collective-permute-start(bf16[2,2,64,2048]{3,2,0,1:T(8,128)(2,1)S(1)} %bitcast.341), channel_id=1, source_target_pairs={{0,4},{4,0},{8,12},{12,8},{16,20},{20,16},{24,28},{28,24},{1,5},{5... | collective-permute-start | bytes 3145736 | tf_op jit(solution)/shard_map/ppermute | solution.py:46
  802.1 86.5 %collective-permute-start.19 = (bf16[4,2,2,64,1536]{4,3,0,1,2:T(8,128)(2,1)}, bf16[4,2,2,64,1536]{4,3,0,1,2:T(8,128)(2,1)}, u32[]{:S(2)}, u32[]{:S(2)}) collective-permute-start(bf16[4,2,2,64,1536]{4,3,0,1,2:T(8,128)(2,1)} %bitcast.297), channel_id=1, source_target_pairs={{0,4},{4,0},{8,12},{12,8},{16,20},{20,16},{24,28},{28,24},{1,5},{5... | collective-permute-start | bytes 9437192 | tf_op jit(solution)/shard_map/ppermute | solution.py:46
  804.7 37.0 %collective-permute-start.12 = (bf16[2,4,256,512]{3,2,1,0:T(8,128)(2,1)}, bf16[2,4,256,512]{3,2,1,0:T(8,128)(2,1)}, u32[]{:S(2)}, u32[]{:S(2)}) collective-permute-start(bf16[2,4,256,512]{3,2,1,0:T(8,128)(2,1)} %pad_maximum_fusion.5), channel_id=1, source_target_pairs={{0,1},{1,0},{2,3},{3,2},{4,5},{5,4},{6,7},{7,6},{8,9},{9,8},{10,11... | collective-permute-start | bytes 6291464 | tf_op jit(solution)/shard_map/ppermute | solution.py:46
  813.0 35.1 %collective-permute-start.10 = (bf16[2,256,2048]{2,1,0:T(8,128)(2,1)}, bf16[2,256,2048]{2,1,0:T(8,128)(2,1)}, u32[]{:S(2)}, u32[]{:S(2)}) collective-permute-start(bf16[2,256,2048]{2,1,0:T(8,128)(2,1)} %pad_maximum_fusion.4), channel_id=1, source_target_pairs={{0,1},{1,0},{2,3},{3,2},{4,5},{5,4},{6,7},{7,6},{8,9},{9,8},{10,11... | collective-permute-start | bytes 6291464 | tf_op jit(solution)/shard_map/ppermute | solution.py:46
  838.5 64.9 %collective-permute-start.27 = (bf16[64,2048]{1,0:T(8,128)(2,1)}, bf16[64,2048]{1,0:T(8,128)(2,1)}, u32[]{:S(2)}, u32[]{:S(2)}) collective-permute-start(bf16[64,2048]{1,0:T(8,128)(2,1)} %fusion.52), channel_id=1, source_target_pairs={{0,16},{4,20},{8,24},{12,28},{16,0},{20,4},{24,8},{28,12},{1,17},{... | collective-permute-start | bytes 786440 | tf_op jit(solution)/shard_map/ppermute | solution.py:46
  845.3 47.6 %collective-permute-start.13 = (bf16[4,256,512]{2,1,0:T(8,128)(2,1)}, bf16[4,256,512]{2,1,0:T(8,128)(2,1)}, u32[]{:S(2)}, u32[]{:S(2)}) collective-permute-start(bf16[4,256,512]{2,1,0:T(8,128)(2,1)} %fusion.18), channel_id=1, source_target_pairs={{0,2},{1,3},{2,0},{3,1},{4,6},{5,7},{6,4},{7,5},{8,10},{9,11},{10,... | collective-permute-start | bytes 3145736 | tf_op jit(solution)/shard_map/ppermute | solution.py:46
  851.4 43.8 %collective-permute-start.11 = (bf16[256,2048]{1,0:T(8,128)(2,1)}, bf16[256,2048]{1,0:T(8,128)(2,1)}, u32[]{:S(2)}, u32[]{:S(2)}) collective-permute-start(bf16[256,2048]{1,0:T(8,128)(2,1)} %fusion.22), channel_id=1, source_target_pairs={{0,2},{1,3},{2,0},{3,1},{4,6},{5,7},{6,4},{7,5},{8,10},{9,11},{10,... | collective-permute-start | bytes 3145736 | tf_op jit(solution)/shard_map/ppermute | solution.py:46
  891.7 35.1 %collective-permute-start.20 = (bf16[4,2,64,1536]{3,2,0,1:T(8,128)(2,1)S(1)}, bf16[4,2,64,1536]{3,2,0,1:T(8,128)(2,1)S(1)}, u32[]{:S(2)}, u32[]{:S(2)}) collective-permute-start(bf16[4,2,64,1536]{3,2,0,1:T(8,128)(2,1)S(1)} %fusion.40), channel_id=1, source_target_pairs={{0,8},{4,12},{8,0},{12,4},{16,24},{20,28},{24,16},{28,20},{1,9},{5... | collective-permute-start | bytes 4718600 | tf_op jit(solution)/shard_map/ppermute | solution.py:46
  906.5 24.2 %collective-permute-start.16 = (f32[20480]{0:T(1024)S(1)}, f32[20480]{0:T(1024)S(1)}, u32[]{:S(2)}, u32[]{:S(2)}) collective-permute-start(f32[20480]{0:T(1024)S(1)} %add.289), channel_id=1, source_target_pairs={{0,4},{4,0},{8,12},{12,8},{16,20},{20,16},{24,28},{28,24},{1,5},{5... | collective-permute-start | bytes 245768 | tf_op jit(solution)/shard_map/ppermute | solution.py:46
  927.4 41.1 %collective-permute-start.21 = (bf16[4,64,1536]{2,1,0:T(8,128)(2,1)S(1)}, bf16[4,64,1536]{2,1,0:T(8,128)(2,1)S(1)}, u32[]{:S(2)}, u32[]{:S(2)}) collective-permute-start(bf16[4,64,1536]{2,1,0:T(8,128)(2,1)S(1)} %fusion.50), channel_id=1, source_target_pairs={{0,16},{4,20},{8,24},{12,28},{16,0},{20,4},{24,8},{28,12},{1,17},{... | collective-permute-start | bytes 2359304 | tf_op jit(solution)/shard_map/ppermute | solution.py:46
  (73 other events, 1230.8 us)

commit v2 on v1

--- a/solution.py
+++ b/solution.py
@@ -2,6 +2,7 @@
 
 import jax
 import jax.numpy as jnp
+import numpy as np
 from jax import lax
 from jax.experimental import pallas as pl
 from jax.experimental.pallas import tpu as pltpu
@@ -46,15 +47,22 @@
     return lax.ppermute(value, axis, [(i, i ^ bit) for i in range(size)])
 
 
-def rotary(positions):
+def after(value, *events):
+    return lax.optimization_barrier((value,) + events)[0]
+
+
+def rotary(length):
     quarter = ROT // 2
-    inverse = 10000.0 ** (-jnp.arange(quarter, dtype=F32) * 2.0 / ROT)
-    angle = positions.astype(F32)[:, None] * inverse[None, :]
-    cosine, sine = jnp.cos(angle), jnp.sin(angle)
-    rest = positions.shape[0], HD - ROT
-    one = jnp.concatenate([cosine, cosine, jnp.ones(rest, F32)], axis=1)
-    two = jnp.concatenate([-sine, sine, jnp.zeros(rest, F32)], axis=1)
-    return jnp.tile(one, (1, LANES // HD)), jnp.tile(two, (1, LANES // HD))
+    inverse = np.float32(10000.0) ** (-np.arange(quarter, dtype=np.float32) * 2.0 / ROT)
+    angle = np.arange(length, dtype=np.float32)[:, None] * inverse.astype(np.float32)[None, :]
+    cosine, sine = np.cos(angle), np.sin(angle)
+    one = np.concatenate([cosine, cosine, np.ones((length, HD - ROT))], axis=1)
+    two = np.concatenate([-sine, sine, np.zeros((length, HD - ROT))], axis=1)
+    copies = (1, LANES // HD)
+    return (
+        jnp.asarray(np.tile(one, copies), F32),
+        jnp.asarray(np.tile(two, copies), F32),
+    )
 
 
 def turn(rows, cosine, sine):
@@ -68,55 +76,431 @@
     return rows * cosine + other * sine
 
 
-def qkv_kernel(pieces, rows_ref, *refs):
-    weights = refs[:pieces]
-    bias_ref, cos_ref, sin_ref, out_ref = refs[pieces:]
-    part = pl.program_id(0)
-    depth = weights[0].shape[0]
-    acc = bias_ref[0]
-    for j in range(pieces):
-        acc = acc + jnp.dot(
-            rows_ref[:, j * depth : (j + 1) * depth],
-            weights[j][...],
-            preferred_element_type=F32,
-        )
-    cosine, sine = cos_ref[...], sin_ref[...]
-    for h in range(out_ref.shape[0]):
-        cols = acc[:, h * LANES : (h + 1) * LANES]
-        turned = turn(cols, cosine, sine)
-        out_ref[h, 0, 0, 0] = jnp.where(part < 2, turned, cols).astype(out_ref.dtype)
-
-
-def project(rows, weights, bias, cosine, sine, groups, per_group):
-    tokens = cosine.shape[0]
-    slots = rows.shape[0] // tokens
-    width = rows.shape[1]
-    part_cols = bias.shape[1]
-    pairs = part_cols // LANES
-    pieces = len(weights)
-    depth = width // pieces
+def remote(src, dst, sends, recvs, at, target):
+    return pltpu.make_async_remote_copy(
+        src_ref=src,
+        dst_ref=dst,
+        send_sem=sends.at[at],
+        recv_sem=recvs.at[at],
+        device_id=target,
+        device_id_type=pl.DeviceIdType.MESH,
+    )
+
+
+def start_kernel(
+    shards,
+    groups,
+    pairs,
+    slot_groups,
+    items,
+    dup,
+    x_ref,
+    gain_ref,
+    shift_ref,
+    cot_ref,
+    qkv_ref,
+    qkv_bias_ref,
+    up_ref,
+    up_bias_ref,
+    out_ref,
+    down_ref,
+    cos_ref,
+    sin_ref,
+    normed_out,
+    grads_out,
+    wqkv_out,
+    wup_out,
+    hidden_out,
+    du_out,
+    qkv_in,
+    do_in,
+    normed,
+    grads,
+    wqkv,
+    wup,
+    down,
+    outw,
+    cosine,
+    sine,
+    stage,
+    dstage,
+    dh,
+    hidden,
+    du,
+    local_sem,
+    store_sem,
+    qs,
+    qr,
+    us,
+    ur,
+    rs,
+    rr,
+    as_,
+    ar,
+    ds_,
+    dr,
+):
+    place = lax.axis_index("ctx")
+    member = lax.axis_index("fsdp")
+    side = place % 2
+    rows, width = x_ref.shape
+    half = rows // 2
+    wide = width // groups
+    deep = up_ref.shape[1] // groups
+    part = wide // 2
+
+    barrier = pltpu.get_barrier_semaphore()
+    for j in range(1, groups):
+        pl.semaphore_signal(
+            barrier, inc=1, device_id={"fsdp": member ^ j}, device_id_type=pl.DeviceIdType.MESH
+        )
+    for k in range(1, shards):
+        pl.semaphore_signal(
+            barrier, inc=1, device_id={"ctx": place ^ k}, device_id_type=pl.DeviceIdType.MESH
+        )
+
+    def local(src, dst, at):
+        copy = pltpu.make_async_copy(src, dst, local_sem.at[at])
+        copy.start()
+        return copy
+
+    def block(at, size):
+        return pl.ds(pl.multiple_of(at, size), size)
+
+    own_rows = block(member * wide, wide)
+    loads = [
+        local(
+            qkv_ref.at[:, block(p * width + member * wide, wide)],
+            wqkv.at[own_rows, pl.ds(p * wide, wide)],
+            p,
+        )
+        for p in range(3)
+    ]
+    loads.append(local(up_ref.at[:, block(member * deep, deep)], wup.at[own_rows, :], 3))
+    loads.append(local(cot_ref, grads.at[pl.ds(0, rows)], 4))
+    loads.append(local(out_ref, outw, 5))
+    loads.append(local(down_ref, down, 6))
+    upper = 2 * shards - 1 - place
+    for at, (table, held) in enumerate(((cos_ref, cosine), (sin_ref, sine))):
+        loads.append(
+            local(table.at[block(place * half, half)], held.at[pl.ds(0, half)], 7 + 2 * at)
+        )
+        loads.append(
+            local(table.at[block(upper * half, half)], held.at[pl.ds(half, half)], 8 + 2 * at)
+        )
+    pl.semaphore_wait(barrier, groups - 1 + shards - 1)
+
+    half_rows = block(member * wide + side * part, part)
+    started = []
+
+    def begin(copy):
+        copy.start()
+        started.append(copy)
+        return copy
+
+    q_far = {}
+    for j in (2, 3):
+        for p in range(3):
+            q_far[j, p] = begin(
+                remote(
+                    qkv_ref.at[block(side * part, part), block(p * width + (member ^ j) * wide, wide)],
+                    wqkv.at[half_rows, pl.ds(p * wide, wide)],
+                    qs,
+                    qr,
+                    (j - 2) * 3 + p,
+                    {"fsdp": member ^ j},
+                )
+            )
+
+    tokens = x_ref[...].astype(F32)
+    centred = tokens - jnp.mean(tokens, axis=-1, keepdims=True)
+    spread = lax.rsqrt(jnp.mean(centred * centred, axis=-1, keepdims=True) + EPS)
+    normed[0:rows, :] = (centred * spread * gain_ref[...] + shift_ref[...]).astype(BF16)
+    n_far = begin(
+        remote(
+            normed.at[pl.ds(0, rows)], normed.at[pl.ds(2 * rows, rows)], rs, rr, 0, {"fsdp": member ^ 2}
+        )
+    )
+    n_near = begin(
+        remote(normed.at[pl.ds(0, rows)], normed.at[pl.ds(rows, rows)], rs, rr, 1, {"fsdp": member ^ 1})
+    )
+    q_near = [
+        begin(
+            remote(
+                qkv_ref.at[:, block(p * width + (member ^ 1) * wide, wide)],
+                wqkv.at[own_rows, pl.ds(p * wide, wide)],
+                qs,
+                qr,
+                6 + p,
+                {"fsdp": member ^ 1},
+            )
+        )
+        for p in range(3)
+    ]
+
+    q_side = []
+    for j in (2, 3):
+        for p in range(3):
+            q_far[j, p].wait_recv()
+            spot = wqkv.at[block((member ^ j) * wide + side * part, part), pl.ds(p * wide, wide)]
+            q_side.append(
+                begin(remote(spot, spot, qs, qr, 9 + (j - 2) * 3 + p, {"ctx": place ^ 1}))
+            )
+    n_far.wait_recv()
+    n_last = begin(
+        remote(
+            normed.at[pl.ds(2 * rows, rows)],
+            normed.at[pl.ds(3 * rows, rows)],
+            rs,
+            rr,
+            2,
+            {"fsdp": member ^ 1},
+        )
+    )
+
+    loads[4].wait()
+    g_far = begin(
+        remote(
+            grads.at[pl.ds(0, rows)], grads.at[pl.ds(2 * rows, rows)], rs, rr, 3, {"fsdp": member ^ 2}
+        )
+    )
+    g_near = begin(
+        remote(grads.at[pl.ds(0, rows)], grads.at[pl.ds(rows, rows)], rs, rr, 4, {"fsdp": member ^ 1})
+    )
+    u_far = [
+        begin(
+            remote(
+                up_ref.at[block(side * part, part), block((member ^ j) * deep, deep)],
+                wup.at[half_rows, :],
+                us,
+                ur,
+                j - 2,
+                {"fsdp": member ^ j},
+            )
+        )
+        for j in (2, 3)
+    ]
+    u_near = begin(
+        remote(
+            up_ref.at[:, block((member ^ 1) * deep, deep)],
+            wup.at[own_rows, :],
+            us,
+            ur,
+            2,
+            {"fsdp": member ^ 1},
+        )
+    )
+
+    for at in (0, 1, 2, 7, 8, 9, 10):
+        loads[at].wait()
+    for copy in q_near + q_side:
+        copy.wait_recv()
+    n_near.wait_recv()
+    arrivals = []
+    stores = []
+
+    def keep(src, dst):
+        copy = pltpu.make_async_copy(src, dst, store_sem.at[len(stores)])
+        copy.start()
+        stores.append(copy)
+
+    def owner(target):
+        return target // (slot_groups * dup), (target // dup) % slot_groups
+
+    for item in range(items):
+        if item == items - 1:
+            n_last.wait_recv()
+
+        def project(p, _, item=item):
+            for g in range(slot_groups):
+                slot = item * slot_groups + g
+                acc = qkv_bias_ref[p * groups + member] + jnp.dot(
+                    normed[slot * rows : (slot + 1) * rows, :],
+                    wqkv[:, block(p * wide, wide)],
+                    preferred_element_type=F32,
+                )
+                for h in range(pairs):
+                    cols = acc[:, h * LANES : (h + 1) * LANES]
+                    turned = turn(cols, cosine[...], sine[...])
+                    stage[item, h, g, p] = jnp.where(p < 2, turned, cols).astype(BF16)
+            return 0
+
+        lax.fori_loop(0, 3, project, 0)
+        for k in range(1, shards):
+            pair, group = owner(place ^ k)
+            arrivals.append(
+                begin(
+                    remote(
+                        stage.at[item, pair, group],
+                        qkv_in.at[item, place],
+                        as_,
+                        ar,
+                        item * shards + k,
+                        {"ctx": place ^ k},
+                    )
+                )
+            )
+        pair, group = owner(place)
+        keep(stage.at[item, pair, group], qkv_in.at[item, place])
+
+    g_far.wait_recv()
+    g_last = begin(
+        remote(
+            grads.at[pl.ds(2 * rows, rows)],
+            grads.at[pl.ds(3 * rows, rows)],
+            rs,
+            rr,
+            5,
+            {"fsdp": member ^ 1},
+        )
+    )
+    g_near.wait_recv()
+    loads[5].wait()
+    g_last.wait_recv()
+    for slot in range(groups):
+        item, g = slot // slot_groups, slot % slot_groups
+        att = contract_cols(grads[slot * rows : (slot + 1) * rows, :], outw[...]).astype(BF16)
+        for h in range(pairs):
+            dstage[h, g, item] = att[:, h * LANES : (h + 1) * LANES]
+    for k in range(1, shards):
+        pair, group = owner(place ^ k)
+        arrivals.append(
+            begin(
+                remote(
+                    dstage.at[pair, group],
+                    do_in.at[place],
+                    ds_,
+                    dr,
+                    k,
+                    {"ctx": place ^ k},
+                )
+            )
+        )
+    pair, group = owner(place)
+    keep(dstage.at[pair, group], do_in.at[place])
+    keep(normed, normed_out)
+    keep(grads, grads_out)
+    keep(wqkv, wqkv_out)
+
+    u_side = []
+    for j in (2, 3):
+        u_far[j - 2].wait_recv()
+        spot = wup.at[block((member ^ j) * wide + side * part, part), :]
+        u_side.append(begin(remote(spot, spot, us, ur, 3 + j - 2, {"ctx": place ^ 1})))
+
+    loads[6].wait()
+    tile = 512
+    high = 2 * rows
+
+    def spot_of(at):
+        return block((at % 2) * high, high), block((at // 2) * tile, tile)
+
+    def back(at, _):
+        r, c = spot_of(at)
+        dh[r, c] = contract_cols(grads[r, :], down[c, :])
+        return 0
+
+    lax.fori_loop(0, 2 * (deep // tile), back, 0)
+    loads[3].wait()
+    u_near.wait_recv()
+    for copy in u_side:
+        copy.wait_recv()
+    keep(wup, wup_out)
+
+    def forward(at, _):
+        r, c = spot_of(at)
+        value = matmul(normed[r, :], wup[:, c]) + up_bias_ref[member, :, c]
+        hidden[r, c] = gelu_value(value).astype(BF16)
+        du[r, c] = (dh[r, c] * gelu_slope(value)).astype(BF16)
+        return 0
+
+    lax.fori_loop(0, 2 * (deep // tile), forward, 0)
+    keep(hidden, hidden_out)
+    keep(du, du_out)
+    for copy in arrivals:
+        copy.wait_recv()
+    for copy in started:
+        copy.wait_send()
+    for copy in stores:
+        copy.wait()
+
+
+def begin_layer(
+    x, gain, shift, cot, qkv_w, qkv_b, up_w, up_b, out_w, down_w, cosine, sine,
+    shards, groups, pairs, slot_groups, items, dup,
+):
+    rows, width = x.shape
+    wide = width // groups
+    deep = up_w.shape[1] // groups
+    total = rows * groups
+    whole = pl.BlockSpec(memory_space=pltpu.VMEM)
+    apart = pl.BlockSpec(memory_space=pl.ANY)
+    dma = pltpu.SemaphoreType.DMA
+    shape = jax.ShapeDtypeStruct
+    stores = items + 1 + 6
     return pl.pallas_call(
-        partial(qkv_kernel, pieces),
-        grid=(3, slots),
-        out_shape=jax.ShapeDtypeStruct((pairs, groups, per_group, 3, tokens, LANES), BF16),
-        in_specs=[pl.BlockSpec((tokens, width), lambda p, s: (s, 0))]
-        + [pl.BlockSpec((depth, part_cols), lambda p, s: (0, p))] * pieces
-        + [
-            pl.BlockSpec((1, 1, part_cols), lambda p, s: (p, 0, 0)),
-            pl.BlockSpec((tokens, LANES), lambda p, s: (0, 0)),
-            pl.BlockSpec((tokens, LANES), lambda p, s: (0, 0)),
+        partial(start_kernel, shards, groups, pairs, slot_groups, items, dup),
+        out_shape=[
+            shape((total, width), BF16),
+            shape((total, width), BF16),
+            shape((width, 3 * wide), BF16),
+            shape((width, deep), BF16),
+            shape((total, deep), BF16),
+            shape((total, deep), BF16),
+            shape((items, shards, 3, rows, LANES), BF16),
+            shape((shards, items, rows, LANES), BF16),
         ],
-        out_specs=pl.BlockSpec(
-            (pairs, 1, 1, 1, tokens, LANES),
-            lambda p, s: (0, s // per_group, s % per_group, p, 0, 0),
+        in_specs=[whole, whole, whole, apart, apart, whole, apart, whole, apart, apart, apart, apart],
+        out_specs=[apart] * 8,
+        scratch_shapes=[
+            pltpu.VMEM((total, width), BF16),
+            pltpu.VMEM((total, width), BF16),
+            pltpu.VMEM((width, 3 * wide), BF16),
+            pltpu.VMEM((width, deep), BF16),
+            pltpu.VMEM((deep, width), BF16),
+            pltpu.VMEM((wide, width), BF16),
+            pltpu.VMEM((rows, LANES), F32),
+            pltpu.VMEM((rows, LANES), F32),
+            pltpu.VMEM((items, pairs, slot_groups, 3, rows, LANES), BF16),
+            pltpu.VMEM((pairs, slot_groups, items, rows, LANES), BF16),
+            pltpu.VMEM((total, deep), F32),
+            pltpu.VMEM((total, deep), BF16),
+            pltpu.VMEM((total, deep), BF16),
+            dma((11,)),
+            dma((stores,)),
+            dma((15,)),
+            dma((15,)),
+            dma((5,)),
+            dma((5,)),
+            dma((6,)),
+            dma((6,)),
+            dma((items * shards,)),
+            dma((items * shards,)),
+            dma((shards,)),
+            dma((shards,)),
+        ],
+        compiler_params=pltpu.CompilerParams(
+            collective_id=0, has_side_effects=True, vmem_limit_bytes=62 * 2**20
         ),
-        compiler_params=pltpu.CompilerParams(vmem_limit_bytes=40 * 2**20),
         cost_estimate=pl.CostEstimate(
-            flops=2 * rows.shape[0] * width * part_cols * 3,
-            bytes_accessed=30 * 2**20,
-            transcendentals=0,
+            flops=2 * total * width * (3 * wide + wide + 2 * deep),
+            bytes_accessed=60 * 2**20,
+            transcendentals=total * deep,
         ),
-    )(rows, *weights, bias.reshape(3, 1, part_cols), cosine, sine)
+    )(
+        x,
+        gain.reshape(1, width),
+        shift.reshape(1, width),
+        cot,
+        qkv_w,
+        qkv_b.reshape(3 * groups, 1, wide),
+        up_w,
+        up_b.reshape(groups, 1, deep),
+        out_w,
+        down_w,
+        cosine,
+        sine,
+    )
 
 
 def attend_kernel(
@@ -139,7 +523,7 @@
     def load(part, item):
         first, second, side = where_is(item)
         return jnp.concatenate(
-            [qkv_ref[first, 0, part, side], qkv_ref[second, 0, part, side]], axis=0
+            [qkv_ref[0, first, part, side], qkv_ref[0, second, part, side]], axis=0
         )
 
     def load_do(item):
@@ -227,8 +611,8 @@
     lax.fori_loop(0, count, finish, 0)
 
 
-def attend(qkv, grads, cosine, sine, heads, dup):
-    shards, items = qkv.shape[:2]
+def attend(qkv, grads, item, cosine, sine, heads, dup):
+    shards, items = qkv.shape[1], 1
     half = qkv.shape[-2]
     tokens = shards * 2 * half
     block = 2 * half
@@ -240,9 +624,11 @@
         out_shape=jax.ShapeDtypeStruct((shards, items, 4, 2, half, LANES), BF16),
         in_specs=[
             pl.BlockSpec(
-                (shards, 1, 3, 2, half, LANES), lambda i: (0, i, 0, 0, 0, 0), pipeline_mode=once
+                (1, shards, 3, 2, half, LANES), lambda i: (item, 0, 0, 0, 0, 0), pipeline_mode=once
             ),
-            pl.BlockSpec((shards, 1, 2, half, LANES), lambda i: (0, i, 0, 0, 0), pipeline_mode=once),
+            pl.BlockSpec(
+                (shards, 1, 2, half, LANES), lambda i: (0, item, 0, 0, 0), pipeline_mode=once
+            ),
             pl.BlockSpec((tokens, LANES), lambda i: (0, 0), pipeline_mode=once),
             pl.BlockSpec((tokens, LANES), lambda i: (0, 0), pipeline_mode=once),
         ],
@@ -280,17 +666,11 @@
     return value
 
 
-def gather_rows(own):
-    far = swap(own, "fsdp", 2)
-    pair = swap(jnp.stack([own, far]), "fsdp", 1)
-    return [own, pair[0], far, pair[1]]
-
-
 def scatter_rows(parts):
-    near = swap(jnp.stack([parts[1], parts[3]]).astype(BF16), "fsdp", 1).astype(F32)
-    mine = parts[0] + near[0]
-    far = swap((parts[2] + near[1]).astype(BF16), "fsdp", 2)
-    return mine + far.astype(F32)
+    last = swap(parts[3].astype(BF16), "fsdp", 1).astype(F32)
+    far = swap((parts[2] + last).astype(BF16), "fsdp", 2).astype(F32)
+    near = swap(parts[1].astype(BF16), "fsdp", 1).astype(F32)
+    return parts[0] + near + far
 
 
 def total_sum(value):
@@ -326,47 +706,16 @@
     member = lax.axis_index("fsdp")
     wide = width // groups
     deep = hidden_width // groups
-    bits = shards.bit_length() - 1
+    x_first = list(range(shards.bit_length() - 1))
+    z_first = x_first[1:2] + x_first[:1] + x_first[2:]
 
     tokens = inputs[0].astype(F32)
     mean = jnp.mean(tokens, axis=-1, keepdims=True)
     centred = tokens - mean
     inv_scale = lax.rsqrt(jnp.mean(centred * centred, axis=-1, keepdims=True) + EPS)
     normal = centred * inv_scale
-    flat = (normal * norm_gain + norm_shift).astype(BF16)
-
-    def relative(value, axis):
-        return [
-            lax.dynamic_index_in_dim(value, member ^ j, axis, keepdims=False) for j in range(groups)
-        ]
-
-    flat_rel = jnp.stack(relative(flat.reshape(rows, groups, wide), 1))
-    got = gather_rows(flat_rel)
-    normed = jnp.concatenate(
-        [
-            jnp.concatenate([got[j][i ^ j] for i in range(groups)], axis=1)
-            for j in range(groups)
-        ],
-        axis=0,
-    )
     grad_low = cotangent[0]
-    grads = jnp.concatenate(gather_rows(grad_low), axis=0)
-
-    qkv_cols = qkv_weight.reshape(wide, 3, groups, wide)
-    up_cols = up_weight.reshape(wide, groups, deep)
-    qkv_pieces, up_pieces = [], []
-    for j in range(groups):
-        piece = lax.dynamic_index_in_dim(qkv_cols, member ^ j, 2, keepdims=False).reshape(
-            wide, 3 * wide
-        )
-        qkv_pieces.append(swap(piece, "fsdp", j) if j else piece)
-    for j in range(groups):
-        piece = lax.dynamic_index_in_dim(up_cols, member ^ j, 1, keepdims=False)
-        up_pieces.append(swap(piece, "fsdp", j) if j else piece)
-    qkv_bias_own = lax.dynamic_index_in_dim(
-        qkv_bias.reshape(3, groups, wide), member, 1, keepdims=False
-    )
-    up_bias_own = lax.dynamic_index_in_dim(up_bias.reshape(groups, deep), member, 0, keepdims=False)
+    grad_full = grad_low.astype(F32)
 
     pairs = wide // LANES
     heads_in_pair = LANES // HD
@@ -376,67 +725,62 @@
     per_group = groups // slot_groups
     heads = heads_in_pair // dup
 
-    def spread(value):
-        shape = value.shape
-        if dup > 1:
-            value = jnp.broadcast_to(
-                value[:, :, None], shape[:2] + (dup,) + shape[2:]
-            )
-        return value.reshape((shards,) + shape[2:])
-
-    local = jnp.arange(rows, dtype=jnp.int32)
-    blocks = jnp.where(local < half, place, 2 * shards - 1 - place)
-    cosine, sine = rotary(blocks * half + local % half)
-    qkv_out = project(normed, qkv_pieces, qkv_bias_own, cosine, sine, slot_groups, per_group)
-    qkv_in = lax.all_to_all(spread(qkv_out), "ctx", 0, 0)
-
-    grad_att = contract_cols(grads, out_weight).astype(BF16)
-    grad_att = grad_att.reshape(slot_groups, per_group, rows, pairs, LANES).transpose(3, 0, 1, 2, 4)
-    grad_in = lax.all_to_all(spread(grad_att), "ctx", 0, 0)
-
-    up_own = jnp.concatenate(up_pieces, axis=0)
-    up_rows = matmul(normed, up_own) + up_bias_own
-    hidden = gelu_value(up_rows).astype(BF16)
-    grad_hidden = contract_cols(grads, down_weight)
-    grad_up = (grad_hidden * gelu_slope(up_rows)).astype(BF16)
+    cos_full, sin_full = rotary(shards * rows)
+    normed, grads, qkv_own, up_own, hidden, grad_up, qkv_in, grad_in = begin_layer(
+        inputs[0],
+        norm_gain,
+        norm_shift,
+        grad_low,
+        qkv_weight,
+        qkv_bias,
+        up_weight,
+        up_bias,
+        out_weight,
+        down_weight,
+        cos_full,
+        sin_full,
+        shards,
+        groups,
+        pairs,
+        slot_groups,
+        per_group,
+        dup,
+    )
+
     down_grad = contract_rows(hidden, grads).astype(BF16)
     up_grad = contract_rows(normed, grad_up).astype(BF16)
     hw = deep // shards
     down_weight_grad = scatter_sum(
-        down_grad.reshape(shards, hw, width), 0, place, list(range(bits))
+        down_grad.reshape(shards, hw, width), 0, place, x_first
     )
     up_part = scatter_sum(
-        up_grad.reshape(groups, shards, wide // shards, deep), 1, place, list(range(bits))
-    )
-
-    full = jnp.arange(shards * rows, dtype=jnp.int32)
-    cos_full, sin_full = rotary(full)
-    back = attend(
-        qkv_in.reshape(shards, per_group, 3, 2, half, LANES),
-        grad_in.reshape(shards, per_group, 2, half, LANES),
-        cos_full,
-        sin_full,
-        heads,
-        dup,
-    )
-    back = lax.all_to_all(back, "ctx", 0, 0)
-    back = back.reshape(pairs, slot_groups, dup, per_group, 4, rows, LANES)
-    back = jnp.sum(back, axis=2) if dup > 1 else back[:, :, 0]
-    back = back.transpose(3, 1, 2, 4, 0, 5).reshape(4, groups * rows, wide)
+        up_grad.reshape(groups, shards, wide // shards, deep), 1, place, z_first
+    )
+
+    backs = []
+    for item in range(per_group):
+        back = attend(
+            qkv_in.reshape(per_group, shards, 3, 2, half, LANES),
+            grad_in.reshape(shards, per_group, 2, half, LANES),
+            item,
+            cos_full,
+            sin_full,
+            heads,
+            dup,
+        )
+        back = lax.all_to_all(back, "ctx", 0, 0)
+        back = back.reshape(pairs, slot_groups, dup, 4, rows, LANES)
+        back = jnp.sum(back, axis=2) if dup > 1 else back[:, :, 0]
+        backs.append(back.transpose(2, 1, 3, 0, 4).reshape(4, slot_groups * rows, wide))
+    back = jnp.concatenate(backs, axis=1)
     attended = back[0]
     grad_qkv = jnp.concatenate([back[1], back[2], back[3]], axis=1)
 
     share = matmul(hidden, down_weight) + matmul(attended, out_weight)
     result = tokens + scatter_rows(list(share.reshape(groups, rows, width))) + out_bias + down_bias
 
-    qkv_own = jnp.concatenate(qkv_pieces, axis=0)
     grad_share = contract_cols(grad_up, up_own) + contract_cols(grad_qkv, qkv_own)
-    grad_share = grad_share.reshape(groups, rows, groups, wide)
-    grad_share = [
-        jnp.stack([grad_share[j, :, i ^ j] for i in range(groups)]) for j in range(groups)
-    ]
-    grad_normed = scatter_rows(grad_share)
-    grad_normed = jnp.concatenate(relative(grad_normed, 0), axis=1)
+    grad_normed = scatter_rows(list(grad_share.reshape(groups, rows, width)))
     grad_full = grad_low.astype(F32)
     grad_normal = grad_normed * norm_gain
     grad_tokens = inv_scale * (
@@ -449,15 +793,20 @@
     qkv_grad = contract_rows(normed, grad_qkv).astype(BF16)
     out_grad = contract_rows(attended, grads).astype(BF16)
     ow = wide // shards
-    out_weight_grad = scatter_sum(out_grad.reshape(shards, ow, width), 0, place, list(range(bits)))
+    out_weight_grad = scatter_sum(out_grad.reshape(shards, ow, width), 0, place, z_first)
     qkv_part = scatter_sum(
-        qkv_grad.reshape(groups, shards, ow, 3 * wide), 1, place, list(range(bits))
-    )
+        qkv_grad.reshape(groups, shards, ow, 3 * wide), 1, place, x_first
+    )
+
+    def relative(value):
+        return [
+            lax.dynamic_index_in_dim(value, member ^ j, 0, keepdims=False) for j in range(groups)
+        ]
 
     def exchange(part):
-        part = part.astype(BF16)
-        got = [part[0]] + [swap(part[j], "fsdp", j) for j in range(1, groups)]
-        return relative(jnp.stack(got), 0)
+        sent = relative(part.astype(BF16))
+        got = [sent[0]] + [swap(sent[j], "fsdp", j) for j in range(1, groups)]
+        return relative(jnp.stack(got))
 
     up_weight_grad = jnp.concatenate(exchange(up_part), axis=1).astype(F32)
     qkv_weight_grad = jnp.concatenate(
@@ -472,22 +821,14 @@
     up_bias_all = lax.dynamic_update_slice(
         jnp.zeros((groups, deep), F32), up_bias_cols, (member, 0)
     ).reshape(-1)
-    sums = total_sum(
+    early = total_sum(jnp.concatenate([jnp.sum(grad_full, axis=0), up_bias_all]))
+    late = total_sum(
         jnp.concatenate(
-            [
-                jnp.sum(grad_normed * normal, axis=0),
-                jnp.sum(grad_normed, axis=0),
-                jnp.sum(grad_full, axis=0),
-                qkv_bias_all,
-                up_bias_all,
-            ]
-        )
-    )
-    gain_grad = sums[:width]
-    shift_grad = sums[width : 2 * width]
-    out_bias_grad = sums[2 * width : 3 * width]
-    qkv_bias_grad = sums[3 * width : 6 * width]
-    up_bias_grad = sums[6 * width :]
+            [jnp.sum(grad_normed * normal, axis=0), jnp.sum(grad_normed, axis=0), qkv_bias_all]
+        )
+    )
+    out_bias_grad, up_bias_grad = early[:width], early[width:]
+    gain_grad, shift_grad, qkv_bias_grad = late[:width], late[width : 2 * width], late[2 * width :]
     return (
         result.astype(BF16)[None],
         input_grad[None],

time: 999 us -> 801 us (0.80)
  Pallas kernels: 87.6 us -> 264 us
  local copies, waits for them, and re-layouts: 174 us -> 55.3 us
  waiting for transfers between devices: 407 us -> 304 us
  other arithmetic: 124 us -> 40.9 us
  matrix products: 130 us -> 85.5 us
  starting transfers between devices: 62.6 us -> 42 us
    pallas_call x1, Pallas kernels: 14.7 us -> 191 us  [begin_layer(): pl.pallas_call(partial(start_kernel, shards, groups, pairs, slot_groups,...]
    ppermute x37 -> x34, waiting for transfers between devices: 407 us -> 267 us  [swap(): return lax.ppermute(value, axis, [(i, i ^ bit) for i in range(size)])]
    concatenate x3 -> x2, other arithmetic: 58.7 us -> 0.01 us  [the longest x1 0.01 us: on_device(): jnp.concatenate([jnp.sum(grad_normed * normal, axis=0), jnp.sum(grad_norm...]
    all_to_all x1 -> x2, waiting for transfers between devices: 0.01 us -> 36.7 us  [on_device(): back = lax.all_to_all(back, 'ctx', 0, 0)]
    reshape x10 -> x2, local copies, waits for them, and re-layouts: 36.4 us -> 5.49 us  [on_device(): back.transpose(2, 1, 3, 0, 4).reshape(4, slot_groups * rows, wide)]
    dynamic_slice x10 -> x3, local copies, waits for them, and re-layouts: 30.3 us -> 0.24 us  [relative(): lax.dynamic_index_in_dim(value, member ^ j, 0, keepdims=False)]
    unnamed x141 -> x44, local copies, waits for them, and re-layouts: 38 us -> 8.54 us
    dot_general x4 -> x2, matrix products: 54.3 us -> 27.6 us  [contract_cols(): lax.dot_general(left, right, (((1,), (1,)), ((), ())), preferred_element_...]
  transfers between devices with their start and end apart: 40 -> 36, of which waited for: 14 -> 15; matrix products, arithmetic and copies ran while one was open for 34% -> 21% of each run, Pallas kernels for 9% -> 5%
where the time goes in v2:
time: 801 us; the launch traced here: 793 us
  waiting for transfers between devices  304 us (38%)
  Pallas kernels  264 us (33%)
  matrix products  85.5 us (11%)
  local copies, waits for them, and re-layouts  55.3 us (7%)
  starting transfers between devices  42 us (5%)
  other arithmetic  40.9 us (5%)
    ppermute x34, waiting for transfers between devices, swap(): return lax.ppermute(value, axis, [(i, i ^ bit) for i in range(size)])  267 us
    pallas_call x1, Pallas kernels, begin_layer(): pl.pallas_call(partial(start_kernel, shards, groups, pairs, slot_groups,...  191 us
    pallas_call x2, Pallas kernels, attend(): pl.pallas_call(partial(attend_kernel, shards, heads, dup), grid=(items,),...  73.2 us
    all_to_all x2, waiting for transfers between devices, on_device(): back = lax.all_to_all(back, 'ctx', 0, 0)  36.7 us
    dot_general x4, matrix products, contract_rows(): lax.dot_general(left, right, (((0,), (0,)), ((), ())), preferred_element_...  36.1 us
    ppermute x34, starting transfers between devices, swap(): return lax.ppermute(value, axis, [(i, i ^ bit) for i in range(size)])  33.7 us
    dot_general x2, matrix products, contract_cols(): lax.dot_general(left, right, (((1,), (1,)), ((), ())), preferred_element_...  27.6 us
    add x10, other arithmetic, scatter_sum(): value = keep.astype(F32) + got.astype(F32)  22.2 us
  transfers between devices with their start and end apart: 36, of which 15 were waited for; matrix products, arithmetic and copies ran while one was open for 21% of the time, Pallas kernels for 5%

profile of v2, /device:TPU:0, one launch (start us, length us, event | category | flops | bytes accessed | tf_op | source)
XLA Modules:
  0.0 793.2 jit_solution(5544560857758444977)
XLA Ops:
  0.6 190.5 %shard_map.229 = (bf16[1024,2048]{1,0:T(8,128)(2,1)}, bf16[1024,2048]{1,0:T(8,128)(2,1)}, bf16[2048,1536]{1,0:T(8,128)(2,1)}, bf16[2048,2048]{1,0:T(8,128)(2,1)}...) custom-call(bf16[256,2048]{1,0:T(8,128)(2,1)} %bitcast.158, ...), custom_call_target="tpu_custom_call" | custom-call | flops 25769803776 | bytes 62914560 | tf_op jit(solution)/shard_map/pallas_call | solution.py:441
  191.2 36.6 %shard_map.230 = bf16[8,1,4,2,128,128]{5,4,3,2,1,0:T(8,128)(2,1)} custom-call(bf16[2,8,3,2,128,128]{5,4,3,2,1,0:T(8,128)(2,1)} %bitcast.186, bf16[8,2,2,128,128]{4,3,2,1,0:T(8,128)(2,1)} %bitcast.188, f32[2048,128]{1,0:T(8,128)} %constant.146.clone.cos_ref, f32[2048,128]{1,0:T(8,128)} %constant.147.clone.sin_ref), custom_call_target="tpu_custom_call" | custom-call | flops 12079595520 | bytes 16777216 | tf_op jit(solution)/shard_map/pallas_call | solution.py:621
  227.8 3.8 all-to-all-start
  231.6 12.0 %convolution_convert_fusion.1 = bf16[2048,2048]{1,0:T(8,128)(2,1)S(1)} fusion(bf16[1024,2048]{1,0:T(8,128)(2,1)} %get-tuple-element.26, bf16[1024,2048]{1,0:T(8,128)(2,1)} %get-tuple-element.23), kind=kOutput, calls=%fused_computation.4 | convolution fusion | flops 8594128896 | bytes 16777216 | tf_op jit(solution)/shard_map/dot_general | solution.py:34
  246.2 3.7 copy-done.3
  251.9 11.5 %convolution_convert_fusion = bf16[2048,2048]{1,0:T(8,128)(2,1)} fusion(bf16[1024,2048]{1,0:T(8,128)(2,1)S(1)} %copy-done.13, bf16[1024,2048]{1,0:T(8,128)(2,1)S(1)} %copy-done.11), kind=kOutput, calls=%fused_computation.3 | convolution fusion | flops 8594128896 | bytes 16777216 | tf_op jit(solution)/shard_map/dot_general | solution.py:34
  263.3 6.7 constant_dynamic-slice_fusion.1
  278.0 36.6 %shard_map.231 = bf16[8,1,4,2,128,128]{5,4,3,2,1,0:T(8,128)(2,1)} custom-call(bf16[2,8,3,2,128,128]{5,4,3,2,1,0:T(8,128)(2,1)} %bitcast.187, bf16[8,2,2,128,128]{4,3,2,1,0:T(8,128)(2,1)} %bitcast.189, f32[2048,128]{1,0:T(8,128)} %constant.146.clone.cos_ref, f32[2048,128]{1,0:T(8,128)} %constant.147.clone.sin_ref), custom_call_target="tpu_custom_call" | custom-call | flops 12079595520 | bytes 16777216 | tf_op jit(solution)/shard_map/pallas_call | solution.py:621
  314.6 4.6 all-to-all-start.1
  319.2 14.7 %fusion.38 = f32[1024,2048]{1,0:T(8,128)} fusion(bf16[1024,2048]{1,0:T(8,128)(2,1)} %get-tuple-element.20, bf16[2048,2048]{1,0:T(8,128)(2,1)} %down_ref.1), kind=kOutput, calls=%fused_computation.123 | convolution fusion | flops 8589934592 | bytes 20971520 | tf_op jit(solution)/shard_map/dot_general | solution.py:42
  333.9 13.3 %fusion.39 = f32[1024,2048]{1,0:T(8,128)} fusion(bf16[1024,2048]{1,0:T(8,128)(2,1)S(1)} %copy-done.4, bf16[2048,2048]{1,0:T(8,128)(2,1)} %get-tuple-element.24), kind=kOutput, calls=%fused_computation.124 | convolution fusion | flops 8589934592 | bytes 20971520 | tf_op jit(solution)/shard_map/dot_general | solution.py:38
  354.4 36.7 %all-to-all-done.1 = bf16[8,1,4,2,128,128]{5,4,3,2,1,0:T(8,128)(2,1)} async-done(((bf16[8,1,4,2,128,128]{5,4,3,2,1,0:T(8,128)(2,1)}), bf16[8,1,4,2,128,128]{5,4,3,2,1,0:T(8,128)(2,1)}, u32[]{:S(2)}, u32[]{:S(2)}) %all-to-all-start.1) | async-done | bytes 2097184 | tf_op jit(solution)/shard_map/all_to_all | solution.py:771
  391.1 4.5 copy.81
  402.0 14.3 %fusion.36 = (bf16[1024,2048]{1,0:T(8,128)(2,1)}, f32[1024,2048]{1,0:T(8,128)}) fusion(f32[1024,2048]{1,0:T(8,128)} %fusion.39, bf16[2048,1536]{1,0:T(8,128)(2,1)} %get-tuple-element.25, bf16[1024,512]{1,0:T(8,128)(2,1)S(1)} %get-tuple-element.40, bf16[1024,512]{1,0:T(8,128)(2,1)S(1)} %get-tuple-element.41, bf16[1024,512]{1,0:T(8,128)(2,1)S(1)} %get-tuple-element.39), kind=kOutput, calls=%fused_computation.121 | convolution fusion | flops 6456082432 | bytes 30408704 | tf_op jit(solution)/shard_map/dot_general | solution.py:38
  420.1 7.0 fusion.37
  429.3 9.1 %convolution_convert_fusion.2 = bf16[2048,1536]{1,0:T(8,128)(2,1)S(1)} fusion(bf16[1024,2048]{1,0:T(8,128)(2,1)} %get-tuple-element.26, bf16[1024,512]{1,0:T(8,128)(2,1)S(1)} %get-tuple-element.40, bf16[1024,512]{1,0:T(8,128)(2,1)} %copy-done.5, bf16[1024,512]{1,0:T(8,128)(2,1)S(1)} %get-tuple-element.39), kind=kOutput, calls=%fused_computation.5 | convolution fusion | flops 6455033856 | bytes 13631488 | tf_op jit(solution)/shard_map/dot_general | solution.py:34
  444.0 3.6 convolution_convert_fusion.3
  449.8 7.4 convert_add_fusion
  458.7 5.4 convert_add_fusion.1
  469.3 13.4 %collective-permute-done.17 = bf16[2,2,64,2048]{3,2,0,1:T(8,128)(2,1)S(1)} collective-permute-done((bf16[2,2,64,2048]{3,2,0,1:T(8,128)(2,1)S(1)}, bf16[2,2,64,2048]{3,2,0,1:T(8,128)(2,1)S(1)}, u32[]{:S(2)}, u32[]{:S(2)}) %collective-permute-start.17) | collective-permute-done | bytes 1048608 | tf_op jit(solution)/shard_map/ppermute | solution.py:47
  487.7 59.7 %collective-permute-done.18 = bf16[2,64,2048]{2,1,0:T(8,128)(2,1)S(1)} collective-permute-done((bf16[2,64,2048]{2,1,0:T(8,128)(2,1)S(1)}, bf16[2,64,2048]{2,1,0:T(8,128)(2,1)S(1)}, u32[]{:S(2)}, u32[]{:S(2)}) %collective-permute-start.18) | collective-permute-done | bytes 524320 | tf_op jit(solution)/shard_map/ppermute | solution.py:47
  550.7 3.4 fusion.8
  554.2 17.8 %collective-permute-done.2 = bf16[256,2048]{1,0:T(8,128)(2,1)} collective-permute-done((bf16[256,2048]{1,0:T(8,128)(2,1)S(1)}, bf16[256,2048]{1,0:T(8,128)(2,1)}, u32[]{:S(2)}, u32[]{:S(2)}) %collective-permute-start.2) | collective-permute-done | bytes 1048608 | tf_op jit(solution)/shard_map/ppermute | solution.py:47
  572.0 5.3 convert_reduce_fusion.3
  585.2 12.3 %collective-permute-done.8 = f32[10240]{0:T(1024)S(1)} collective-permute-done((f32[10240]{0:T(1024)S(1)}, f32[10240]{0:T(1024)S(1)}, u32[]{:S(2)}, u32[]{:S(2)}) %collective-permute-start.8) | collective-permute-done | bytes 40992 | tf_op jit(solution)/shard_map/ppermute | solution.py:47
  604.8 41.0 %collective-permute-done.23 = f32[10240]{0:T(1024)S(1)} collective-permute-done((f32[10240]{0:T(1024)S(1)}, f32[10240]{0:T(1024)S(1)}, u32[]{:S(2)}, u32[]{:S(2)}) %collective-permute-start.23) | collective-permute-done | bytes 40992 | tf_op jit(solution)/shard_map/ppermute | solution.py:47
  662.1 35.4 %collective-permute-done.27 = bf16[4,64,2048]{2,1,0:T(8,128)(2,1)S(1)} collective-permute-done((bf16[4,64,2048]{2,1,0:T(8,128)(2,1)S(1)}, bf16[4,64,2048]{2,1,0:T(8,128)(2,1)S(1)}, u32[]{:S(2)}, u32[]{:S(2)}) %collective-permute-start.27) | collective-permute-done | bytes 1048608 | tf_op jit(solution)/shard_map/ppermute | solution.py:47
  699.8 23.3 %collective-permute-done.12 = bf16[4,2,64,1536]{3,2,0,1:T(8,128)(2,1)S(1)} collective-permute-done((bf16[4,2,64,1536]{3,2,0,1:T(8,128)(2,1)S(1)}, bf16[4,2,64,1536]{3,2,0,1:T(8,128)(2,1)S(1)}, u32[]{:S(2)}, u32[]{:S(2)}) %collective-permute-start.12) | collective-permute-done | bytes 1572896 | tf_op jit(solution)/shard_map/ppermute | solution.py:47
  723.9 35.4 %collective-permute-done.33 = bf16[256,2048]{1,0:T(8,128)(2,1)S(1)} collective-permute-done((bf16[256,2048]{1,0:T(8,128)(2,1)S(1)}, bf16[256,2048]{1,0:T(8,128)(2,1)S(1)}, u32[]{:S(2)}, u32[]{:S(2)}) %collective-permute-start.33) | collective-permute-done | bytes 1048608 | tf_op jit(solution)/shard_map/ppermute | solution.py:47
  761.1 14.9 %collective-permute-done.13 = bf16[4,64,1536]{2,1,0:T(8,128)(2,1)S(1)} collective-permute-done((bf16[4,64,1536]{2,1,0:T(8,128)(2,1)S(1)}, bf16[4,64,1536]{2,1,0:T(8,128)(2,1)S(1)}, u32[]{:S(2)}, u32[]{:S(2)}) %collective-permute-start.13) | collective-permute-done | bytes 786464 | tf_op jit(solution)/shard_map/ppermute | solution.py:47
  779.7 3.7 collective-permute-done.16
  783.4 4.4 collective-permute-done.15
  (183 shorter events, 99.6 us)
Async XLA Ops:
  227.8 86.9 %all-to-all-start = ((bf16[8,1,4,2,128,128]{5,4,3,2,1,0:T(8,128)(2,1)}), bf16[8,1,4,2,128,128]{5,4,3,2,1,0:T(8,128)(2,1)S(1)}, u32[]{:S(2)}, u32[]{:S(2)}) async-start(bf16[8,1,4,2,128,128]{5,4,3,2,1,0:T(8,128)(2,1)} %shard_map.230), calls=%async_computation | async-start | bytes 4194304 | tf_op jit(solution)/shard_map/all_to_all | solution.py:771
  249.9 207.3 %collective-permute-start.25 = (bf16[4,2,2,64,2048]{4,3,2,1,0:T(8,128)(2,1)}, bf16[4,2,2,64,2048]{4,3,2,1,0:T(8,128)(2,1)}, u32[]{:S(2)}, u32[]{:S(2)}) collective-permute-start(bf16[4,2,2,64,2048]{4,3,2,1,0:T(8,128)(2,1)} %dynamic-slice_bitcast_fusion), channel_id=1, source_target_pairs={{0,8},{4,12},{8,0},{12,4},{16,24},{20,28},{24,16},{28,20},{1,9},{5... | collective-permute-start | bytes 12582920 | tf_op jit(solution)/shard_map/ppermute | solution.py:47
  272.3 175.6 %collective-permute-start.31 = (bf16[2,2,256,2048]{3,2,0,1:T(8,128)(2,1)}, bf16[2,2,256,2048]{3,2,0,1:T(8,128)(2,1)}, u32[]{:S(2)}, u32[]{:S(2)}) collective-permute-start(bf16[2,2,256,2048]{3,2,0,1:T(8,128)(2,1)} %bitcast.147), channel_id=1, source_target_pairs={{0,4},{4,0},{8,12},{12,8},{16,20},{20,16},{24,28},{28,24},{1,5},{5... | collective-permute-start | bytes 12582920 | tf_op jit(solution)/shard_map/ppermute | solution.py:47
  314.6 76.5 %all-to-all-start.1 = ((bf16[8,1,4,2,128,128]{5,4,3,2,1,0:T(8,128)(2,1)}), bf16[8,1,4,2,128,128]{5,4,3,2,1,0:T(8,128)(2,1)}, u32[]{:S(2)}, u32[]{:S(2)}) async-start(bf16[8,1,4,2,128,128]{5,4,3,2,1,0:T(8,128)(2,1)} %shard_map.231), calls=%async_computation.1 | async-start | bytes 4194304 | tf_op jit(solution)/shard_map/all_to_all | solution.py:771
  419.6 46.2 %collective-permute-start.4 = (bf16[256,2048]{1,0:T(8,128)(2,1)}, bf16[256,2048]{1,0:T(8,128)(2,1)}, u32[]{:S(2)}, u32[]{:S(2)}) collective-permute-start(bf16[256,2048]{1,0:T(8,128)(2,1)} %get-tuple-element.38), channel_id=1, source_target_pairs={{0,1},{1,0},{2,3},{3,2},{4,5},{5,4},{6,7},{7,6},{8,9},{9,8},{10,11... | collective-permute-start | bytes 3145736 | tf_op jit(solution)/shard_map/ppermute | solution.py:47
  419.6 129.7 %collective-permute-start.3 = (bf16[256,2048]{1,0:T(8,128)(2,1)}, bf16[256,2048]{1,0:T(8,128)(2,1)}, u32[]{:S(2)}, u32[]{:S(2)}) collective-permute-start(bf16[256,2048]{1,0:T(8,128)(2,1)} %get-tuple-element.37), channel_id=1, source_target_pairs={{0,1},{1,0},{2,3},{3,2},{4,5},{5,4},{6,7},{7,6},{8,9},{9,8},{10,11... | collective-permute-start | bytes 3145736 | tf_op jit(solution)/shard_map/ppermute | solution.py:47
  428.6 56.0 %collective-permute-start.1 = (bf16[256,2048]{1,0:T(8,128)(2,1)}, bf16[256,2048]{1,0:T(8,128)(2,1)}, u32[]{:S(2)}, u32[]{:S(2)}) collective-permute-start(bf16[256,2048]{1,0:T(8,128)(2,1)} %get-tuple-element.43), channel_id=1, source_target_pairs={{0,1},{1,0},{2,3},{3,2},{4,5},{5,4},{6,7},{7,6},{8,9},{9,8},{10,11... | collective-permute-start | bytes 3145736 | tf_op jit(solution)/shard_map/ppermute | solution.py:47
  447.9 106.3 %collective-permute-start = (bf16[256,2048]{1,0:T(8,128)(2,1)}, bf16[256,2048]{1,0:T(8,128)(2,1)}, u32[]{:S(2)}, u32[]{:S(2)}) collective-permute-start(bf16[256,2048]{1,0:T(8,128)(2,1)} %get-tuple-element.42), channel_id=1, source_target_pairs={{0,1},{1,0},{2,3},{3,2},{4,5},{5,4},{6,7},{7,6},{8,9},{9,8},{10,11... | collective-permute-start | bytes 3145736 | tf_op jit(solution)/shard_map/ppermute | solution.py:47
  457.2 25.6 %collective-permute-start.17 = (bf16[2,2,64,2048]{3,2,0,1:T(8,128)(2,1)S(1)}, bf16[2,2,64,2048]{3,2,0,1:T(8,128)(2,1)S(1)}, u32[]{:S(2)}, u32[]{:S(2)}) collective-permute-start(bf16[2,2,64,2048]{3,2,0,1:T(8,128)(2,1)S(1)} %bitcast.168), channel_id=1, source_target_pairs={{0,8},{4,12},{8,0},{12,4},{16,24},{20,28},{24,16},{28,20},{1,9},{5... | collective-permute-start | bytes 3145736 | tf_op jit(solution)/shard_map/ppermute | solution.py:47
  465.7 187.7 %collective-permute-start.11 = (bf16[4,2,2,64,1536]{4,3,0,1,2:T(8,128)(2,1)}, bf16[4,2,2,64,1536]{4,3,0,1,2:T(8,128)(2,1)}, u32[]{:S(2)}, u32[]{:S(2)}) collective-permute-start(bf16[4,2,2,64,1536]{4,3,0,1,2:T(8,128)(2,1)} %bitcast.148), channel_id=1, source_target_pairs={{0,4},{4,0},{8,12},{12,8},{16,20},{20,16},{24,28},{28,24},{1,5},{5... | collective-permute-start | bytes 9437192 | tf_op jit(solution)/shard_map/ppermute | solution.py:47
  482.7 68.0 %collective-permute-start.5 = (bf16[256,2048]{1,0:T(8,128)(2,1)S(1)}, bf16[256,2048]{1,0:T(8,128)(2,1)S(1)}, u32[]{:S(2)}, u32[]{:S(2)}) collective-permute-start(bf16[256,2048]{1,0:T(8,128)(2,1)S(1)} %fusion.16), channel_id=1, source_target_pairs={{0,2},{1,3},{2,0},{3,1},{4,6},{5,7},{6,4},{7,5},{8,10},{9,11},{10,... | collective-permute-start | bytes 3145736 | tf_op jit(solution)/shard_map/ppermute | solution.py:47
  484.7 62.8 %collective-permute-start.18 = (bf16[2,64,2048]{2,1,0:T(8,128)(2,1)S(1)}, bf16[2,64,2048]{2,1,0:T(8,128)(2,1)S(1)}, u32[]{:S(2)}, u32[]{:S(2)}) collective-permute-start(bf16[2,64,2048]{2,1,0:T(8,128)(2,1)S(1)} %fusion.28), channel_id=1, source_target_pairs={{0,4},{4,0},{8,12},{12,8},{16,20},{20,16},{24,28},{28,24},{1,5},{5... | collective-permute-start | bytes 1572872 | tf_op jit(solution)/shard_map/ppermute | solution.py:47
  547.4 24.6 %collective-permute-start.2 = (bf16[256,2048]{1,0:T(8,128)(2,1)S(1)}, bf16[256,2048]{1,0:T(8,128)(2,1)}, u32[]{:S(2)}, u32[]{:S(2)}) collective-permute-start(bf16[256,2048]{1,0:T(8,128)(2,1)S(1)} %fusion.18), channel_id=1, source_target_pairs={{0,2},{1,3},{2,0},{3,1},{4,6},{5,7},{6,4},{7,5},{8,10},{9,11},{10,... | collective-permute-start | bytes 3145736 | tf_op jit(solution)/shard_map/ppermute | solution.py:47
  549.2 102.2 %collective-permute-start.26 = (bf16[4,2,64,2048]{3,2,1,0:T(8,128)(2,1)}, bf16[4,2,64,2048]{3,2,1,0:T(8,128)(2,1)S(1)}, u32[]{:S(2)}, u32[]{:S(2)}) collective-permute-start(bf16[4,2,64,2048]{3,2,1,0:T(8,128)(2,1)} %fusion.14), channel_id=1, source_target_pairs={{0,4},{4,0},{8,12},{12,8},{16,20},{20,16},{24,28},{28,24},{1,5},{5... | collective-permute-start | bytes 6291464 | tf_op jit(solution)/shard_map/ppermute | solution.py:47
  554.1 23.2 %collective-permute-start.6 = (f32[10240]{0:T(1024)S(1)}, f32[10240]{0:T(1024)S(1)}, u32[]{:S(2)}, u32[]{:S(2)}) collective-permute-start(f32[10240]{0:T(1024)S(1)} %pad_maximum_fusion.3), channel_id=1, source_target_pairs={{0,1},{1,0},{2,3},{3,2},{4,5},{5,4},{6,7},{7,6},{8,9},{9,8},{10,11... | collective-permute-start | bytes 122888 | tf_op jit(solution)/shard_map/ppermute | solution.py:47
  581.4 16.1 %collective-permute-start.8 = (f32[10240]{0:T(1024)S(1)}, f32[10240]{0:T(1024)S(1)}, u32[]{:S(2)}, u32[]{:S(2)}) collective-permute-start(f32[10240]{0:T(1024)S(1)} %add.220), channel_id=1, source_target_pairs={{0,4},{4,0},{8,12},{12,8},{16,20},{20,16},{24,28},{28,24},{1,5},{5... | collective-permute-start | bytes 122888 | tf_op jit(solution)/shard_map/ppermute | solution.py:47
  582.8 19.7 %collective-permute-start.19 = (bf16[64,2048]{1,0:T(8,128)(2,1)S(1)}, bf16[64,2048]{1,0:T(8,128)(2,1)S(1)}, u32[]{:S(2)}, u32[]{:S(2)}) collective-permute-start(bf16[64,2048]{1,0:T(8,128)(2,1)S(1)} %fusion.29), channel_id=1, source_target_pairs={{0,16},{4,20},{8,24},{12,28},{16,0},{20,4},{24,8},{28,12},{1,17},{... | collective-permute-start | bytes 786440 | tf_op jit(solution)/shard_map/ppermute | solution.py:47
  583.4 14.9 %collective-permute-start.22 = (f32[10240]{0:T(1024)S(1)}, f32[10240]{0:T(1024)S(1)}, u32[]{:S(2)}, u32[]{:S(2)}) collective-permute-start(f32[10240]{0:T(1024)S(1)} %add.240), channel_id=1, source_target_pairs={{0,4},{4,0},{8,12},{12,8},{16,20},{20,16},{24,28},{28,24},{1,5},{5... | collective-permute-start | bytes 122888 | tf_op jit(solution)/shard_map/ppermute | solution.py:47
  598.3 60.1 %collective-permute-start.32 = (bf16[2,256,2048]{2,1,0:T(8,128)(2,1)S(1)}, bf16[2,256,2048]{2,1,0:T(8,128)(2,1)}, u32[]{:S(2)}, u32[]{:S(2)}) collective-permute-start(bf16[2,256,2048]{2,1,0:T(8,128)(2,1)S(1)} %fusion.15), channel_id=1, source_target_pairs={{0,8},{4,12},{8,0},{12,4},{16,24},{20,28},{24,16},{28,20},{1,9},{5... | collective-permute-start | bytes 6291464 | tf_op jit(solution)/shard_map/ppermute | solution.py:47
  602.0 43.8 %collective-permute-start.23 = (f32[10240]{0:T(1024)S(1)}, f32[10240]{0:T(1024)S(1)}, u32[]{:S(2)}, u32[]{:S(2)}) collective-permute-start(f32[10240]{0:T(1024)S(1)} %add.241), channel_id=1, source_target_pairs={{0,8},{4,12},{8,0},{12,4},{16,24},{20,28},{24,16},{28,20},{1,9},{5... | collective-permute-start | bytes 122888 | tf_op jit(solution)/shard_map/ppermute | solution.py:47
  602.5 44.4 %collective-permute-start.10 = (f32[10240]{0:T(1024)S(1)}, f32[10240]{0:T(1024)S(1)}, u32[]{:S(2)}, u32[]{:S(2)}) collective-permute-start(f32[10240]{0:T(1024)S(1)} %add.222), channel_id=1, source_target_pairs={{0,16},{4,20},{8,24},{12,28},{16,0},{20,4},{24,8},{28,12},{1,17},{... | collective-permute-start | bytes 122888 | tf_op jit(solution)/shard_map/ppermute | solution.py:47
  645.8 4.9 collective-permute-start.24
  652.2 45.3 %collective-permute-start.27 = (bf16[4,64,2048]{2,1,0:T(8,128)(2,1)S(1)}, bf16[4,64,2048]{2,1,0:T(8,128)(2,1)S(1)}, u32[]{:S(2)}, u32[]{:S(2)}) collective-permute-start(bf16[4,64,2048]{2,1,0:T(8,128)(2,1)S(1)} %fusion.23), channel_id=1, source_target_pairs={{0,16},{4,20},{8,24},{12,28},{16,0},{20,4},{24,8},{28,12},{1,17},{... | collective-permute-start | bytes 3145736 | tf_op jit(solution)/shard_map/ppermute | solution.py:47
  656.6 66.6 %collective-permute-start.12 = (bf16[4,2,64,1536]{3,2,0,1:T(8,128)(2,1)S(1)}, bf16[4,2,64,1536]{3,2,0,1:T(8,128)(2,1)S(1)}, u32[]{:S(2)}, u32[]{:S(2)}) collective-permute-start(bf16[4,2,64,1536]{3,2,0,1:T(8,128)(2,1)S(1)} %fusion.21), channel_id=1, source_target_pairs={{0,8},{4,12},{8,0},{12,4},{16,24},{20,28},{24,16},{28,20},{1,9},{5... | collective-permute-start | bytes 4718600 | tf_op jit(solution)/shard_map/ppermute | solution.py:47
  661.0 98.2 %collective-permute-start.33 = (bf16[256,2048]{1,0:T(8,128)(2,1)S(1)}, bf16[256,2048]{1,0:T(8,128)(2,1)S(1)}, u32[]{:S(2)}, u32[]{:S(2)}) collective-permute-start(bf16[256,2048]{1,0:T(8,128)(2,1)S(1)} %fusion.24), channel_id=1, source_target_pairs={{0,16},{4,20},{8,24},{12,28},{16,0},{20,4},{24,8},{28,12},{1,17},{... | collective-permute-start | bytes 3145736 | tf_op jit(solution)/shard_map/ppermute | solution.py:47
  697.9 62.9 %collective-permute-start.30 = (bf16[64,2048]{1,0:T(8,128)(2,1)S(1)}, bf16[64,2048]{1,0:T(8,128)(2,1)S(1)}, u32[]{:S(2)}, u32[]{:S(2)}) collective-permute-start(bf16[64,2048]{1,0:T(8,128)(2,1)S(1)} %get-tuple-element.51), channel_id=1, source_target_pairs={{0,3},{1,2},{2,1},{3,0},{4,7},{5,6},{6,5},{7,4},{8,11},{9,10},{10,... | collective-permute-start | bytes 786440 | tf_op jit(solution)/shard_map/ppermute | solution.py:47
  698.0 62.8 %collective-permute-start.29 = (bf16[64,2048]{1,0:T(8,128)(2,1)S(1)}, bf16[64,2048]{1,0:T(8,128)(2,1)S(1)}, u32[]{:S(2)}, u32[]{:S(2)}) collective-permute-start(bf16[64,2048]{1,0:T(8,128)(2,1)S(1)} %get-tuple-element.52), channel_id=1, source_target_pairs={{0,2},{1,3},{2,0},{3,1},{4,6},{5,7},{6,4},{7,5},{8,10},{9,11},{10,... | collective-permute-start | bytes 786440 | tf_op jit(solution)/shard_map/ppermute | solution.py:47
  699.5 61.4 %collective-permute-start.28 = (bf16[64,2048]{1,0:T(8,128)(2,1)S(1)}, bf16[64,2048]{1,0:T(8,128)(2,1)S(1)}, u32[]{:S(2)}, u32[]{:S(2)}) collective-permute-start(bf16[64,2048]{1,0:T(8,128)(2,1)S(1)} %get-tuple-element.53), channel_id=1, source_target_pairs={{0,1},{1,0},{2,3},{3,2},{4,5},{5,4},{6,7},{7,6},{8,9},{9,8},{10,11... | collective-permute-start | bytes 786440 | tf_op jit(solution)/shard_map/ppermute | solution.py:47
  723.7 52.3 %collective-permute-start.13 = (bf16[4,64,1536]{2,1,0:T(8,128)(2,1)S(1)}, bf16[4,64,1536]{2,1,0:T(8,128)(2,1)S(1)}, u32[]{:S(2)}, u32[]{:S(2)}) collective-permute-start(bf16[4,64,1536]{2,1,0:T(8,128)(2,1)S(1)} %fusion.27), channel_id=1, source_target_pairs={{0,16},{4,20},{8,24},{12,28},{16,0},{20,4},{24,8},{28,12},{1,17},{... | collective-permute-start | bytes 2359304 | tf_op jit(solution)/shard_map/ppermute | solution.py:47
  776.3 7.1 collective-permute-start.16
  776.4 11.4 %collective-permute-start.15 = (bf16[64,1536]{1,0:T(8,128)(2,1)S(1)}, bf16[64,1536]{1,0:T(8,128)(2,1)S(1)}, u32[]{:S(2)}, u32[]{:S(2)}) collective-permute-start(bf16[64,1536]{1,0:T(8,128)(2,1)S(1)} %get-tuple-element.63), channel_id=1, source_target_pairs={{0,2},{1,3},{2,0},{3,1},{4,6},{5,7},{6,4},{7,5},{8,10},{9,11},{10,... | collective-permute-start | bytes 589832 | tf_op jit(solution)/shard_map/ppermute | solution.py:47
  778.0 9.8 %collective-permute-start.14 = (bf16[64,1536]{1,0:T(8,128)(2,1)S(1)}, bf16[64,1536]{1,0:T(8,128)(2,1)S(1)}, u32[]{:S(2)}, u32[]{:S(2)}) collective-permute-start(bf16[64,1536]{1,0:T(8,128)(2,1)S(1)} %get-tuple-element.64), channel_id=1, source_target_pairs={{0,1},{1,0},{2,3},{3,2},{4,5},{5,4},{6,7},{7,6},{8,9},{9,8},{10,11... | collective-permute-start | bytes 589832 | tf_op jit(solution)/shard_map/ppermute | solution.py:47
  (24 other events, 522.9 us)

commit v3 on v2

--- a/solution.py
+++ b/solution.py
@@ -650,6 +650,382 @@
     )(qkv, grads, cosine, sine)
 
 
+def middle_kernel(
+    items,
+    heads,
+    qkv_in,
+    do_in,
+    hidden_in,
+    normed_in,
+    grads_in,
+    du_in,
+    cos_in,
+    sin_in,
+    back_in,
+    down_out,
+    up_out,
+    d_send,
+    d_keep,
+    d_recv,
+    d_last,
+    u_send,
+    u_keep,
+    u_recv,
+    u_last,
+    out,
+    local_sem,
+    store_sem,
+    own_sem,
+    ds_,
+    dr,
+    us,
+    ur,
+    bs,
+    br,
+):
+    place = lax.axis_index("ctx")
+    shards = out.shape[1]
+    x_at, z_at = place % 2, (place // 2) % 2
+    near, over = {"ctx": place ^ 1}, {"ctx": place ^ 2}
+    barrier = pltpu.get_barrier_semaphore()
+    for k in range(1, shards):
+        pl.semaphore_signal(
+            barrier, inc=1, device_id={"ctx": place ^ k}, device_id_type=pl.DeviceIdType.MESH
+        )
+
+    def fetch(src, dst, at):
+        copy = pltpu.make_async_copy(src, dst, local_sem.at[at])
+        copy.start()
+        return copy
+
+    def block(at, size):
+        return pl.ds(pl.multiple_of(at, size), size)
+
+    members, tops, lanes, width = u_send.shape
+    wide = lanes * 2 * tops
+    units = d_send.shape[2]
+    piece = lanes // 2
+
+    def down_one(top):
+        return remote(d_send.at[top], d_recv.at[top], ds_, dr, top, near)
+
+    def down_two(top):
+        return remote(d_send.at[top, 0], d_last.at[top], ds_, dr, tops + top, over)
+
+    def up_one(member):
+        return remote(u_send.at[member], u_recv.at[member], us, ur, member, over)
+
+    def up_two(member):
+        return remote(
+            u_send.at[member, :, pl.ds(0, piece)], u_last.at[member], us, ur, members + member, near
+        )
+
+    def back_one(item, part, k):
+        return remote(
+            out.at[item, place ^ k, :, part],
+            back_in.at[item, place, :, part],
+            bs,
+            br,
+            (item * 2 + part) * shards + k,
+            {"ctx": place ^ k},
+        )
+
+    def back_own(item, part):
+        return pltpu.make_async_copy(
+            out.at[item, place, :, part],
+            back_in.at[item, place, :, part],
+            own_sem.at[item * 2 + part],
+        )
+
+    def sums(hidden, normed, grads, du):
+        loads = [
+            fetch(src, dst, at)
+            for at, (src, dst) in enumerate(
+                ((hidden_in, hidden), (grads_in, grads), (normed_in, normed), (du_in, du))
+            )
+        ]
+        loads[0].wait()
+        loads[1].wait()
+        pl.semaphore_wait(barrier, shards - 1)
+
+        def down(which, into, top):
+            def one(low, _):
+                at = ((top * 2 + low) * 2 + which) * units
+                into[top, low] = contract_rows(hidden[:, block(at, units)], grads[...]).astype(BF16)
+                return 0
+
+            lax.fori_loop(0, 2, one, 0)
+
+        for top in range(tops):
+            down(1 - x_at, d_send, top)
+            down_one(top).start()
+        loads[2].wait()
+        loads[3].wait()
+
+        def up(which, into, member):
+            def one(top, _):
+                at = member * wide + (top * 2 + which) * lanes
+                into[member, top] = contract_rows(normed[:, block(at, lanes)], du[...]).astype(BF16)
+                return 0
+
+            lax.fori_loop(0, tops, one, 0)
+
+        for member in range(members):
+            up(1 - z_at, u_send, member)
+            up_one(member).start()
+        for top in range(tops):
+            down(x_at, d_keep, top)
+        for member in range(members):
+            up(z_at, u_keep, member)
+
+    tokens = hidden_in.shape[0]
+    pl.run_scoped(
+        sums,
+        pltpu.VMEM(hidden_in.shape, BF16),
+        pltpu.VMEM((tokens, width), BF16),
+        pltpu.VMEM((tokens, width), BF16),
+        pltpu.VMEM(du_in.shape, BF16),
+    )
+
+    half = out.shape[-2]
+    size = 2 * half
+
+    def attention(qkv, do, cosine, sine, s_buf, dp_buf, dk_buf, dv_buf):
+        loads = []
+        for item in range(items):
+            loads.append(fetch(qkv_in.at[item], qkv.at[item], 2 * item))
+            loads.append(fetch(do_in.at[:, item], do.at[item], 2 * item + 1))
+        loads.append(fetch(cos_in, cosine, 2 * items))
+        loads.append(fetch(sin_in, sine, 2 * items + 1))
+        for load in loads:
+            load.wait()
+        lane = lax.broadcasted_iota(jnp.int32, (size, LANES), 1) // HD
+        own = [lane == h for h in range(heads)]
+        key_at = lax.broadcasted_iota(jnp.int32, (size, size), 0)
+        query_at = lax.broadcasted_iota(jnp.int32, (size, size), 1)
+        nothing = jnp.zeros((size, LANES), BF16)
+        scale = HD**-0.5
+
+        for item in range(items):
+            dk_buf[...] = jnp.zeros_like(dk_buf)
+            dv_buf[...] = jnp.zeros_like(dv_buf)
+            for part in (1, 0):
+
+                def where_is(at, part=part):
+                    if part:
+                        return 2 * shards - 1 - 2 * at, 2 * shards - 2 - 2 * at
+                    return 2 * at, 2 * at + 1
+
+                def shard_of(at):
+                    low = at < shards // 2
+                    first = jnp.where(low, 2 * at, 2 * shards - 1 - 2 * at)
+                    second = jnp.where(low, 2 * at + 1, 2 * shards - 2 - 2 * at)
+                    return first, second, jnp.where(low, 0, 1)
+
+                def load(which, at, item=item):
+                    first, second, side = shard_of(at)
+                    return jnp.concatenate(
+                        [qkv[item, first, which, side], qkv[item, second, which, side]], axis=0
+                    )
+
+                def store(which, at, value, item=item, part=part, where_is=where_is):
+                    first, second = where_is(at)
+                    out[item, first, which, part] = value[:half].astype(BF16)
+                    out[item, second, which, part] = value[half:].astype(BF16)
+
+                def per_query(at, _, item=item, load=load, store=store, shard_of=shard_of):
+                    query = load(0, at) * jnp.asarray(scale, BF16)
+                    first, second, where = shard_of(at)
+                    grad = jnp.concatenate([do[item, first, where], do[item, second, where]], axis=0)
+                    queries = [jnp.where(own[h], query, nothing) for h in range(heads)]
+                    grads = [jnp.where(own[h], grad, nothing) for h in range(heads)]
+
+                    def measure(key, state, diagonal):
+                        keys, values = load(1, key), load(2, key)
+                        new = []
+                        for h in range(heads):
+                            top, total, dot = state[h]
+                            s = contract_cols(keys, queries[h])
+                            if diagonal:
+                                s = jnp.where(key_at <= query_at, s, -1e30)
+                            dp = contract_cols(values, grads[h])
+                            s_buf[h, key] = s
+                            dp_buf[h, key] = dp
+                            new_top = jnp.maximum(top, jnp.max(s, axis=0, keepdims=True))
+                            e = jnp.exp(s - new_top)
+                            fade = jnp.exp(top - new_top)
+                            new.append(
+                                (
+                                    new_top,
+                                    total * fade + jnp.sum(e, axis=0, keepdims=True),
+                                    dot * fade + jnp.sum(e * dp, axis=0, keepdims=True),
+                                )
+                            )
+                        return tuple(new)
+
+                    zero = jnp.zeros((1, size), F32)
+                    start = tuple((zero - 1e30, zero, zero) for _ in range(heads))
+                    state = lax.fori_loop(0, at, lambda k, st: measure(k, st, False), start)
+                    state = measure(at, state, True)
+                    logs = [top + jnp.log(total) for top, total, _ in state]
+                    deltas = [dot / total for _, total, dot in state]
+
+                    def apply(key, state):
+                        keys, values = load(1, key), load(2, key)
+                        attended, dq = state
+                        dk, dv = dk_buf[key], dv_buf[key]
+                        for h in range(heads):
+                            p = jnp.exp(s_buf[h, key] - logs[h])
+                            ds = (p * (dp_buf[h, key] - deltas[h])).astype(BF16)
+                            p = p.astype(BF16)
+                            dv = dv + matmul(p, grads[h])
+                            dk = dk + matmul(ds, queries[h])
+                            attended = attended + jnp.where(own[h], contract_rows(p, values), 0.0)
+                            dq = dq + jnp.where(own[h], contract_rows(ds, keys), 0.0)
+                        dk_buf[key] = dk
+                        dv_buf[key] = dv
+                        return attended, dq
+
+                    empty = jnp.zeros((size, LANES), F32)
+                    attended, dq = lax.fori_loop(0, at + 1, apply, (empty, empty))
+                    store(0, at, attended)
+                    rows = block(at * size, size)
+                    store(1, at, turn(dq * scale, cosine[rows, :], -sine[rows, :]))
+                    return 0
+
+                low = part * (shards // 2)
+                lax.fori_loop(low, low + shards // 2, per_query, 0)
+
+                def finish(at, _, store=store):
+                    rows = block(at * size, size)
+                    store(2, at, turn(dk_buf[at], cosine[rows, :], -sine[rows, :]))
+                    store(3, at, dv_buf[at])
+                    return 0
+
+                lax.fori_loop(low, low + shards // 2, finish, 0)
+                for k in range(1, shards):
+                    back_one(item, part, k).start()
+                back_own(item, part).start()
+
+    pl.run_scoped(
+        attention,
+        pltpu.VMEM((items,) + qkv_in.shape[1:], BF16),
+        pltpu.VMEM((items, shards) + do_in.shape[2:], BF16),
+        pltpu.VMEM(cos_in.shape, F32),
+        pltpu.VMEM(sin_in.shape, F32),
+        pltpu.VMEM((heads, shards, size, size), F32),
+        pltpu.VMEM((heads, shards, size, size), F32),
+        pltpu.VMEM((shards, size, LANES), F32),
+        pltpu.VMEM((shards, size, LANES), F32),
+    )
+
+    for top in range(tops):
+        down_one(top).wait()
+    for top in range(tops):
+        d_send[top, 0] = (
+            d_keep[top, 1 - z_at].astype(F32) + d_recv[top, 1 - z_at].astype(F32)
+        ).astype(BF16)
+        down_two(top).start()
+    theirs = block((1 - x_at) * piece, piece)
+    mine = block(x_at * piece, piece)
+    for member in range(members):
+        up_one(member).wait()
+    for member in range(members):
+        for top in range(tops):
+            u_send[member, top, pl.ds(0, piece)] = (
+                u_keep[member, top, theirs].astype(F32) + u_recv[member, top, theirs].astype(F32)
+            ).astype(BF16)
+        up_two(member).start()
+    stores = []
+    for top in range(tops):
+        d_keep[top, z_at] = (
+            d_keep[top, z_at].astype(F32) + d_recv[top, z_at].astype(F32)
+        ).astype(BF16)
+    for member in range(members):
+        for top in range(tops):
+            u_keep[member, top, mine] = (
+                u_keep[member, top, mine].astype(F32) + u_recv[member, top, mine].astype(F32)
+            ).astype(BF16)
+    for top in range(tops):
+        down_two(top).wait_recv()
+        d_last[top] = (d_keep[top, z_at].astype(F32) + d_last[top].astype(F32)).astype(BF16)
+        stores.append(pltpu.make_async_copy(d_last.at[top], down_out.at[top], store_sem.at[top]))
+        stores[-1].start()
+    for member in range(members):
+        up_two(member).wait_recv()
+        for top in range(tops):
+            u_last[member, top] = (
+                u_keep[member, top, mine].astype(F32) + u_last[member, top].astype(F32)
+            ).astype(BF16)
+        stores.append(
+            pltpu.make_async_copy(u_last.at[member], up_out.at[member], store_sem.at[tops + member])
+        )
+        stores[-1].start()
+    for item in range(items):
+        for part in (1, 0):
+            for k in range(1, shards):
+                back_one(item, part, k).wait()
+            back_own(item, part).wait()
+    for top in range(tops):
+        down_two(top).wait_send()
+    for member in range(members):
+        up_two(member).wait_send()
+    for copy in stores:
+        copy.wait()
+
+
+def middle(qkv_in, do_in, hidden, normed, grads, du, cosine, sine, heads, groups):
+    items, shards = qkv_in.shape[:2]
+    half = qkv_in.shape[-2]
+    width = normed.shape[1]
+    deep = hidden.shape[1]
+    units = deep // shards
+    tops = shards // 4
+    lanes = width // groups // tops // 2
+    apart = pl.BlockSpec(memory_space=pl.ANY)
+    dma = pltpu.SemaphoreType.DMA
+    shape = jax.ShapeDtypeStruct
+    pairs = shards * (shards + 1) // 2 * items * heads
+    return pl.pallas_call(
+        partial(middle_kernel, items, heads),
+        out_shape=[
+            shape((items, shards, 4, 2, half, LANES), BF16),
+            shape((tops, units, width), BF16),
+            shape((groups, tops, lanes // 2, deep), BF16),
+        ],
+        in_specs=[apart] * 8,
+        out_specs=[apart] * 3,
+        scratch_shapes=[
+            pltpu.VMEM((tops, 2, units, width), BF16),
+            pltpu.VMEM((tops, 2, units, width), BF16),
+            pltpu.VMEM((tops, 2, units, width), BF16),
+            pltpu.VMEM((tops, units, width), BF16),
+            pltpu.VMEM((groups, tops, lanes, deep), BF16),
+            pltpu.VMEM((groups, tops, lanes, deep), BF16),
+            pltpu.VMEM((groups, tops, lanes, deep), BF16),
+            pltpu.VMEM((groups, tops, lanes // 2, deep), BF16),
+            pltpu.VMEM((items, shards, 4, 2, half, LANES), BF16),
+            dma((max(4, 2 * items + 2),)),
+            dma((tops + groups,)),
+            dma((2 * items,)),
+            dma((2 * tops,)),
+            dma((2 * tops,)),
+            dma((2 * groups,)),
+            dma((2 * groups,)),
+            dma((2 * items * shards,)),
+            dma((2 * items * shards,)),
+        ],
+        compiler_params=pltpu.CompilerParams(
+            collective_id=1, has_side_effects=True, vmem_limit_bytes=63 * 2**20
+        ),
+        cost_estimate=pl.CostEstimate(
+            flops=pairs * 10 * (2 * half) ** 2 * 256 + 8 * width * deep * hidden.shape[0],
+            bytes_accessed=40 * 2**20,
+            transcendentals=2 * pairs * (2 * half) ** 2,
+        ),
+    )(qkv_in, do_in, hidden, normed, grads, du, cosine, sine)
+
+
 def scatter_sum(parts, axis_at, place, bits):
     lead, tail = parts.shape[:axis_at], parts.shape[axis_at + 1 :]
     total = len(bits)
@@ -664,6 +1040,13 @@
         got = swap(send.astype(BF16), "ctx", 1 << bit)
         value = keep.astype(F32) + got.astype(F32)
     return value
+
+
+def last_half(value, axis_at, place):
+    mine = (place // 4) % 2
+    send = lax.dynamic_index_in_dim(value, 1 - mine, axis_at, keepdims=False)
+    keep = lax.dynamic_index_in_dim(value, mine, axis_at, keepdims=False)
+    return keep.astype(F32) + swap(send, "ctx", 4).astype(F32)
 
 
 def scatter_rows(parts):
@@ -747,31 +1130,108 @@
         dup,
     )
 
-    down_grad = contract_rows(hidden, grads).astype(BF16)
-    up_grad = contract_rows(normed, grad_up).astype(BF16)
+    def assembled(back):
+        back = back.reshape(pairs, slot_groups, dup, 4, rows, LANES)
+        back = jnp.sum(back, axis=2) if dup > 1 else back[:, :, 0]
+        return back.transpose(2, 1, 3, 0, 4).reshape(4, slot_groups * rows, wide)
+
     hw = deep // shards
-    down_weight_grad = scatter_sum(
-        down_grad.reshape(shards, hw, width), 0, place, x_first
-    )
-    up_part = scatter_sum(
-        up_grad.reshape(groups, shards, wide // shards, deep), 1, place, z_first
-    )
-
-    backs = []
-    for item in range(per_group):
-        back = attend(
+    if len(x_first) == 3 and dup == 1:
+        back_in, down_sum, up_sum = middle(
             qkv_in.reshape(per_group, shards, 3, 2, half, LANES),
             grad_in.reshape(shards, per_group, 2, half, LANES),
-            item,
+            hidden,
+            normed,
+            grads,
+            grad_up,
             cos_full,
             sin_full,
             heads,
-            dup,
-        )
-        back = lax.all_to_all(back, "ctx", 0, 0)
-        back = back.reshape(pairs, slot_groups, dup, 4, rows, LANES)
-        back = jnp.sum(back, axis=2) if dup > 1 else back[:, :, 0]
-        backs.append(back.transpose(2, 1, 3, 0, 4).reshape(4, slot_groups * rows, wide))
+            groups,
+        )
+        backs = [assembled(back_in[item]) for item in range(per_group)]
+        down_weight_grad = last_half(down_sum, 0, place)
+        up_part = last_half(up_sum, 1, place)
+    else:
+        down_grad = contract_rows(hidden, grads).astype(BF16)
+        up_grad = contract_rows(normed, grad_up).astype(BF16)
+        down_weight_grad = scatter_sum(
+            down_grad.reshape(shards, hw, width), 0, place, x_first
+        )
+        up_part = scatter_sum(
+            up_grad.reshape(groups, shards, wide // shards, deep), 1, place, z_first
+        )
+
+        backs = []
+        for item in range(per_group):
+            back = attend(
+                qkv_in.reshape(per_group, shards, 3, 2, half, LANES),
+                grad_in.reshape(shards, per_group, 2, half, LANES),
+                item,
+                cos_full,
+                sin_full,
+                heads,
+                dup,
+            )
+            back = lax.all_to_all(back, "ctx", 0, 0)
+            back = back.reshape(pairs, slot_groups, dup, 4, rows, LANES)
+            back = jnp.sum(back, axis=2) if dup > 1 else back[:, :, 0]
+            backs.append(back.transpose(2, 1, 3, 0, 4).reshape(4, slot_groups * rows, wide))
+        back = jnp.concatenate(backs, axis=1)
+        attended = back[0]
+        grad_qkv = jnp.concatenate([back[1], back[2], back[3]], axis=1)
+
+        share = matmul(hidden, down_weight) + matmul(attended, out_weight)
+        result = tokens + scatter_rows(list(share.reshape(groups, rows, width))) + out_bias + down_bias
+
+        grad_share = contract_cols(grad_up, up_own) + contract_cols(grad_qkv, qkv_own)
+        grad_normed = scatter_rows(list(grad_share.reshape(groups, rows, width)))
+        grad_full = grad_low.astype(F32)
+        grad_normal = grad_normed * norm_gain
+        grad_tokens = inv_scale * (
+            grad_normal
+            - jnp.mean(grad_normal, axis=-1, keepdims=True)
+            - normal * jnp.mean(grad_normal * normal, axis=-1, keepdims=True)
+        )
+        input_grad = (grad_full + grad_tokens).astype(BF16)
+
+        qkv_grad = contract_rows(normed, grad_qkv).astype(BF16)
+        out_grad = contract_rows(attended, grads).astype(BF16)
+        ow = wide // shards
+        out_weight_grad = scatter_sum(out_grad.reshape(shards, ow, width), 0, place, z_first)
+        qkv_part = scatter_sum(
+            qkv_grad.reshape(groups, shards, ow, 3 * wide), 1, place, x_first
+        )
+
+        def relative(value):
+            return [
+                lax.dynamic_index_in_dim(value, member ^ j, 0, keepdims=False) for j in range(groups)
+            ]
+
+        def exchange(part):
+            sent = relative(part.astype(BF16))
+            got = [sent[0]] + [swap(sent[j], "fsdp", j) for j in range(1, groups)]
+            return relative(jnp.stack(got))
+
+        up_weight_grad = jnp.concatenate(exchange(up_part), axis=1).astype(F32)
+        qkv_weight_grad = jnp.concatenate(
+            [item.reshape(ow, 3, 1, wide) for item in exchange(qkv_part)], axis=2
+        ).reshape(ow, 3 * width).astype(F32)
+
+        qkv_bias_cols = jnp.sum(grad_qkv.astype(F32), axis=0).reshape(3, 1, wide)
+        backs = []
+        for item in range(per_group):
+            back = attend(
+                qkv_in.reshape(per_group, shards, 3, 2, half, LANES),
+                grad_in.reshape(shards, per_group, 2, half, LANES),
+                item,
+                cos_full,
+                sin_full,
+                heads,
+                dup,
+            )
+            back = lax.all_to_all(back, "ctx", 0, 0)
+            backs.append(assembled(back))
     back = jnp.concatenate(backs, axis=1)
     attended = back[0]
     grad_qkv = jnp.concatenate([back[1], back[2], back[3]], axis=1)

time: 801 us -> 750 us (0.936)
  Pallas kernels: 264 us -> 407 us
  waiting for transfers between devices: 304 us -> 175 us
  matrix products: 85.5 us -> 61.6 us
  starting transfers between devices: 42 us -> 22.9 us
  other arithmetic: 40.9 us -> 24.7 us
    pallas_call x2 -> x1, Pallas kernels: 73.2 us -> 217 us  [middle(): pl.pallas_call(partial(middle_kernel, items, heads), out_shape=[shape((it...]
    ppermute x34 -> x30, waiting for transfers between devices: 267 us -> 175 us  [swap(): return lax.ppermute(value, axis, [(i, i ^ bit) for i in range(size)])]
    all_to_all x2 -> x0, waiting for transfers between devices: 36.7 us -> none  [on_device(): back = lax.all_to_all(back, 'ctx', 0, 0)]
    dot_general x4 -> x2, matrix products: 36.1 us -> 15.4 us  [contract_rows(): lax.dot_general(left, right, (((0,), (0,)), ((), ())), preferred_element_...]
    add x10 -> x5, other arithmetic: 22.2 us -> 4.68 us  [scatter_sum(): value = keep.astype(F32) + got.astype(F32)]
    ppermute x34 -> x30, starting transfers between devices: 33.7 us -> 22.9 us  [swap(): return lax.ppermute(value, axis, [(i, i ^ bit) for i in range(size)])]
    all_to_all x2 -> x0, starting transfers between devices: 8.37 us -> none  [on_device(): back = lax.all_to_all(back, 'ctx', 0, 0)]
  transfers between devices with their start and end apart: 36 -> 30, of which waited for: 15 -> 11; matrix products, arithmetic and copies ran while one was open for 21% -> 10% of each run, Pallas kernels for 5% -> 0%
where the time goes in v3:
time: 750 us; the launch traced here: 741 us
  Pallas kernels  407 us (54%)
  waiting for transfers between devices  175 us (23%)
  matrix products  61.6 us (8%)
  local copies, waits for them, and re-layouts  47.8 us (6%)
  other arithmetic  24.7 us (3%)
  starting transfers between devices  22.9 us (3%)
    pallas_call x1, Pallas kernels, middle(): pl.pallas_call(partial(middle_kernel, items, heads), out_shape=[shape((it...  217 us
    pallas_call x1, Pallas kernels, begin_layer(): pl.pallas_call(partial(start_kernel, shards, groups, pairs, slot_groups,...  191 us
    ppermute x30, waiting for transfers between devices, swap(): return lax.ppermute(value, axis, [(i, i ^ bit) for i in range(size)])  175 us
    dot_general x2, matrix products, contract_cols(): lax.dot_general(left, right, (((1,), (1,)), ((), ())), preferred_element_...  27.6 us
    ppermute x30, starting transfers between devices, swap(): return lax.ppermute(value, axis, [(i, i ^ bit) for i in range(size)])  22.9 us
    dot_general x2, matrix products, matmul(): return jnp.dot(left, right, preferred_element_type=F32)  18.6 us
    dot_general x2, matrix products, contract_rows(): lax.dot_general(left, right, (((0,), (0,)), ((), ())), preferred_element_...  15.4 us
  transfers between devices with their start and end apart: 30, of which 11 were waited for; matrix products, arithmetic and copies ran while one was open for 10% of the time, Pallas kernels for 0%

profile of v3, /device:TPU:0, one launch (start us, length us, event | category | flops | bytes accessed | tf_op | source)
XLA Modules:
  0.0 740.5 jit_solution(1323171116895120730)
XLA Ops:
  0.6 190.5 %shard_map.229 = (bf16[1024,2048]{1,0:T(8,128)(2,1)}, bf16[1024,2048]{1,0:T(8,128)(2,1)}, bf16[2048,1536]{1,0:T(8,128)(2,1)}, bf16[2048,2048]{1,0:T(8,128)(2,1)}...) custom-call(bf16[256,2048]{1,0:T(8,128)(2,1)} %bitcast.125, ...), custom_call_target="tpu_custom_call" | custom-call | flops 25769803776 | bytes 62914560 | tf_op jit(solution)/shard_map/pallas_call | solution.py:441
  191.2 14.5 %fusion.36 = f32[1024,2048]{1,0:T(8,128)} fusion(bf16[1024,2048]{1,0:T(8,128)(2,1)} %get-tuple-element.28.du_in, bf16[2048,2048]{1,0:T(8,128)(2,1)} %get-tuple-element.30), kind=kOutput, calls=%fused_computation.108 | convolution fusion | flops 8589934592 | bytes 20971520 | tf_op jit(solution)/shard_map/dot_general | solution.py:38
  205.7 216.9 %shard_map.230 = (bf16[2,8,4,2,128,128]{5,4,3,2,1,0:T(8,128)(2,1)}, bf16[2,256,2048]{2,1,0:T(8,128)(2,1)}, bf16[4,2,64,2048]{3,2,1,0:T(8,128)(2,1)}) custom-call(bf16[2,8,3,2,128,128]{5,4,3,2,1,0:T(8,128)(2,1)} %bitcast.151, bf16[8,2,2,128,128]{4,3,2,1,0:T(8,128)(2,1)} %bitcast.152, bf16[1024,2048]{1,0:T(8,128)(2,1)} %get-tuple-element.23.hidden_in, ...), custom_call_target="tpu_custom_call" | custom-call | flops 58518929408 | bytes 41943040 | tf_op jit(solution)/shard_map/pallas_call | solution.py:989
  422.6 4.1 fusion.31
  428.3 2.2 reshape.138
  430.5 3.2 constant_dynamic-update-slice_fusion.1
  433.7 2.9 copy.67
  436.6 2.7 reshape.139
  443.0 13.1 %fusion.33 = (bf16[1024,2048]{1,0:T(8,128)(2,1)S(1)}, f32[1024,2048]{1,0:T(8,128)}) fusion(f32[1024,2048]{1,0:T(8,128)} %fusion.36, bf16[2048,1536]{1,0:T(8,128)(2,1)} %get-tuple-element.31, bf16[1024,512]{1,0:T(8,128)(2,1)S(1)} %get-tuple-element.44, bf16[1024,512]{1,0:T(8,128)(2,1)S(1)} %get-tuple-element.45, bf16[1024,512]{1,0:T(8,128)(2,1)S(1)} %get-tuple-element.43), kind=kOutput, calls=%fused_computation.105 | convolution fusion | flops 6456082432 | bytes 30408704 | tf_op jit(solution)/shard_map/dot_general | solution.py:38
  459.0 11.6 %fusion.35 = f32[1024,2048]{1,0:T(8,128)S(1)} fusion(bf16[1024,2048]{1,0:T(8,128)(2,1)S(1)} %copy-done.15, bf16[2048,2048]{1,0:T(8,128)(2,1)} %down_ref.1), kind=kOutput, calls=%fused_computation.107 | convolution fusion | flops 8589934592 | bytes 20971520 | tf_op jit(solution)/shard_map/dot_general | solution.py:42
  470.6 7.0 fusion.34
  480.6 9.2 %convolution_convert_fusion = bf16[2048,1536]{1,0:T(8,128)(2,1)} fusion(bf16[1024,2048]{1,0:T(8,128)(2,1)S(1)} %copy-done.14, bf16[1024,512]{1,0:T(8,128)(2,1)S(1)} %get-tuple-element.44, bf16[1024,512]{1,0:T(8,128)(2,1)S(1)} %get-tuple-element.45, bf16[1024,512]{1,0:T(8,128)(2,1)S(1)} %get-tuple-element.43), kind=kOutput, calls=%fused_computation.1 | convolution fusion | flops 6455033856 | bytes 13631488 | tf_op jit(solution)/shard_map/dot_general | solution.py:34
  489.8 5.1 constant_dynamic-slice_fusion.9
  496.9 2.4 dynamic-slice_bitcast_fusion.1
  500.7 6.2 convolution_convert_fusion.1
  513.6 33.2 %collective-permute-done.25 = bf16[4,64,2048]{2,1,0:T(8,128)(2,1)} collective-permute-done((bf16[4,64,2048]{2,1,0:T(8,128)(2,1)}, bf16[4,64,2048]{2,1,0:T(8,128)(2,1)}, u32[]{:S(2)}, u32[]{:S(2)}) %collective-permute-start.25) | collective-permute-done | bytes 1048608 | tf_op jit(solution)/shard_map/ppermute | solution.py:47
  548.9 2.4 collective-permute-start.29
  551.3 2.1 fusion.14
  557.3 34.6 %collective-permute-done.17 = bf16[2,2,64,2048]{3,2,0,1:T(8,128)(2,1)S(1)} collective-permute-done((bf16[2,2,64,2048]{3,2,0,1:T(8,128)(2,1)}, bf16[2,2,64,2048]{3,2,0,1:T(8,128)(2,1)S(1)}, u32[]{:S(2)}, u32[]{:S(2)}) %collective-permute-start.17) | collective-permute-done | bytes 1048608 | tf_op jit(solution)/shard_map/ppermute | solution.py:47
  592.3 5.2 collective-permute-done.29
  601.9 3.9 collective-permute-done.27
  607.8 3.2 fusion.8
  611.1 20.2 %collective-permute-done.2 = bf16[256,2048]{1,0:T(8,128)(2,1)S(1)} collective-permute-done((bf16[256,2048]{1,0:T(8,128)(2,1)S(1)}, bf16[256,2048]{1,0:T(8,128)(2,1)S(1)}, u32[]{:S(2)}, u32[]{:S(2)}) %collective-permute-start.2) | collective-permute-done | bytes 1048608 | tf_op jit(solution)/shard_map/ppermute | solution.py:47
  631.3 5.0 convert_reduce_fusion.3
  636.3 2.9 convert_add_fusion
  645.9 2.8 collective-permute-start.19
  651.2 31.1 %collective-permute-done.12 = bf16[4,2,64,1536]{3,2,0,1:T(8,128)(2,1)S(1)} collective-permute-done((bf16[4,2,64,1536]{3,2,0,1:T(8,128)(2,1)S(1)}, bf16[4,2,64,1536]{3,2,0,1:T(8,128)(2,1)S(1)}, u32[]{:S(2)}, u32[]{:S(2)}) %collective-permute-start.12) | collective-permute-done | bytes 1572896 | tf_op jit(solution)/shard_map/ppermute | solution.py:47
  684.5 2.9 collective-permute-start.10
  688.4 33.9 %collective-permute-done.24 = f32[10240]{0:T(1024)S(1)} collective-permute-done((f32[10240]{0:T(1024)S(1)}, f32[10240]{0:T(1024)S(1)}, u32[]{:S(2)}, u32[]{:S(2)}) %collective-permute-start.24) | collective-permute-done | bytes 40992 | tf_op jit(solution)/shard_map/ppermute | solution.py:47
  726.4 4.5 collective-permute-done.16
  731.0 4.4 collective-permute-done.15
  737.5 2.2 reshape.149
  (149 shorter events, 52.9 us)
Async XLA Ops:
  443.0 36.2 %copy-start.4 = (bf16[1024,512]{1,0:T(8,128)(2,1)}, bf16[1024,512]{1,0:T(8,128)(2,1)S(1)}, u32[]{:S(2)}) copy-start(bf16[1024,512]{1,0:T(8,128)(2,1)S(1)} %get-tuple-element.45) | copy-start | bytes 3145732
  457.7 91.2 %collective-permute-start.4 = (bf16[256,2048]{1,0:T(8,128)(2,1)}, bf16[256,2048]{1,0:T(8,128)(2,1)}, u32[]{:S(2)}, u32[]{:S(2)}) collective-permute-start(bf16[256,2048]{1,0:T(8,128)(2,1)} %get-tuple-element.42), channel_id=1, source_target_pairs={{0,1},{1,0},{2,3},{3,2},{4,5},{5,4},{6,7},{7,6},{8,9},{9,8},{10,11... | collective-permute-start | bytes 3145736 | tf_op jit(solution)/shard_map/ppermute | solution.py:47
  457.7 149.4 %collective-permute-start.3 = (bf16[256,2048]{1,0:T(8,128)(2,1)}, bf16[256,2048]{1,0:T(8,128)(2,1)}, u32[]{:S(2)}, u32[]{:S(2)}) collective-permute-start(bf16[256,2048]{1,0:T(8,128)(2,1)} %get-tuple-element.41), channel_id=1, source_target_pairs={{0,1},{1,0},{2,3},{3,2},{4,5},{5,4},{6,7},{7,6},{8,9},{9,8},{10,11... | collective-permute-start | bytes 3145736 | tf_op jit(solution)/shard_map/ppermute | solution.py:47
  479.2 74.2 %collective-permute-start.1 = (bf16[256,2048]{1,0:T(8,128)(2,1)}, bf16[256,2048]{1,0:T(8,128)(2,1)}, u32[]{:S(2)}, u32[]{:S(2)}) collective-permute-start(bf16[256,2048]{1,0:T(8,128)(2,1)} %get-tuple-element.47), channel_id=1, source_target_pairs={{0,1},{1,0},{2,3},{3,2},{4,5},{5,4},{6,7},{7,6},{8,9},{9,8},{10,11... | collective-permute-start | bytes 3145736 | tf_op jit(solution)/shard_map/ppermute | solution.py:47
  496.8 139.5 %collective-permute-start.11 = (bf16[4,2,2,64,1536]{4,3,0,1,2:T(8,128)(2,1)}, bf16[4,2,2,64,1536]{4,3,0,1,2:T(8,128)(2,1)}, u32[]{:S(2)}, u32[]{:S(2)}) collective-permute-start(bf16[4,2,2,64,1536]{4,3,0,1,2:T(8,128)(2,1)} %bitcast.121), channel_id=1, source_target_pairs={{0,4},{4,0},{8,12},{12,8},{16,20},{20,16},{24,28},{28,24},{1,5},{5... | collective-permute-start | bytes 9437192 | tf_op jit(solution)/shard_map/ppermute | solution.py:47
  499.3 47.5 %collective-permute-start.25 = (bf16[4,64,2048]{2,1,0:T(8,128)(2,1)}, bf16[4,64,2048]{2,1,0:T(8,128)(2,1)}, u32[]{:S(2)}, u32[]{:S(2)}) collective-permute-start(bf16[4,64,2048]{2,1,0:T(8,128)(2,1)} %dynamic-slice_bitcast_fusion.1), channel_id=1, source_target_pairs={{0,16},{4,20},{8,24},{12,28},{16,0},{20,4},{24,8},{28,12},{1,17},{... | collective-permute-start | bytes 3145736 | tf_op jit(solution)/shard_map/ppermute | solution.py:47
  546.8 45.1 %collective-permute-start.17 = (bf16[2,2,64,2048]{3,2,0,1:T(8,128)(2,1)}, bf16[2,2,64,2048]{3,2,0,1:T(8,128)(2,1)S(1)}, u32[]{:S(2)}, u32[]{:S(2)}) collective-permute-start(bf16[2,2,64,2048]{3,2,0,1:T(8,128)(2,1)} %bitcast.133), channel_id=1, source_target_pairs={{0,8},{4,12},{8,0},{12,4},{16,24},{20,28},{24,16},{28,20},{1,9},{5... | collective-permute-start | bytes 3145736 | tf_op jit(solution)/shard_map/ppermute | solution.py:47
  548.9 48.6 %collective-permute-start.29 = (bf16[256,2048]{1,0:T(8,128)(2,1)S(1)}, bf16[256,2048]{1,0:T(8,128)(2,1)S(1)}, u32[]{:S(2)}, u32[]{:S(2)}) collective-permute-start(bf16[256,2048]{1,0:T(8,128)(2,1)S(1)} %dynamic-slice_bitcast_fusion), channel_id=1, source_target_pairs={{0,16},{4,20},{8,24},{12,28},{16,0},{20,4},{24,8},{28,12},{1,17},{... | collective-permute-start | bytes 3145736 | tf_op jit(solution)/shard_map/ppermute | solution.py:47
  553.4 54.3 %collective-permute-start.5 = (bf16[256,2048]{1,0:T(8,128)(2,1)S(1)}, bf16[256,2048]{1,0:T(8,128)(2,1)S(1)}, u32[]{:S(2)}, u32[]{:S(2)}) collective-permute-start(bf16[256,2048]{1,0:T(8,128)(2,1)S(1)} %fusion.14), channel_id=1, source_target_pairs={{0,2},{1,3},{2,0},{3,1},{4,6},{5,7},{6,4},{7,5},{8,10},{9,11},{10,... | collective-permute-start | bytes 3145736 | tf_op jit(solution)/shard_map/ppermute | solution.py:47
  557.3 42.8 %copy-start.7 = (bf16[2,256,2048]{2,1,0:T(8,128)(2,1)S(1)}, bf16[2,256,2048]{2,1,0:T(8,128)(2,1)}, u32[]{:S(2)}) copy-start(bf16[2,256,2048]{2,1,0:T(8,128)(2,1)} %get-tuple-element.33) | copy-start | bytes 6291460
  591.9 8.2 %collective-permute-start.28 = (bf16[64,2048]{1,0:T(8,128)(2,1)S(1)}, bf16[64,2048]{1,0:T(8,128)(2,1)S(1)}, u32[]{:S(2)}, u32[]{:S(2)}) collective-permute-start(bf16[64,2048]{1,0:T(8,128)(2,1)S(1)} %get-tuple-element.57), channel_id=1, source_target_pairs={{0,3},{1,2},{2,1},{3,0},{4,7},{5,6},{6,5},{7,4},{8,11},{9,10},{10,... | collective-permute-start | bytes 786440 | tf_op jit(solution)/shard_map/ppermute | solution.py:47
  597.4 8.3 %collective-permute-start.27 = (bf16[64,2048]{1,0:T(8,128)(2,1)S(1)}, bf16[64,2048]{1,0:T(8,128)(2,1)S(1)}, u32[]{:S(2)}, u32[]{:S(2)}) collective-permute-start(bf16[64,2048]{1,0:T(8,128)(2,1)S(1)} %get-tuple-element.58), channel_id=1, source_target_pairs={{0,2},{1,3},{2,0},{3,1},{4,6},{5,7},{6,4},{7,5},{8,10},{9,11},{10,... | collective-permute-start | bytes 786440 | tf_op jit(solution)/shard_map/ppermute | solution.py:47
  600.1 5.6 collective-permute-start.26
  605.7 5.4 collective-permute-start
  605.7 25.6 %collective-permute-start.2 = (bf16[256,2048]{1,0:T(8,128)(2,1)S(1)}, bf16[256,2048]{1,0:T(8,128)(2,1)S(1)}, u32[]{:S(2)}, u32[]{:S(2)}) collective-permute-start(bf16[256,2048]{1,0:T(8,128)(2,1)S(1)} %fusion.16), channel_id=1, source_target_pairs={{0,2},{1,3},{2,0},{3,1},{4,6},{5,7},{6,4},{7,5},{8,10},{9,11},{10,... | collective-permute-start | bytes 3145736 | tf_op jit(solution)/shard_map/ppermute | solution.py:47
  607.1 34.6 %collective-permute-start.18 = (bf16[2,64,2048]{2,1,0:T(8,128)(2,1)S(1)}, bf16[2,64,2048]{2,1,0:T(8,128)(2,1)S(1)}, u32[]{:S(2)}, u32[]{:S(2)}) collective-permute-start(bf16[2,64,2048]{2,1,0:T(8,128)(2,1)S(1)} %fusion.24), channel_id=1, source_target_pairs={{0,4},{4,0},{8,12},{12,8},{16,20},{20,16},{24,28},{28,24},{1,5},{5... | collective-permute-start | bytes 1572872 | tf_op jit(solution)/shard_map/ppermute | solution.py:47
  611.0 28.5 %collective-permute-start.6 = (f32[10240]{0:T(1024)S(1)}, f32[10240]{0:T(1024)S(1)}, u32[]{:S(2)}, u32[]{:S(2)}) collective-permute-start(f32[10240]{0:T(1024)S(1)} %pad_maximum_fusion.3), channel_id=1, source_target_pairs={{0,1},{1,0},{2,3},{3,2},{4,5},{5,4},{6,7},{7,6},{8,9},{9,8},{10,11... | collective-permute-start | bytes 122888 | tf_op jit(solution)/shard_map/ppermute | solution.py:47
  636.3 4.3 collective-permute-start.20
  639.4 42.9 %collective-permute-start.12 = (bf16[4,2,64,1536]{3,2,0,1:T(8,128)(2,1)S(1)}, bf16[4,2,64,1536]{3,2,0,1:T(8,128)(2,1)S(1)}, u32[]{:S(2)}, u32[]{:S(2)}) collective-permute-start(bf16[4,2,64,1536]{3,2,0,1:T(8,128)(2,1)S(1)} %fusion.19), channel_id=1, source_target_pairs={{0,8},{4,12},{8,0},{12,4},{16,24},{20,28},{24,16},{28,20},{1,9},{5... | collective-permute-start | bytes 4718600 | tf_op jit(solution)/shard_map/ppermute | solution.py:47
  639.5 4.2 collective-permute-start.7
  640.6 4.8 collective-permute-start.21
  643.7 5.0 collective-permute-start.8
  645.4 4.7 collective-permute-start.22
  645.9 41.7 %collective-permute-start.19 = (bf16[64,2048]{1,0:T(8,128)(2,1)S(1)}, bf16[64,2048]{1,0:T(8,128)(2,1)S(1)}, u32[]{:S(2)}, u32[]{:S(2)}) collective-permute-start(bf16[64,2048]{1,0:T(8,128)(2,1)S(1)} %fusion.25), channel_id=1, source_target_pairs={{0,16},{4,20},{8,24},{12,28},{16,0},{20,4},{24,8},{28,12},{1,17},{... | collective-permute-start | bytes 786440 | tf_op jit(solution)/shard_map/ppermute | solution.py:47
  648.7 35.8 %collective-permute-start.9 = (f32[10240]{0:T(1024)S(1)}, f32[10240]{0:T(1024)S(1)}, u32[]{:S(2)}, u32[]{:S(2)}) collective-permute-start(f32[10240]{0:T(1024)S(1)} %add.208), channel_id=1, source_target_pairs={{0,8},{4,12},{8,0},{12,4},{16,24},{20,28},{24,16},{28,20},{1,9},{5... | collective-permute-start | bytes 122888 | tf_op jit(solution)/shard_map/ppermute | solution.py:47
  650.0 37.4 %collective-permute-start.23 = (f32[10240]{0:T(1024)S(1)}, f32[10240]{0:T(1024)S(1)}, u32[]{:S(2)}, u32[]{:S(2)}) collective-permute-start(f32[10240]{0:T(1024)S(1)} %add.228), channel_id=1, source_target_pairs={{0,8},{4,12},{8,0},{12,4},{16,24},{20,28},{24,16},{28,20},{1,9},{5... | collective-permute-start | bytes 122888 | tf_op jit(solution)/shard_map/ppermute | solution.py:47
  682.9 40.7 %collective-permute-start.13 = (bf16[4,64,1536]{2,1,0:T(8,128)(2,1)S(1)}, bf16[4,64,1536]{2,1,0:T(8,128)(2,1)S(1)}, u32[]{:S(2)}, u32[]{:S(2)}) collective-permute-start(bf16[4,64,1536]{2,1,0:T(8,128)(2,1)S(1)} %fusion.23), channel_id=1, source_target_pairs={{0,16},{4,20},{8,24},{12,28},{16,0},{20,4},{24,8},{28,12},{1,17},{... | collective-permute-start | bytes 2359304 | tf_op jit(solution)/shard_map/ppermute | solution.py:47
  684.5 38.5 %collective-permute-start.10 = (f32[10240]{0:T(1024)S(1)}, f32[10240]{0:T(1024)S(1)}, u32[]{:S(2)}, u32[]{:S(2)}) collective-permute-start(f32[10240]{0:T(1024)S(1)} %add.209), channel_id=1, source_target_pairs={{0,16},{4,20},{8,24},{12,28},{16,0},{20,4},{24,8},{28,12},{1,17},{... | collective-permute-start | bytes 122888 | tf_op jit(solution)/shard_map/ppermute | solution.py:47
  687.4 34.9 %collective-permute-start.24 = (f32[10240]{0:T(1024)S(1)}, f32[10240]{0:T(1024)S(1)}, u32[]{:S(2)}, u32[]{:S(2)}) collective-permute-start(f32[10240]{0:T(1024)S(1)} %add.229), channel_id=1, source_target_pairs={{0,16},{4,20},{8,24},{12,28},{16,0},{20,4},{24,8},{28,12},{1,17},{... | collective-permute-start | bytes 122888 | tf_op jit(solution)/shard_map/ppermute | solution.py:47
  723.9 7.1 collective-permute-start.16
  724.6 10.8 %collective-permute-start.15 = (bf16[64,1536]{1,0:T(8,128)(2,1)S(1)}, bf16[64,1536]{1,0:T(8,128)(2,1)S(1)}, u32[]{:S(2)}, u32[]{:S(2)}) collective-permute-start(bf16[64,1536]{1,0:T(8,128)(2,1)S(1)} %get-tuple-element.69), channel_id=1, source_target_pairs={{0,2},{1,3},{2,0},{3,1},{4,6},{5,7},{6,4},{7,5},{8,10},{9,11},{10,... | collective-permute-start | bytes 589832 | tf_op jit(solution)/shard_map/ppermute | solution.py:47
  725.6 9.8 %collective-permute-start.14 = (bf16[64,1536]{1,0:T(8,128)(2,1)S(1)}, bf16[64,1536]{1,0:T(8,128)(2,1)S(1)}, u32[]{:S(2)}, u32[]{:S(2)}) collective-permute-start(bf16[64,1536]{1,0:T(8,128)(2,1)S(1)} %get-tuple-element.70), channel_id=1, source_target_pairs={{0,1},{1,0},{2,3},{3,2},{4,5},{5,4},{6,7},{7,6},{8,9},{9,8},{10,11... | collective-permute-start | bytes 589832 | tf_op jit(solution)/shard_map/ppermute | solution.py:47
  (14 other events, 147.8 us)

commit v4 on v3

--- a/solution.py
+++ b/solution.py
@@ -1026,6 +1026,557 @@
     )(qkv_in, do_in, hidden, normed, grads, du, cosine, sine)
 
 
+FLIGHTS = 64
+
+
+def finish_kernel(
+    items,
+    pairs,
+    slot_groups,
+    back_in,
+    normed_in,
+    grads_in,
+    hidden_in,
+    du_in,
+    wqkv_in,
+    wup_in,
+    outw_in,
+    down_in,
+    d_in,
+    u_in,
+    x_in,
+    cot_in,
+    gain_ref,
+    out_bias_ref,
+    down_bias_ref,
+    result_out,
+    input_out,
+    qkv_out,
+    up_out,
+    o_out,
+    d_out,
+    sums_out,
+    big,
+    q_send,
+    q_keep,
+    q_recv,
+    q_two,
+    q_three,
+    q_done,
+    o_send,
+    o_keep,
+    o_recv,
+    o_two,
+    o_three,
+    d_three,
+    u_three,
+    u_done,
+    p_send,
+    p_recv,
+    p_own,
+    n_send,
+    n_recv,
+    n_own,
+    sums,
+    s_recv,
+    s_part,
+    s_all,
+    local_sem,
+    store_sem,
+    sends,
+    recvs,
+):
+    place = lax.axis_index("ctx")
+    member = lax.axis_index("fsdp")
+    shards = back_in.shape[1]
+    groups, tops, _, piece, qcols = q_send.shape
+    rows, width = p_own.shape
+    wide = width // groups
+    deep = hidden_in.shape[1]
+    x_at, z_at, top_at = place % 2, (place // 2) % 2, place // 4
+    near, over, far = {"ctx": place ^ 1}, {"ctx": place ^ 2}, {"ctx": place ^ 4}
+
+    barrier = pltpu.get_barrier_semaphore()
+    for j in range(1, groups):
+        pl.semaphore_signal(
+            barrier, inc=1, device_id={"fsdp": member ^ j}, device_id_type=pl.DeviceIdType.MESH
+        )
+    for k in range(1, shards):
+        pl.semaphore_signal(
+            barrier, inc=1, device_id={"ctx": place ^ k}, device_id_type=pl.DeviceIdType.MESH
+        )
+
+    def block(at, size):
+        return pl.ds(pl.multiple_of(at, size), size)
+
+    names = {}
+
+    def flight(name, src, dst, target):
+        at = names.setdefault(name, len(names))
+        return remote(src, dst, sends, recvs, at, target)
+
+    def fetch(src, dst, at):
+        copy = pltpu.make_async_copy(src, dst, local_sem.at[at])
+        copy.start()
+        return copy
+
+    def core(j):
+        return {"fsdp": member ^ j}
+
+    def d_last():
+        return flight("d", d_in.at[1 - top_at], d_three, far)
+
+    def u_last():
+        return flight("u", u_in.at[:, 1 - top_at], u_three, far)
+
+    def o_first(top):
+        return flight(("o1", top), o_send.at[top], o_recv.at[top], over)
+
+    def o_second():
+        return flight("o2", o_send.at[:, pl.ds(0, piece)], o_two, near)
+
+    def o_last():
+        return flight("o3", o_send.at[0, pl.ds(piece, piece)], o_three, far)
+
+    def q_first(f):
+        return flight(("q1", f), q_send.at[f], q_recv.at[f], near)
+
+    def q_second(f):
+        return flight(("q2", f), q_send.at[f, :, 0], q_two.at[f], over)
+
+    def q_last(f):
+        return flight(("q3", f), q_send.at[f, 0, 1], q_three.at[f], far)
+
+    def q_swap(j):
+        return flight(("q4", j), q_done.at[member ^ j], qkv_out.at[member], core(j))
+
+    def u_swap(j):
+        return flight(("u4", j), u_done.at[member ^ j], up_out.at[member], core(j))
+
+    def rows_last(name, send, recv):
+        return flight((name, 3), send.at[0], recv.at[0], core(1))
+
+    def rows_far(name, send, recv):
+        return flight((name, 2), send.at[1], recv.at[1], core(2))
+
+    def rows_near(name, send, recv):
+        return flight((name, 1), send.at[2], recv.at[2], core(1))
+
+    def sums_one(j):
+        return flight(("s1", j), sums, s_recv.at[j - 1], core(j))
+
+    span = width // shards
+
+    def sums_two(k):
+        return flight(
+            ("s2", k), s_all.at[:, block((place ^ k) * span, span)], s_part.at[k], {"ctx": place ^ k}
+        )
+
+    def sums_three(k):
+        mine = block(place * span, span)
+        return flight(("s3", k), sums_out.at[:, mine], sums_out.at[:, mine], {"ctx": place ^ k})
+
+    pl.semaphore_wait(barrier, groups - 1 + shards - 1)
+    d_last().start()
+    u_last().start()
+
+    def phase_a(normed, grads):
+        loads = [fetch(normed_in, normed, 0), fetch(grads_in, grads, 1)]
+        for item in range(items):
+            for owner in range(shards):
+                pair, g = owner // slot_groups, owner % slot_groups
+                spot = pl.ds((item * slot_groups + g) * rows, rows)
+                for kind in range(4):
+                    loads.append(
+                        fetch(
+                            back_in.at[item, owner, kind],
+                            big.at[spot, pl.ds(kind * wide + pair * LANES, LANES)],
+                            2 + (item * shards + owner) * 4 + kind,
+                        )
+                    )
+        sums[...] = jnp.zeros_like(sums)
+        for load in loads:
+            load.wait()
+
+        def out_grad(top, low, into):
+            at = (top * 2 + low) * LANES
+            into[top] = contract_rows(big[:, block(at, LANES)], grads[...]).astype(BF16)
+
+        for top in range(tops):
+            out_grad(top, 1 - z_at, o_send)
+            o_first(top).start()
+
+        for f in range(groups):
+
+            def one(at, _, f=f):
+                top, low = at // 2, at % 2
+                value = contract_rows(
+                    normed[:, block(f * wide + at * LANES, LANES)], big[:, wide:]
+                )
+                first, second = value[:piece], value[piece:]
+                q_send[f, top, low] = jnp.where(x_at == 0, second, first).astype(BF16)
+                q_keep[f, top, low] = jnp.where(x_at == 0, first, second).astype(BF16)
+                return 0
+
+            lax.fori_loop(0, 2 * tops, one, 0)
+            q_first(f).start()
+        for top in range(tops):
+            out_grad(top, z_at, o_keep)
+        for kind in range(3):
+            cols = big[:, (kind + 1) * wide : (kind + 2) * wide].astype(F32)
+            sums[2 + kind : 3 + kind, block(member * wide, wide)] = jnp.sum(
+                cols, axis=0, keepdims=True
+            )
+
+    total = rows * groups
+    pl.run_scoped(
+        phase_a, pltpu.VMEM((total, width), BF16), pltpu.VMEM((total, width), BF16)
+    )
+
+    tile = 256
+
+    def keep_share(pair, at, value, send, own):
+        cols = block(at * tile, tile)
+        if pair == 1:
+            send[1, :, cols] = value[:rows].astype(BF16)
+            send[0, :, cols] = value[rows:].astype(BF16)
+        else:
+            own[:, cols] = value[:rows]
+            send[2, :, cols] = value[rows:].astype(BF16)
+
+    def phase_b(hidden, down, outw):
+        loads = [
+            fetch(hidden_in, hidden, 0),
+            fetch(down_in, down, 1),
+            fetch(outw_in, outw, 2),
+        ]
+        for load in loads:
+            load.wait()
+        for pair in (1, 0):
+            spot = pl.ds(pair * 2 * rows, 2 * rows)
+
+            def one(at, _, pair=pair, spot=spot):
+                cols = block(at * tile, tile)
+                value = matmul(hidden[spot, :], down[:, cols]) + matmul(
+                    big[spot, pl.ds(0, wide)], outw[:, cols]
+                )
+                keep_share(pair, at, value, p_send, p_own)
+                return 0
+
+            lax.fori_loop(0, width // tile, one, 0)
+            if pair == 1:
+                rows_last("p", p_send, p_recv).start()
+            else:
+                rows_near("p", p_send, p_recv).start()
+
+    pl.run_scoped(
+        phase_b,
+        pltpu.VMEM(hidden_in.shape, BF16),
+        pltpu.VMEM(down_in.shape, BF16),
+        pltpu.VMEM(outw_in.shape, BF16),
+    )
+
+    def pass_rows(name, send, recv):
+        rows_last(name, send, recv).wait_recv()
+        send[1] = (send[1].astype(F32) + recv[0].astype(F32)).astype(BF16)
+        rows_far(name, send, recv).start()
+
+    pass_rows("p", p_send, p_recv)
+
+    theirs = block((1 - x_at) * piece, piece)
+    mine = block(x_at * piece, piece)
+    for top in range(tops):
+        o_first(top).wait()
+    for top in range(tops):
+        o_send[top, pl.ds(0, piece)] = (
+            o_keep[top, theirs].astype(F32) + o_recv[top, theirs].astype(F32)
+        ).astype(BF16)
+    o_second().start()
+
+    def q_pass(f):
+        q_first(f).wait()
+        for top in range(tops):
+            q_send[f, top, 0] = (
+                q_keep[f, top, 1 - z_at].astype(F32) + q_recv[f, top, 1 - z_at].astype(F32)
+            ).astype(BF16)
+        q_second(f).start()
+
+    def q_turn(f):
+        q_second(f).wait_recv()
+        other = 1 - top_at
+        q_send[f, 0, 1] = (
+            q_keep[f, other, z_at].astype(F32)
+            + q_recv[f, other, z_at].astype(F32)
+            + q_two[f, other].astype(F32)
+        ).astype(BF16)
+        q_last(f).start()
+
+    for f in range(groups // 2):
+        q_pass(f)
+
+    def phase_c(du, wup, wqkv):
+        loads = [
+            fetch(du_in, du, 0),
+            fetch(wup_in, wup, 1),
+            fetch(wqkv_in, wqkv, 2),
+        ]
+        for load in loads:
+            load.wait()
+        for pair in (1, 0):
+            spot = pl.ds(pair * 2 * rows, 2 * rows)
+
+            def one(at, _, pair=pair, spot=spot):
+                cols = block(at * tile, tile)
+                value = contract_cols(du[spot, :], wup[cols, :]) + contract_cols(
+                    big[spot, pl.ds(wide, 3 * wide)], wqkv[cols, :]
+                )
+                keep_share(pair, at, value, n_send, n_own)
+                return 0
+
+            lax.fori_loop(0, width // tile, one, 0)
+            if pair == 1:
+                rows_last("n", n_send, n_recv).start()
+            else:
+                rows_near("n", n_send, n_recv).start()
+        step = deep // groups
+
+        def column_sums(at, _):
+            cols = block(at * step, step)
+            value = jnp.sum(du[:, cols].astype(F32), axis=0, keepdims=True)
+            for j in range(groups):
+                sums[5 + j : 6 + j, cols] = jnp.where(member == j, value, 0.0)
+            return 0
+
+        lax.fori_loop(0, groups, column_sums, 0)
+
+    pl.run_scoped(
+        phase_c,
+        pltpu.VMEM(du_in.shape, BF16),
+        pltpu.VMEM(wup_in.shape, BF16),
+        pltpu.VMEM(wqkv_in.shape, BF16),
+    )
+    pass_rows("n", n_send, n_recv)
+    for f in range(groups // 2, groups):
+        q_pass(f)
+    for f in range(groups // 2):
+        q_turn(f)
+    o_second().wait_recv()
+    o_send[0, pl.ds(piece, piece)] = (
+        o_keep[1 - top_at, mine].astype(F32)
+        + o_recv[1 - top_at, mine].astype(F32)
+        + o_two[1 - top_at].astype(F32)
+    ).astype(BF16)
+    o_last().start()
+
+    def phase_d(x, cot, out, d_own, d_sum, o_sum):
+        loads = [
+            fetch(x_in, x, 0),
+            fetch(cot_in, cot, 1),
+            fetch(u_in.at[:, top_at], u_done, 2),
+            fetch(d_in.at[top_at], d_own, 3),
+        ]
+        for load in loads:
+            load.wait()
+
+        u_last().wait_recv()
+        for f in range(groups):
+            u_done[f] = (u_done[f].astype(F32) + u_three[f].astype(F32)).astype(BF16)
+        for j in range(1, groups):
+            u_swap(j).start()
+        own_up = pltpu.make_async_copy(u_done.at[member], up_out.at[member], store_sem.at[0])
+        own_up.start()
+
+        for f in range(groups // 2, groups):
+            q_turn(f)
+        rows_near("n", n_send, n_recv).wait_recv()
+        rows_far("n", n_send, n_recv).wait_recv()
+        step = 64
+
+        def normal_part(at, _):
+            r = block(at * step, step)
+            tokens = x[r, :].astype(F32)
+            centred = tokens - jnp.mean(tokens, axis=-1, keepdims=True)
+            spread = lax.rsqrt(jnp.mean(centred * centred, axis=-1, keepdims=True) + EPS)
+            normal = centred * spread
+            dn = n_own[r, :] + n_recv[2, r, :].astype(F32) + n_recv[1, r, :].astype(F32)
+            sums[0:1, :] = sums[0:1, :] + jnp.sum(dn * normal, axis=0, keepdims=True)
+            sums[1:2, :] = sums[1:2, :] + jnp.sum(dn, axis=0, keepdims=True)
+            dnorm = dn * gain_ref[...]
+            grad = cot[r, :].astype(F32)
+            sums[9:10, :] = sums[9:10, :] + jnp.sum(grad, axis=0, keepdims=True)
+            change = spread * (
+                dnorm
+                - jnp.mean(dnorm, axis=-1, keepdims=True)
+                - normal * jnp.mean(dnorm * normal, axis=-1, keepdims=True)
+            )
+            cot[r, :] = (grad + change).astype(BF16)
+            return 0
+
+        lax.fori_loop(0, rows // step, normal_part, 0)
+        for j in range(1, groups):
+            sums_one(j).start()
+        own_input = pltpu.make_async_copy(cot, input_out, store_sem.at[1])
+        own_input.start()
+
+        rows_near("p", p_send, p_recv).wait_recv()
+        rows_far("p", p_send, p_recv).wait_recv()
+
+        def output_part(at, _):
+            r = block(at * step, step)
+            value = x[r, :].astype(F32) + p_own[r, :] + p_recv[2, r, :].astype(F32)
+            value = value + p_recv[1, r, :].astype(F32) + out_bias_ref[...] + down_bias_ref[...]
+            out[r, :] = value.astype(BF16)
+            return 0
+
+        lax.fori_loop(0, rows // step, output_part, 0)
+        own_out = pltpu.make_async_copy(out, result_out, store_sem.at[2])
+        own_out.start()
+
+        for j in range(1, groups):
+            sums_one(j).wait_recv()
+        s_all[...] = sums[...] + s_recv[0] + s_recv[1] + s_recv[2]
+        for k in range(1, shards):
+            sums_two(k).start()
+        d_last().wait_recv()
+        d_sum[...] = d_own[...].astype(F32) + d_three[...].astype(F32)
+        own_down = pltpu.make_async_copy(d_sum, d_out, store_sem.at[3])
+        own_down.start()
+
+        for f in range(groups):
+            q_last(f).wait_recv()
+            q_done[f] = (
+                q_keep[f, top_at, z_at].astype(F32)
+                + q_recv[f, top_at, z_at].astype(F32)
+                + q_two[f, top_at].astype(F32)
+                + q_three[f].astype(F32)
+            ).astype(BF16)
+        for j in range(1, groups):
+            q_swap(j).start()
+        own_q = pltpu.make_async_copy(q_done.at[member], qkv_out.at[member], store_sem.at[4])
+        own_q.start()
+        o_last().wait_recv()
+        o_sum[...] = (
+            o_keep[top_at, mine].astype(F32)
+            + o_recv[top_at, mine].astype(F32)
+            + o_two[top_at].astype(F32)
+            + o_three[...].astype(F32)
+        )
+        own_o = pltpu.make_async_copy(o_sum, o_out, store_sem.at[5])
+        own_o.start()
+        for k in range(1, shards):
+            sums_two(k).wait()
+        cols = block(place * span, span)
+        value = s_all[:, cols]
+        for k in range(1, shards):
+            value = value + s_part[k]
+        sums_out[:, cols] = value
+        for k in range(1, shards):
+            sums_three(k).start()
+        for copy in (own_up, own_input, own_out, own_down, own_q, own_o):
+            copy.wait()
+
+    pl.run_scoped(
+        phase_d,
+        pltpu.VMEM((rows, width), BF16),
+        pltpu.VMEM((rows, width), BF16),
+        pltpu.VMEM((rows, width), BF16),
+        pltpu.VMEM(d_in.shape[1:], BF16),
+        pltpu.VMEM(d_in.shape[1:], F32),
+        pltpu.VMEM((piece, width), F32),
+    )
+    d_last().wait_send()
+    u_last().wait_send()
+    o_second().wait_send()
+    o_last().wait_send()
+    for f in range(groups):
+        q_second(f).wait_send()
+        q_last(f).wait_send()
+    for j in range(1, groups):
+        q_swap(j).wait()
+        u_swap(j).wait()
+        sums_one(j).wait_send()
+    for name, send, recv in (("p", p_send, p_recv), ("n", n_send, n_recv)):
+        rows_last(name, send, recv).wait_send()
+        rows_far(name, send, recv).wait_send()
+        rows_near(name, send, recv).wait_send()
+    for k in range(1, shards):
+        sums_three(k).wait()
+
+
+def finish(
+    back_in, normed, grads, hidden, du, wqkv, wup, outw, down, d_sum, u_sum,
+    x, cot, gain, out_bias, down_bias, groups, slot_groups,
+):
+    items, shards = back_in.shape[:2]
+    rows, width = x.shape
+    wide = width // groups
+    deep = hidden.shape[1]
+    tops = shards // 4
+    piece = wide // shards
+    pairs = wide // LANES
+    units = deep // shards
+    apart = pl.BlockSpec(memory_space=pl.ANY)
+    whole = pl.BlockSpec(memory_space=pltpu.VMEM)
+    dma = pltpu.SemaphoreType.DMA
+    shape = jax.ShapeDtypeStruct
+    return pl.pallas_call(
+        partial(finish_kernel, items, pairs, slot_groups),
+        out_shape=[
+            shape((rows, width), BF16),
+            shape((rows, width), BF16),
+            shape((groups, piece, 3 * wide), BF16),
+            shape((groups, piece, deep), BF16),
+            shape((piece, width), F32),
+            shape((units, width), F32),
+            shape((16, width), F32),
+        ],
+        in_specs=[apart] * 13 + [whole] * 3,
+        out_specs=[apart] * 6 + [whole],
+        scratch_shapes=[
+            pltpu.VMEM((rows * groups, 4 * wide), BF16),
+            pltpu.VMEM((groups, tops, 2, piece, 3 * wide), BF16),
+            pltpu.VMEM((groups, tops, 2, piece, 3 * wide), BF16),
+            pltpu.VMEM((groups, tops, 2, piece, 3 * wide), BF16),
+            pltpu.VMEM((groups, tops, piece, 3 * wide), BF16),
+            pltpu.VMEM((groups, piece, 3 * wide), BF16),
+            pltpu.VMEM((groups, piece, 3 * wide), BF16),
+            pltpu.VMEM((tops, 2 * piece, width), BF16),
+            pltpu.VMEM((tops, 2 * piece, width), BF16),
+            pltpu.VMEM((tops, 2 * piece, width), BF16),
+            pltpu.VMEM((tops, piece, width), BF16),
+            pltpu.VMEM((piece, width), BF16),
+            pltpu.VMEM((units, width), BF16),
+            pltpu.VMEM((groups, piece, deep), BF16),
+            pltpu.VMEM((groups, piece, deep), BF16),
+            pltpu.VMEM((3, rows, width), BF16),
+            pltpu.VMEM((3, rows, width), BF16),
+            pltpu.VMEM((rows, width), F32),
+            pltpu.VMEM((3, rows, width), BF16),
+            pltpu.VMEM((3, rows, width), BF16),
+            pltpu.VMEM((rows, width), F32),
+            pltpu.VMEM((16, width), F32),
+            pltpu.VMEM((3, 16, width), F32),
+            pltpu.VMEM((shards, 16, width // shards), F32),
+            pltpu.VMEM((16, width), F32),
+            dma((2 + items * shards * 4,)),
+            dma((6,)),
+            dma((FLIGHTS,)),
+            dma((FLIGHTS,)),
+        ],
+        compiler_params=pltpu.CompilerParams(
+            collective_id=2, has_side_effects=True, vmem_limit_bytes=63 * 2**20
+        ),
+        cost_estimate=pl.CostEstimate(
+            flops=2 * rows * groups * width * (2 * deep + 8 * wide),
+            bytes_accessed=60 * 2**20,
+            transcendentals=0,
+        ),
+    )(
+        back_in, normed, grads, hidden, du, wqkv, wup, outw, down, d_sum, u_sum, x, cot,
+        gain.reshape(1, width), out_bias.reshape(1, width), down_bias.reshape(1, width),
+    )
+
+
 def scatter_sum(parts, axis_at, place, bits):
     lead, tail = parts.shape[:axis_at], parts.shape[axis_at + 1 :]
     total = len(bits)
@@ -1040,13 +1591,6 @@
         got = swap(send.astype(BF16), "ctx", 1 << bit)
         value = keep.astype(F32) + got.astype(F32)
     return value
-
-
-def last_half(value, axis_at, place):
-    mine = (place // 4) % 2
-    send = lax.dynamic_index_in_dim(value, 1 - mine, axis_at, keepdims=False)
-    keep = lax.dynamic_index_in_dim(value, mine, axis_at, keepdims=False)
-    return keep.astype(F32) + swap(send, "ctx", 4).astype(F32)
 
 
 def scatter_rows(parts):
@@ -1149,9 +1693,44 @@
             heads,
             groups,
         )
-        backs = [assembled(back_in[item]) for item in range(per_group)]
-        down_weight_grad = last_half(down_sum, 0, place)
-        up_part = last_half(up_sum, 1, place)
+        result, input_grad, qkv_parts, up_parts, out_weight_grad, down_weight_grad, sums = finish(
+            back_in.reshape(per_group, shards, 4, rows, LANES),
+            normed,
+            grads,
+            hidden,
+            grad_up,
+            qkv_own,
+            up_own,
+            out_weight,
+            down_weight,
+            down_sum,
+            up_sum,
+            inputs[0],
+            grad_low,
+            norm_gain,
+            out_bias,
+            down_bias,
+            groups,
+            slot_groups,
+        )
+        ow = wide // shards
+        return (
+            result[None],
+            input_grad[None],
+            sums[0],
+            sums[1],
+            qkv_parts.reshape(groups, ow, 3, wide)
+            .transpose(1, 2, 0, 3)
+            .reshape(ow, 3 * width)
+            .astype(F32),
+            sums[2:5].reshape(-1),
+            out_weight_grad,
+            sums[9],
+            up_parts.transpose(1, 0, 2).reshape(ow, hidden_width).astype(F32),
+            sums[5 : 5 + groups].reshape(-1),
+            down_weight_grad,
+            sums[9],
+        )
     else:
         down_grad = contract_rows(hidden, grads).astype(BF16)
         up_grad = contract_rows(normed, grad_up).astype(BF16)

time: 750 us -> 610 us (0.81)
  waiting for transfers between devices: 175 us -> 0 us
  Pallas kernels: 407 us -> 581 us
  matrix products: 61.6 us -> 0 us
  local copies, waits for them, and re-layouts: 47.8 us -> 18.8 us
  other arithmetic: 24.7 us -> 0.24 us
  starting transfers between devices: 22.9 us -> 0 us
    ppermute x30 -> x0, waiting for transfers between devices: 175 us -> none  [swap(): return lax.ppermute(value, axis, [(i, i ^ bit) for i in range(size)])]
    pallas_call x0 -> x1, Pallas kernels: none -> 174 us  [finish(): pl.pallas_call(partial(finish_kernel, items, pairs, slot_groups), out_sha...]
    dot_general x6 -> x0, matrix products: 61.6 us -> none  [the longest x2 27.6 us: contract_cols(): lax.dot_general(left, right, (((1,), (1,)), ((), ())), preferred_element_...]
    ppermute x30 -> x0, starting transfers between devices: 22.9 us -> none  [swap(): return lax.ppermute(value, axis, [(i, i ^ bit) for i in range(size)])]
    dynamic_slice x7 -> x0, local copies, waits for them, and re-layouts: 10.1 us -> none  [the longest x2 6.9 us: scatter_sum(): keep = lax.dynamic_index_in_dim(value, mine, at, keepdims=False)]
    reduce_sum x6 -> x0, other arithmetic: 10 us -> none  [the longest x1 4.96 us: on_device(): jnp.sum(grad_full, axis=0)]
    convert_element_type x6 -> x0, other arithmetic: 8.03 us -> none  [the longest x2 4.28 us: scatter_rows(): far = swap((parts[2] + last).astype(BF16), 'fsdp', 2).astype(F32)]
    another operation x4 -> x0, local copies, waits for them, and re-layouts: 7.7 us -> none  [the longest x2 4.57 us: assembled(): back = jnp.sum(back, axis=2) if dup > 1 else back[:, :, 0]]
  transfers between devices with their start and end apart: 30 -> 0, of which waited for: 11 -> 0; matrix products, arithmetic and copies ran while one was open for 10% -> 0% of each run, Pallas kernels for 0% -> 0%
where the time goes in v4:
time: 610 us; the launch traced here: 601 us
  Pallas kernels  581 us (95%)
  local copies, waits for them, and re-layouts  18.8 us (3%)
    pallas_call x1, Pallas kernels, middle(): pl.pallas_call(partial(middle_kernel, items, heads), out_shape=[shape((it...  217 us
    pallas_call x1, Pallas kernels, begin_layer(): pl.pallas_call(partial(start_kernel, shards, groups, pairs, slot_groups,...  191 us
    pallas_call x1, Pallas kernels, finish(): pl.pallas_call(partial(finish_kernel, items, pairs, slot_groups), out_sha...  174 us

profile of v4, /device:TPU:0, one launch (start us, length us, event | category | flops | bytes accessed | tf_op | source)
XLA Modules:
  0.0 601.0 jit_solution(15403776225779832551)
XLA Ops:
  0.6 190.5 %shard_map.229 = (bf16[1024,2048]{1,0:T(8,128)(2,1)}, bf16[1024,2048]{1,0:T(8,128)(2,1)}, bf16[2048,1536]{1,0:T(8,128)(2,1)}, bf16[2048,2048]{1,0:T(8,128)(2,1)}...) custom-call(bf16[256,2048]{1,0:T(8,128)(2,1)} %bitcast.33, ...), custom_call_target="tpu_custom_call" | custom-call | flops 25769803776 | bytes 62914560 | tf_op jit(solution)/shard_map/pallas_call | solution.py:441
  191.2 216.6 %shard_map.230 = (bf16[2,8,4,2,128,128]{5,4,3,2,1,0:T(8,128)(2,1)}, bf16[2,256,2048]{2,1,0:T(8,128)(2,1)}, bf16[4,2,64,2048]{3,2,1,0:T(8,128)(2,1)}) custom-call(bf16[2,8,3,2,128,128]{5,4,3,2,1,0:T(8,128)(2,1)} %bitcast.45, bf16[8,2,2,128,128]{4,3,2,1,0:T(8,128)(2,1)} %bitcast.46, bf16[1024,2048]{1,0:T(8,128)(2,1)} %get-tuple-element.32.hidden_in, ...), custom_call_target="tpu_custom_call" | custom-call | flops 58518929408 | bytes 41943040 | tf_op jit(solution)/shard_map/pallas_call | solution.py:989
  407.9 173.6 %shard_map.231 = (bf16[256,2048]{1,0:T(8,128)(2,1)}, bf16[256,2048]{1,0:T(8,128)(2,1)}, bf16[4,64,1536]{2,1,0:T(8,128)(2,1)}, bf16[4,64,2048]{2,1,0:T(8,128)(2,1...) custom-call(bf16[2,8,4,256,128]{4,3,2,1,0:T(8,128)(2,1)} %bitcast.44, ...), custom_call_target="tpu_custom_call" | custom-call | flops 34359738368 | bytes 62914560 | tf_op jit(solution)/shard_map/pallas_call | solution.py:1522
  581.5 1.5 fusion
  583.0 0.0 copy-start.5
  583.0 0.9 slice.18
  583.9 0.9 slice_bitcast_fusion
  584.8 0.6 reshape.76
  585.4 0.6 copy.31
  586.1 2.7 reshape.80
  588.8 0.0 copy-start.1
  588.8 2.2 copy.28
  591.0 3.2 reshape.78
  594.2 0.0 copy-done.1
  594.2 0.0 copy-start.3
  594.2 0.2 convert_bitcast_fusion
  594.4 0.0 copy-start.2
  594.5 1.5 copy.30
  595.9 0.0 copy-start.4
  595.9 0.0 copy-start
  595.9 0.0 copy-done.5
  595.9 0.6 copy.37
  596.5 0.0 copy-done.3
  596.5 1.0 copy.38
  597.5 0.0 copy-done.2
  597.5 1.0 copy.39
  598.5 0.0 copy-done.4
  598.5 0.8 copy.40
  599.3 0.0 copy-done
  599.3 1.3 copy.41
Async XLA Ops:
  583.0 12.9 %copy-start.5 = (f32[1,2048]{1,0:T(1,128)}, f32[1,2048]{1,0:T(1,128)S(1)}, u32[]{:S(2)}) copy-start(f32[1,2048]{1,0:T(1,128)S(1)} %get-tuple-element.48) | copy-start | bytes 24580
  588.8 5.4 copy-start.1
  594.2 2.3 copy-start.3
  594.4 3.1 copy-start.2
  595.9 2.6 copy-start.4
  595.9 3.3 copy-start

commit v5 on v4

--- a/solution.py
+++ b/solution.py
@@ -216,11 +216,6 @@
     centred = tokens - jnp.mean(tokens, axis=-1, keepdims=True)
     spread = lax.rsqrt(jnp.mean(centred * centred, axis=-1, keepdims=True) + EPS)
     normed[0:rows, :] = (centred * spread * gain_ref[...] + shift_ref[...]).astype(BF16)
-    n_far = begin(
-        remote(
-            normed.at[pl.ds(0, rows)], normed.at[pl.ds(2 * rows, rows)], rs, rr, 0, {"fsdp": member ^ 2}
-        )
-    )
     n_near = begin(
         remote(normed.at[pl.ds(0, rows)], normed.at[pl.ds(rows, rows)], rs, rr, 1, {"fsdp": member ^ 1})
     )
@@ -246,51 +241,11 @@
             q_side.append(
                 begin(remote(spot, spot, qs, qr, 9 + (j - 2) * 3 + p, {"ctx": place ^ 1}))
             )
-    n_far.wait_recv()
-    n_last = begin(
+    n_far = begin(
         remote(
-            normed.at[pl.ds(2 * rows, rows)],
-            normed.at[pl.ds(3 * rows, rows)],
-            rs,
-            rr,
-            2,
-            {"fsdp": member ^ 1},
-        )
-    )
-
-    loads[4].wait()
-    g_far = begin(
-        remote(
-            grads.at[pl.ds(0, rows)], grads.at[pl.ds(2 * rows, rows)], rs, rr, 3, {"fsdp": member ^ 2}
-        )
-    )
-    g_near = begin(
-        remote(grads.at[pl.ds(0, rows)], grads.at[pl.ds(rows, rows)], rs, rr, 4, {"fsdp": member ^ 1})
-    )
-    u_far = [
-        begin(
-            remote(
-                up_ref.at[block(side * part, part), block((member ^ j) * deep, deep)],
-                wup.at[half_rows, :],
-                us,
-                ur,
-                j - 2,
-                {"fsdp": member ^ j},
-            )
-        )
-        for j in (2, 3)
-    ]
-    u_near = begin(
-        remote(
-            up_ref.at[:, block((member ^ 1) * deep, deep)],
-            wup.at[own_rows, :],
-            us,
-            ur,
-            2,
-            {"fsdp": member ^ 1},
-        )
-    )
-
+            normed.at[pl.ds(0, rows)], normed.at[pl.ds(2 * rows, rows)], rs, rr, 0, {"fsdp": member ^ 2}
+        )
+    )
     for at in (0, 1, 2, 7, 8, 9, 10):
         loads[at].wait()
     for copy in q_near + q_side:
@@ -309,6 +264,48 @@
 
     for item in range(items):
         if item == items - 1:
+            n_far.wait_recv()
+            n_last = begin(
+                remote(
+                    normed.at[pl.ds(2 * rows, rows)],
+                    normed.at[pl.ds(3 * rows, rows)],
+                    rs,
+                    rr,
+                    2,
+                    {"fsdp": member ^ 1},
+                )
+            )
+            loads[4].wait()
+            g_far = begin(
+                remote(
+                    grads.at[pl.ds(0, rows)],
+                    grads.at[pl.ds(2 * rows, rows)],
+                    rs,
+                    rr,
+                    3,
+                    {"fsdp": member ^ 2},
+                )
+            )
+            g_near = begin(
+                remote(
+                    grads.at[pl.ds(0, rows)],
+                    grads.at[pl.ds(rows, rows)],
+                    rs,
+                    rr,
+                    4,
+                    {"fsdp": member ^ 1},
+                )
+            )
+            u_near = begin(
+                remote(
+                    up_ref.at[:, block((member ^ 1) * deep, deep)],
+                    wup.at[own_rows, :],
+                    us,
+                    ur,
+                    0,
+                    {"fsdp": member ^ 1},
+                )
+            )
             n_last.wait_recv()
 
         def project(p, _, item=item):
@@ -354,6 +351,21 @@
             {"fsdp": member ^ 1},
         )
     )
+    tile = 512
+    tiles = deep // tile
+    u_far = {}
+    for c in range(tiles):
+        for j in (2, 3):
+            u_far[c, j] = begin(
+                remote(
+                    up_ref.at[block(side * part, part), block((member ^ j) * deep + c * tile, tile)],
+                    wup.at[half_rows, pl.ds(c * tile, tile)],
+                    us,
+                    ur,
+                    1 + c * 2 + j - 2,
+                    {"fsdp": member ^ j},
+                )
+            )
     g_near.wait_recv()
     loads[5].wait()
     g_last.wait_recv()
@@ -382,39 +394,47 @@
     keep(grads, grads_out)
     keep(wqkv, wqkv_out)
 
-    u_side = []
-    for j in (2, 3):
-        u_far[j - 2].wait_recv()
-        spot = wup.at[block((member ^ j) * wide + side * part, part), :]
-        u_side.append(begin(remote(spot, spot, us, ur, 3 + j - 2, {"ctx": place ^ 1})))
-
     loads[6].wait()
-    tile = 512
     high = 2 * rows
 
-    def spot_of(at):
-        return block((at % 2) * high, high), block((at // 2) * tile, tile)
-
     def back(at, _):
-        r, c = spot_of(at)
+        r, c = block((at % 2) * high, high), block((at // 2) * tile, tile)
         dh[r, c] = contract_cols(grads[r, :], down[c, :])
         return 0
 
-    lax.fori_loop(0, 2 * (deep // tile), back, 0)
+    def forward(c):
+        cols = pl.ds(c * tile, tile)
+
+        def one(at, _):
+            r = block(at * high, high)
+            value = matmul(normed[r, :], wup[:, cols]) + up_bias_ref[member, :, cols]
+            hidden[r, cols] = gelu_value(value).astype(BF16)
+            du[r, cols] = (dh[r, cols] * gelu_slope(value)).astype(BF16)
+            return 0
+
+        lax.fori_loop(0, 2, one, 0)
+
+    lax.fori_loop(0, 2 * tiles, back, 0)
     loads[3].wait()
     u_near.wait_recv()
-    for copy in u_side:
-        copy.wait_recv()
+    u_side = []
+    for c in range(tiles + 1):
+        if c < tiles:
+            for j in (2, 3):
+                u_far[c, j].wait_recv()
+                spot = wup.at[
+                    block((member ^ j) * wide + side * part, part), pl.ds(c * tile, tile)
+                ]
+                u_side.append(
+                    begin(
+                        remote(spot, spot, us, ur, 1 + 2 * (tiles + c) + j - 2, {"ctx": place ^ 1})
+                    )
+                )
+        if c > 0:
+            u_side[2 * c - 2].wait_recv()
+            u_side[2 * c - 1].wait_recv()
+            forward(c - 1)
     keep(wup, wup_out)
-
-    def forward(at, _):
-        r, c = spot_of(at)
-        value = matmul(normed[r, :], wup[:, c]) + up_bias_ref[member, :, c]
-        hidden[r, c] = gelu_value(value).astype(BF16)
-        du[r, c] = (dh[r, c] * gelu_slope(value)).astype(BF16)
-        return 0
-
-    lax.fori_loop(0, 2 * (deep // tile), forward, 0)
     keep(hidden, hidden_out)
     keep(du, du_out)
     for copy in arrivals:
@@ -470,8 +490,8 @@
             dma((stores,)),
             dma((15,)),
             dma((15,)),
-            dma((5,)),
-            dma((5,)),
+            dma((1 + 4 * (deep // 512),)),
+            dma((1 + 4 * (deep // 512),)),
             dma((6,)),
             dma((6,)),
             dma((items * shards,)),
@@ -663,6 +683,7 @@
     sin_in,
     back_in,
     down_out,
+    far_out,
     up_out,
     d_send,
     d_keep,
@@ -686,6 +707,7 @@
     place = lax.axis_index("ctx")
     shards = out.shape[1]
     x_at, z_at = place % 2, (place // 2) % 2
+    top_at = place // 4
     near, over = {"ctx": place ^ 1}, {"ctx": place ^ 2}
     barrier = pltpu.get_barrier_semaphore()
     for k in range(1, shards):
@@ -704,16 +726,18 @@
     members, tops, lanes, width = u_send.shape
     wide = lanes * 2 * tops
     units = d_send.shape[2]
-    piece = lanes // 2
 
     def down_one(top):
-        return remote(d_send.at[top], d_recv.at[top], ds_, dr, top, near)
-
-    def down_two(top):
-        return remote(d_send.at[top, 0], d_last.at[top], ds_, dr, tops + top, over)
+        spot = (1 - top_at) if top == 0 else top_at
+        return remote(d_send.at[spot], d_recv.at[spot], ds_, dr, top, near)
+
+    def down_two():
+        return remote(d_send.at[1 - top_at, 0], d_last, ds_, dr, tops, over)
 
     def up_one(member):
         return remote(u_send.at[member], u_recv.at[member], us, ur, member, over)
+
+    piece = lanes // 2
 
     def up_two(member):
         return remote(
@@ -757,7 +781,7 @@
             lax.fori_loop(0, 2, one, 0)
 
         for top in range(tops):
-            down(1 - x_at, d_send, top)
+            down(1 - x_at, d_send, (1 - top_at) if top == 0 else top_at)
             down_one(top).start()
         loads[2].wait()
         loads[3].wait()
@@ -919,55 +943,67 @@
         pltpu.VMEM((shards, size, LANES), F32),
     )
 
-    for top in range(tops):
-        down_one(top).wait()
-    for top in range(tops):
-        d_send[top, 0] = (
-            d_keep[top, 1 - z_at].astype(F32) + d_recv[top, 1 - z_at].astype(F32)
-        ).astype(BF16)
-        down_two(top).start()
+    stores = []
+
+    def keep(src, dst):
+        copy = pltpu.make_async_copy(src, dst, store_sem.at[len(stores)])
+        copy.start()
+        stores.append(copy)
+
     theirs = block((1 - x_at) * piece, piece)
     mine = block(x_at * piece, piece)
+    down_one(0).wait()
+    d_send[1 - top_at, 0] = (
+        d_keep[1 - top_at, 1 - z_at].astype(F32) + d_recv[1 - top_at, 1 - z_at].astype(F32)
+    ).astype(BF16)
+    down_two().start()
     for member in range(members):
         up_one(member).wait()
-    for member in range(members):
-        for top in range(tops):
+
+        def pass_up(top, _, member=member):
             u_send[member, top, pl.ds(0, piece)] = (
                 u_keep[member, top, theirs].astype(F32) + u_recv[member, top, theirs].astype(F32)
             ).astype(BF16)
+            return 0
+
+        lax.fori_loop(0, tops, pass_up, 0)
         up_two(member).start()
-    stores = []
-    for top in range(tops):
-        d_keep[top, z_at] = (
-            d_keep[top, z_at].astype(F32) + d_recv[top, z_at].astype(F32)
+    down_one(1).wait()
+
+    def add_down(low, _):
+        d_keep[top_at, low] = (
+            d_keep[top_at, low].astype(F32) + d_recv[top_at, low].astype(F32)
         ).astype(BF16)
-    for member in range(members):
-        for top in range(tops):
-            u_keep[member, top, mine] = (
-                u_keep[member, top, mine].astype(F32) + u_recv[member, top, mine].astype(F32)
-            ).astype(BF16)
-    for top in range(tops):
-        down_two(top).wait_recv()
-        d_last[top] = (d_keep[top, z_at].astype(F32) + d_last[top].astype(F32)).astype(BF16)
-        stores.append(pltpu.make_async_copy(d_last.at[top], down_out.at[top], store_sem.at[top]))
-        stores[-1].start()
+        return 0
+
+    lax.fori_loop(0, 2, add_down, 0)
+    keep(d_keep.at[top_at], down_out)
+    down_two().wait_recv()
+    d_last[...] = (
+        d_keep[1 - top_at, z_at].astype(F32)
+        + d_recv[1 - top_at, z_at].astype(F32)
+        + d_last[...].astype(F32)
+    ).astype(BF16)
+    keep(d_last, far_out)
     for member in range(members):
         up_two(member).wait_recv()
-        for top in range(tops):
+
+        def add_up(top, _, member=member):
             u_last[member, top] = (
-                u_keep[member, top, mine].astype(F32) + u_last[member, top].astype(F32)
+                u_keep[member, top, mine].astype(F32)
+                + u_recv[member, top, mine].astype(F32)
+                + u_last[member, top].astype(F32)
             ).astype(BF16)
-        stores.append(
-            pltpu.make_async_copy(u_last.at[member], up_out.at[member], store_sem.at[tops + member])
-        )
-        stores[-1].start()
+            return 0
+
+        lax.fori_loop(0, tops, add_up, 0)
+        keep(u_last.at[member], up_out.at[member])
     for item in range(items):
         for part in (1, 0):
             for k in range(1, shards):
                 back_one(item, part, k).wait()
             back_own(item, part).wait()
-    for top in range(tops):
-        down_two(top).wait_send()
+    down_two().wait_send()
     for member in range(members):
         up_two(member).wait_send()
     for copy in stores:
@@ -990,16 +1026,17 @@
         partial(middle_kernel, items, heads),
         out_shape=[
             shape((items, shards, 4, 2, half, LANES), BF16),
-            shape((tops, units, width), BF16),
+            shape((2, units, width), BF16),
+            shape((units, width), BF16),
             shape((groups, tops, lanes // 2, deep), BF16),
         ],
         in_specs=[apart] * 8,
-        out_specs=[apart] * 3,
+        out_specs=[apart] * 4,
         scratch_shapes=[
             pltpu.VMEM((tops, 2, units, width), BF16),
             pltpu.VMEM((tops, 2, units, width), BF16),
             pltpu.VMEM((tops, 2, units, width), BF16),
-            pltpu.VMEM((tops, units, width), BF16),
+            pltpu.VMEM((units, width), BF16),
             pltpu.VMEM((groups, tops, lanes, deep), BF16),
             pltpu.VMEM((groups, tops, lanes, deep), BF16),
             pltpu.VMEM((groups, tops, lanes, deep), BF16),
@@ -1008,8 +1045,8 @@
             dma((max(4, 2 * items + 2),)),
             dma((tops + groups,)),
             dma((2 * items,)),
-            dma((2 * tops,)),
-            dma((2 * tops,)),
+            dma((tops + 1,)),
+            dma((tops + 1,)),
             dma((2 * groups,)),
             dma((2 * groups,)),
             dma((2 * items * shards,)),
@@ -1043,6 +1080,7 @@
     outw_in,
     down_in,
     d_in,
+    far_in,
     u_in,
     x_in,
     cot_in,
@@ -1056,6 +1094,9 @@
     o_out,
     d_out,
     sums_out,
+    qkv_land,
+    up_land,
+    d_two,
     big,
     q_send,
     q_keep,
@@ -1123,8 +1164,14 @@
     def core(j):
         return {"fsdp": member ^ j}
 
+    theirs = block((1 - x_at) * piece, piece)
+    mine = block(x_at * piece, piece)
+
+    def d_second():
+        return flight("d2", d_in.at[1 - z_at], d_two, over)
+
     def d_last():
-        return flight("d", d_in.at[1 - top_at], d_three, far)
+        return flight("d", far_in, d_three, far)
 
     def u_last():
         return flight("u", u_in.at[:, 1 - top_at], u_three, far)
@@ -1148,10 +1195,10 @@
         return flight(("q3", f), q_send.at[f, 0, 1], q_three.at[f], far)
 
     def q_swap(j):
-        return flight(("q4", j), q_done.at[member ^ j], qkv_out.at[member], core(j))
+        return flight(("q4", j), q_done.at[member ^ j], qkv_land.at[member], core(j))
 
     def u_swap(j):
-        return flight(("u4", j), u_done.at[member ^ j], up_out.at[member], core(j))
+        return flight(("u4", j), u_done.at[member ^ j], up_land.at[member], core(j))
 
     def rows_last(name, send, recv):
         return flight((name, 3), send.at[0], recv.at[0], core(1))
@@ -1177,8 +1224,9 @@
         return flight(("s3", k), sums_out.at[:, mine], sums_out.at[:, mine], {"ctx": place ^ k})
 
     pl.semaphore_wait(barrier, groups - 1 + shards - 1)
+    d_second().start()
+    u_last().start()
     d_last().start()
-    u_last().start()
 
     def phase_a(normed, grads):
         loads = [fetch(normed_in, normed, 0), fetch(grads_in, grads, 1)]
@@ -1283,8 +1331,6 @@
 
     pass_rows("p", p_send, p_recv)
 
-    theirs = block((1 - x_at) * piece, piece)
-    mine = block(x_at * piece, piece)
     for top in range(tops):
         o_first(top).wait()
     for top in range(tops):
@@ -1313,7 +1359,6 @@
 
     for f in range(groups // 2):
         q_pass(f)
-
     def phase_c(du, wup, wqkv):
         loads = [
             fetch(du_in, du, 0),
@@ -1368,23 +1413,18 @@
     ).astype(BF16)
     o_last().start()
 
-    def phase_d(x, cot, out, d_own, d_sum, o_sum):
+    d_second().wait_recv()
+
+    def phase_d(x, cot, out, d_own, d_more, d_sum, o_sum, u_more, q_full, u_full):
         loads = [
             fetch(x_in, x, 0),
             fetch(cot_in, cot, 1),
             fetch(u_in.at[:, top_at], u_done, 2),
-            fetch(d_in.at[top_at], d_own, 3),
+            fetch(d_in.at[z_at], d_own, 3),
+            fetch(d_two, d_more, 4),
         ]
         for load in loads:
             load.wait()
-
-        u_last().wait_recv()
-        for f in range(groups):
-            u_done[f] = (u_done[f].astype(F32) + u_three[f].astype(F32)).astype(BF16)
-        for j in range(1, groups):
-            u_swap(j).start()
-        own_up = pltpu.make_async_copy(u_done.at[member], up_out.at[member], store_sem.at[0])
-        own_up.start()
 
         for f in range(groups // 2, groups):
             q_turn(f)
@@ -1432,13 +1472,22 @@
         own_out = pltpu.make_async_copy(out, result_out, store_sem.at[2])
         own_out.start()
 
+        u_last().wait_recv()
+        for f in range(groups):
+            u_done[f] = (
+                u_done[f].astype(F32) + u_three[f].astype(F32)
+            ).astype(BF16)
+        for j in range(1, groups):
+            u_swap(j).start()
+        u_full[:, block(member * deep, deep)] = u_done[member].astype(F32)
+
         for j in range(1, groups):
             sums_one(j).wait_recv()
         s_all[...] = sums[...] + s_recv[0] + s_recv[1] + s_recv[2]
         for k in range(1, shards):
             sums_two(k).start()
         d_last().wait_recv()
-        d_sum[...] = d_own[...].astype(F32) + d_three[...].astype(F32)
+        d_sum[...] = d_own[...].astype(F32) + d_more[...].astype(F32) + d_three[...].astype(F32)
         own_down = pltpu.make_async_copy(d_sum, d_out, store_sem.at[3])
         own_down.start()
 
@@ -1452,8 +1501,10 @@
             ).astype(BF16)
         for j in range(1, groups):
             q_swap(j).start()
-        own_q = pltpu.make_async_copy(q_done.at[member], qkv_out.at[member], store_sem.at[4])
-        own_q.start()
+        for kind in range(3):
+            q_full[:, block(kind * width + member * wide, wide)] = q_done[
+                member, :, kind * wide : (kind + 1) * wide
+            ].astype(F32)
         o_last().wait_recv()
         o_sum[...] = (
             o_keep[top_at, mine].astype(F32)
@@ -1472,7 +1523,33 @@
         sums_out[:, cols] = value
         for k in range(1, shards):
             sums_three(k).start()
-        for copy in (own_up, own_input, own_out, own_down, own_q, own_o):
+
+        for j in range(1, groups):
+            u_swap(j).wait_recv()
+        for copy in (own_input, own_out):
+            copy.wait()
+        u_loads = [
+            fetch(up_land.at[member ^ j], u_more.at[j], j) for j in range(1, groups)
+        ]
+        for j in range(1, groups):
+            u_loads[j - 1].wait()
+            u_full[:, block((member ^ j) * deep, deep)] = u_more[j].astype(F32)
+        own_up = pltpu.make_async_copy(u_full, up_out, store_sem.at[0])
+        own_up.start()
+        for j in range(1, groups):
+            q_swap(j).wait_recv()
+        q_loads = [
+            fetch(qkv_land.at[member ^ j], q_three.at[j], j) for j in range(1, groups)
+        ]
+        for j in range(1, groups):
+            q_loads[j - 1].wait()
+            for kind in range(3):
+                q_full[:, block(kind * width + (member ^ j) * wide, wide)] = q_three[
+                    j, :, kind * wide : (kind + 1) * wide
+                ].astype(F32)
+        own_q = pltpu.make_async_copy(q_full, qkv_out, store_sem.at[4])
+        own_q.start()
+        for copy in (own_up, own_down, own_q, own_o):
             copy.wait()
 
     pl.run_scoped(
@@ -1480,20 +1557,25 @@
         pltpu.VMEM((rows, width), BF16),
         pltpu.VMEM((rows, width), BF16),
         pltpu.VMEM((rows, width), BF16),
-        pltpu.VMEM(d_in.shape[1:], BF16),
-        pltpu.VMEM(d_in.shape[1:], F32),
+        pltpu.VMEM(d_three.shape, BF16),
+        pltpu.VMEM(d_three.shape, BF16),
+        pltpu.VMEM(d_three.shape, F32),
         pltpu.VMEM((piece, width), F32),
-    )
+        pltpu.VMEM(u_done.shape, BF16),
+        pltpu.VMEM((piece, 3 * width), F32),
+        pltpu.VMEM((piece, groups * deep), F32),
+    )
+    d_second().wait_send()
+    u_last().wait_send()
     d_last().wait_send()
-    u_last().wait_send()
     o_second().wait_send()
     o_last().wait_send()
     for f in range(groups):
         q_second(f).wait_send()
         q_last(f).wait_send()
     for j in range(1, groups):
-        q_swap(j).wait()
-        u_swap(j).wait()
+        q_swap(j).wait_send()
+        u_swap(j).wait_send()
         sums_one(j).wait_send()
     for name, send, recv in (("p", p_send, p_recv), ("n", n_send, n_recv)):
         rows_last(name, send, recv).wait_send()
@@ -1504,7 +1586,7 @@
 
 
 def finish(
-    back_in, normed, grads, hidden, du, wqkv, wup, outw, down, d_sum, u_sum,
+    back_in, normed, grads, hidden, du, wqkv, wup, outw, down, d_sum, far_sum, u_sum,
     x, cot, gain, out_bias, down_bias, groups, slot_groups,
 ):
     items, shards = back_in.shape[:2]
@@ -1524,14 +1606,17 @@
         out_shape=[
             shape((rows, width), BF16),
             shape((rows, width), BF16),
-            shape((groups, piece, 3 * wide), BF16),
-            shape((groups, piece, deep), BF16),
+            shape((piece, 3 * width), F32),
+            shape((piece, groups * deep), F32),
             shape((piece, width), F32),
             shape((units, width), F32),
             shape((16, width), F32),
+            shape((groups, piece, 3 * wide), BF16),
+            shape((groups, piece, deep), BF16),
+            shape((units, width), BF16),
         ],
-        in_specs=[apart] * 13 + [whole] * 3,
-        out_specs=[apart] * 6 + [whole],
+        in_specs=[apart] * 14 + [whole] * 3,
+        out_specs=[apart] * 6 + [whole] + [apart] * 3,
         scratch_shapes=[
             pltpu.VMEM((rows * groups, 4 * wide), BF16),
             pltpu.VMEM((groups, tops, 2, piece, 3 * wide), BF16),
@@ -1572,7 +1657,7 @@
             transcendentals=0,
         ),
     )(
-        back_in, normed, grads, hidden, du, wqkv, wup, outw, down, d_sum, u_sum, x, cot,
+        back_in, normed, grads, hidden, du, wqkv, wup, outw, down, d_sum, far_sum, u_sum, x, cot,
         gain.reshape(1, width), out_bias.reshape(1, width), down_bias.reshape(1, width),
     )
 
@@ -1681,7 +1766,7 @@
 
     hw = deep // shards
     if len(x_first) == 3 and dup == 1:
-        back_in, down_sum, up_sum = middle(
+        back_in, down_sum, far_sum, up_sum = middle(
             qkv_in.reshape(per_group, shards, 3, 2, half, LANES),
             grad_in.reshape(shards, per_group, 2, half, LANES),
             hidden,
@@ -1693,7 +1778,16 @@
             heads,
             groups,
         )
-        result, input_grad, qkv_parts, up_parts, out_weight_grad, down_weight_grad, sums = finish(
+        (
+            result,
+            input_grad,
+            qkv_weight_grad,
+            up_weight_grad,
+            out_weight_grad,
+            down_weight_grad,
+            sums,
+            *_,
+        ) = finish(
             back_in.reshape(per_group, shards, 4, rows, LANES),
             normed,
             grads,
@@ -1704,6 +1798,7 @@
             out_weight,
             down_weight,
             down_sum,
+            far_sum,
             up_sum,
             inputs[0],
             grad_low,
@@ -1713,20 +1808,16 @@
             groups,
             slot_groups,
         )
-        ow = wide // shards
         return (
             result[None],
             input_grad[None],
             sums[0],
             sums[1],
-            qkv_parts.reshape(groups, ow, 3, wide)
-            .transpose(1, 2, 0, 3)
-            .reshape(ow, 3 * width)
-            .astype(F32),
+            qkv_weight_grad,
             sums[2:5].reshape(-1),
             out_weight_grad,
             sums[9],
-            up_parts.transpose(1, 0, 2).reshape(ow, hidden_width).astype(F32),
+            up_weight_grad,
             sums[5 : 5 + groups].reshape(-1),
             down_weight_grad,
             sums[9],

time: 610 us -> 583 us (0.956)
  Pallas kernels: 581 us -> 556 us
    pallas_call x1, Pallas kernels: 217 us -> 193 us  [middle(): pl.pallas_call(partial(middle_kernel, items, heads), out_shape=[shape((it...]
    pallas_call x1, Pallas kernels: 191 us -> 176 us  [begin_layer(): pl.pallas_call(partial(start_kernel, shards, groups, pairs, slot_groups,...]
    pallas_call x1, Pallas kernels: 174 us -> 187 us  [finish(): pl.pallas_call(partial(finish_kernel, items, pairs, slot_groups), out_sha...]
    convert_element_type x4 -> x0, local copies, waits for them, and re-layouts: 9.58 us -> none  [the longest x3 8.11 us: on_device(): return (result[None], input_grad[None], sums[0], sums[1], qkv_parts.resha...]
where the time goes in v5:
time: 583 us; the launch traced here: 572 us
  Pallas kernels  556 us (95%)
  local copies, waits for them, and re-layouts  14.6 us (3%)
    pallas_call x1, Pallas kernels, middle(): pl.pallas_call(partial(middle_kernel, items, heads), out_shape=[shape((it...  193 us
    pallas_call x1, Pallas kernels, finish(): pl.pallas_call(partial(finish_kernel, items, pairs, slot_groups), out_sha...  187 us
    pallas_call x1, Pallas kernels, begin_layer(): pl.pallas_call(partial(start_kernel, shards, groups, pairs, slot_groups,...  176 us

profile of v5, /device:TPU:0, one launch (start us, length us, event | category | flops | bytes accessed | tf_op | source)
XLA Modules:
  0.0 572.2 jit_solution(4112950815902018544)
XLA Ops:
  0.6 175.8 %shard_map.229 = (bf16[1024,2048]{1,0:T(8,128)(2,1)}, bf16[1024,2048]{1,0:T(8,128)(2,1)}, bf16[2048,1536]{1,0:T(8,128)(2,1)}, bf16[2048,2048]{1,0:T(8,128)(2,1)}...) custom-call(bf16[256,2048]{1,0:T(8,128)(2,1)} %bitcast.26, ...), custom_call_target="tpu_custom_call" | custom-call | flops 25769803776 | bytes 62914560 | tf_op jit(solution)/shard_map/pallas_call | solution.py:461
  176.4 193.4 %shard_map.230 = (bf16[2,8,4,2,128,128]{5,4,3,2,1,0:T(8,128)(2,1)}, bf16[2,256,2048]{2,1,0:T(8,128)(2,1)}, bf16[256,2048]{1,0:T(8,128)(2,1)}, bf16[4,2,64,2048]{3,2,1,0:T(8,128)(2,1)}) custom-call(bf16[2,8,3,2,128,128]{5,4,3,2,1,0:T(8,128)(2,1)} %bitcast.38, bf16[8,2,2,128,128]{4,3,2,1,0:T(8,128)(2,1)} %bitcast.39, ...), custom_call_target="tpu_custom_call" | custom-call | flops 58518929408 | bytes 41943040 | tf_op jit(solution)/shard_map/pallas_call | solution.py:1025
  369.9 187.2 %shard_map.231 = (bf16[256,2048]{1,0:T(8,128)(2,1)}, bf16[256,2048]{1,0:T(8,128)(2,1)}, f32[64,6144]{1,0:T(8,128)}, f32[64,8192]{1,0:T(8,128)}, f32[64,2048]{1,0...) custom-call(bf16[2,8,4,256,128]{4,3,2,1,0:T(8,128)(2,1)} %bitcast.37, ...), custom_call_target="tpu_custom_call" | custom-call | flops 34359738368 | bytes 62914560 | tf_op jit(solution)/shard_map/pallas_call | solution.py:1604
  557.1 0.0 copy-start.2
  557.1 0.0 copy-start.3
  557.1 1.7 fusion
  558.7 0.0 copy-start.4
  558.7 0.9 slice.18
  559.6 0.9 slice_bitcast_fusion
  560.5 0.6 reshape.67
  561.1 0.6 copy.26
  561.8 0.6 copy.34
  562.4 0.0 copy-start.1
  562.4 2.5 copy.35
  564.8 2.3 copy.36
  567.1 0.0 copy-done.2
  567.1 0.0 copy-start
  567.1 1.1 copy.37
  568.3 0.0 copy-done.3
  568.3 0.8 copy.38
  569.1 0.0 copy-done.4
  569.1 0.0 copy-done.1
  569.1 1.3 copy.39
  570.4 0.0 copy-done
  570.4 1.3 copy.40
Async XLA Ops:
  557.1 10.1 %copy-start.2 = (f32[64,6144]{1,0:T(8,128)S(1)}, f32[64,6144]{1,0:T(8,128)}, u32[]{:S(2)}) copy-start(f32[64,6144]{1,0:T(8,128)} %get-tuple-element.93) | copy-start | bytes 4718596
  557.1 11.2 %copy-start.3 = (f32[64,2048]{1,0:T(8,128)S(1)}, f32[64,2048]{1,0:T(8,128)}, u32[]{:S(2)}) copy-start(f32[64,2048]{1,0:T(8,128)} %get-tuple-element.95) | copy-start | bytes 1572868
  558.7 10.3 %copy-start.4 = (f32[1,2048]{1,0:T(1,128)}, f32[1,2048]{1,0:T(1,128)S(1)}, u32[]{:S(2)}) copy-start(f32[1,2048]{1,0:T(1,128)S(1)} %get-tuple-element.50) | copy-start | bytes 24580
  562.4 6.7 %copy-start.1 = (f32[64,8192]{1,0:T(8,128)S(1)}, f32[64,8192]{1,0:T(8,128)}, u32[]{:S(2)}) copy-start(f32[64,8192]{1,0:T(8,128)} %get-tuple-element.97) | copy-start | bytes 6291460
  567.1 3.3 copy-start

commit v6 on v5

--- a/solution.py
+++ b/solution.py
@@ -191,6 +191,10 @@
     pl.semaphore_wait(barrier, groups - 1 + shards - 1)
 
     half_rows = block(member * wide + side * part, part)
+    quarter = part // 2
+    level = (place // 2) % 2
+    own_quarter = (side * 2 + level) * quarter
+    next_quarter = ((1 - side) * 2 + level) * quarter
     started = []
 
     def begin(copy):
@@ -203,8 +207,10 @@
         for p in range(3):
             q_far[j, p] = begin(
                 remote(
-                    qkv_ref.at[block(side * part, part), block(p * width + (member ^ j) * wide, wide)],
-                    wqkv.at[half_rows, pl.ds(p * wide, wide)],
+                    qkv_ref.at[
+                        block(own_quarter, quarter), block(p * width + (member ^ j) * wide, wide)
+                    ],
+                    wqkv.at[block(member * wide + own_quarter, quarter), pl.ds(p * wide, wide)],
                     qs,
                     qr,
                     (j - 2) * 3 + p,
@@ -233,22 +239,35 @@
         for p in range(3)
     ]
 
-    q_side = []
+    q_side = {}
+    q_over = []
     for j in (2, 3):
         for p in range(3):
+            at = (j - 2) * 3 + p
             q_far[j, p].wait_recv()
-            spot = wqkv.at[block((member ^ j) * wide + side * part, part), pl.ds(p * wide, wide)]
-            q_side.append(
-                begin(remote(spot, spot, qs, qr, 9 + (j - 2) * 3 + p, {"ctx": place ^ 1}))
-            )
+            spot = wqkv.at[
+                block((member ^ j) * wide + own_quarter, quarter), pl.ds(p * wide, wide)
+            ]
+            q_side[j, p] = begin(remote(spot, spot, qs, qr, 9 + at, {"ctx": place ^ 1}))
+            q_over.append(begin(remote(spot, spot, qs, qr, 15 + at, {"ctx": place ^ 2})))
     n_far = begin(
         remote(
             normed.at[pl.ds(0, rows)], normed.at[pl.ds(2 * rows, rows)], rs, rr, 0, {"fsdp": member ^ 2}
         )
     )
+    for j in (2, 3):
+        for p in range(3):
+            q_side[j, p].wait_recv()
+            spot = wqkv.at[
+                block((member ^ j) * wide + next_quarter, quarter), pl.ds(p * wide, wide)
+            ]
+            q_over.append(
+                begin(remote(spot, spot, qs, qr, 21 + (j - 2) * 3 + p, {"ctx": place ^ 2}))
+            )
+
     for at in (0, 1, 2, 7, 8, 9, 10):
         loads[at].wait()
-    for copy in q_near + q_side:
+    for copy in q_near + q_over:
         copy.wait_recv()
     n_near.wait_recv()
     arrivals = []
@@ -488,8 +507,8 @@
             pltpu.VMEM((total, deep), BF16),
             dma((11,)),
             dma((stores,)),
-            dma((15,)),
-            dma((15,)),
+            dma((27,)),
+            dma((27,)),
             dma((1 + 4 * (deep // 512),)),
             dma((1 + 4 * (deep // 512),)),
             dma((6,)),
@@ -1224,9 +1243,8 @@
         return flight(("s3", k), sums_out.at[:, mine], sums_out.at[:, mine], {"ctx": place ^ k})
 
     pl.semaphore_wait(barrier, groups - 1 + shards - 1)
+    u_last().start()
     d_second().start()
-    u_last().start()
-    d_last().start()
 
     def phase_a(normed, grads):
         loads = [fetch(normed_in, normed, 0), fetch(grads_in, grads, 1)]
@@ -1359,6 +1377,8 @@
 
     for f in range(groups // 2):
         q_pass(f)
+    d_last().start()
+
     def phase_c(du, wup, wqkv):
         loads = [
             fetch(du_in, du, 0),
@@ -1413,15 +1433,12 @@
     ).astype(BF16)
     o_last().start()
 
-    d_second().wait_recv()
-
     def phase_d(x, cot, out, d_own, d_more, d_sum, o_sum, u_more, q_full, u_full):
         loads = [
             fetch(x_in, x, 0),
             fetch(cot_in, cot, 1),
             fetch(u_in.at[:, top_at], u_done, 2),
             fetch(d_in.at[z_at], d_own, 3),
-            fetch(d_two, d_more, 4),
         ]
         for load in loads:
             load.wait()
@@ -1486,11 +1503,6 @@
         s_all[...] = sums[...] + s_recv[0] + s_recv[1] + s_recv[2]
         for k in range(1, shards):
             sums_two(k).start()
-        d_last().wait_recv()
-        d_sum[...] = d_own[...].astype(F32) + d_more[...].astype(F32) + d_three[...].astype(F32)
-        own_down = pltpu.make_async_copy(d_sum, d_out, store_sem.at[3])
-        own_down.start()
-
         for f in range(groups):
             q_last(f).wait_recv()
             q_done[f] = (
@@ -1523,6 +1535,13 @@
         sums_out[:, cols] = value
         for k in range(1, shards):
             sums_three(k).start()
+
+        d_last().wait_recv()
+        d_second().wait_recv()
+        fetch(d_two, d_more, 4).wait()
+        d_sum[...] = d_own[...].astype(F32) + d_more[...].astype(F32) + d_three[...].astype(F32)
+        own_down = pltpu.make_async_copy(d_sum, d_out, store_sem.at[3])
+        own_down.start()
 
         for j in range(1, groups):
             u_swap(j).wait_recv()

time: 583 us -> 563 us (0.966)
  Pallas kernels: 556 us -> 537 us
    pallas_call x1, Pallas kernels: 176 us -> 162 us  [begin_layer(): pl.pallas_call(partial(start_kernel, shards, groups, pairs, slot_groups,...]
    pallas_call x1, Pallas kernels: 187 us -> 177 us  [finish(): pl.pallas_call(partial(finish_kernel, items, pairs, slot_groups), out_sha...]
where the time goes in v6:
time: 563 us; the launch traced here: 552 us
  Pallas kernels  537 us (95%)
  local copies, waits for them, and re-layouts  14.6 us (3%)
    pallas_call x1, Pallas kernels, middle(): pl.pallas_call(partial(middle_kernel, items, heads), out_shape=[shape((it...  198 us
    pallas_call x1, Pallas kernels, finish(): pl.pallas_call(partial(finish_kernel, items, pairs, slot_groups), out_sha...  177 us
    pallas_call x1, Pallas kernels, begin_layer(): pl.pallas_call(partial(start_kernel, shards, groups, pairs, slot_groups,...  162 us
    unnamed x19, local copies, waits for them, and re-layouts  11.5 us

profile of v6, /device:TPU:0, one launch (start us, length us, event | category | flops | bytes accessed | tf_op | source)
XLA Modules:
  0.0 552.4 jit_solution(11347925447323656194)
XLA Ops:
  0.6 162.3 %shard_map.229 = (bf16[1024,2048]{1,0:T(8,128)(2,1)}, bf16[1024,2048]{1,0:T(8,128)(2,1)}, bf16[2048,1536]{1,0:T(8,128)(2,1)}, bf16[2048,2048]{1,0:T(8,128)(2,1)}...) custom-call(bf16[256,2048]{1,0:T(8,128)(2,1)} %bitcast.26, ...), custom_call_target="tpu_custom_call" | custom-call | flops 25769803776 | bytes 62914560 | tf_op jit(solution)/shard_map/pallas_call | solution.py:480
  163.0 197.6 %shard_map.230 = (bf16[2,8,4,2,128,128]{5,4,3,2,1,0:T(8,128)(2,1)}, bf16[2,256,2048]{2,1,0:T(8,128)(2,1)}, bf16[256,2048]{1,0:T(8,128)(2,1)}, bf16[4,2,64,2048]{3,2,1,0:T(8,128)(2,1)}) custom-call(bf16[2,8,3,2,128,128]{5,4,3,2,1,0:T(8,128)(2,1)} %bitcast.38, bf16[8,2,2,128,128]{4,3,2,1,0:T(8,128)(2,1)} %bitcast.39, ...), custom_call_target="tpu_custom_call" | custom-call | flops 58518929408 | bytes 41943040 | tf_op jit(solution)/shard_map/pallas_call | solution.py:1044
  360.6 176.7 %shard_map.231 = (bf16[256,2048]{1,0:T(8,128)(2,1)}, bf16[256,2048]{1,0:T(8,128)(2,1)}, f32[64,6144]{1,0:T(8,128)}, f32[64,8192]{1,0:T(8,128)}, f32[64,2048]{1,0...) custom-call(bf16[2,8,4,256,128]{4,3,2,1,0:T(8,128)(2,1)} %bitcast.37, ...), custom_call_target="tpu_custom_call" | custom-call | flops 34359738368 | bytes 62914560 | tf_op jit(solution)/shard_map/pallas_call | solution.py:1623
  537.3 0.0 copy-start.2
  537.3 0.0 copy-start.3
  537.3 1.7 fusion
  539.0 0.0 copy-start.4
  539.0 0.9 slice.18
  539.8 0.9 slice_bitcast_fusion
  540.8 0.6 reshape.67
  541.4 0.6 copy.26
  542.0 0.6 copy.34
  542.6 0.0 copy-start.1
  542.6 2.5 copy.35
  545.1 2.3 copy.36
  547.4 0.0 copy-done.2
  547.4 0.0 copy-start
  547.4 1.1 copy.37
  548.5 0.0 copy-done.3
  548.5 0.8 copy.38
  549.3 0.0 copy-done.4
  549.3 0.0 copy-done.1
  549.3 1.3 copy.39
  550.6 0.0 copy-done
  550.6 1.3 copy.40
Async XLA Ops:
  537.3 10.1 %copy-start.2 = (f32[64,6144]{1,0:T(8,128)S(1)}, f32[64,6144]{1,0:T(8,128)}, u32[]{:S(2)}) copy-start(f32[64,6144]{1,0:T(8,128)} %get-tuple-element.93) | copy-start | bytes 4718596
  537.3 11.2 %copy-start.3 = (f32[64,2048]{1,0:T(8,128)S(1)}, f32[64,2048]{1,0:T(8,128)}, u32[]{:S(2)}) copy-start(f32[64,2048]{1,0:T(8,128)} %get-tuple-element.95) | copy-start | bytes 1572868
  539.0 10.3 %copy-start.4 = (f32[1,2048]{1,0:T(1,128)}, f32[1,2048]{1,0:T(1,128)S(1)}, u32[]{:S(2)}) copy-start(f32[1,2048]{1,0:T(1,128)S(1)} %get-tuple-element.50) | copy-start | bytes 24580
  542.6 6.7 %copy-start.1 = (f32[64,8192]{1,0:T(8,128)S(1)}, f32[64,8192]{1,0:T(8,128)}, u32[]{:S(2)}) copy-start(f32[64,8192]{1,0:T(8,128)} %get-tuple-element.97) | copy-start | bytes 6291460
  547.4 3.3 copy-start

commit v7 on v6

--- a/solution.py
+++ b/solution.py
@@ -1681,6 +1681,55 @@
     )
 
 
+def deliver_kernel(count, groups, *refs):
+    arrays, sums = refs[:count], refs[count]
+    outs = refs[count + 1 : 2 * count + 1]
+    gain, shift, qkv_bias, out_bias, up_bias, down_bias = refs[2 * count + 1 : 2 * count + 7]
+    held = refs[2 * count + 7 : 3 * count + 7]
+    sem = refs[-1]
+    loads = [
+        pltpu.make_async_copy(src, dst, sem.at[at]) for at, (src, dst) in enumerate(zip(arrays, held))
+    ]
+    copies = [
+        pltpu.make_async_copy(src, dst, sem.at[count + at])
+        for at, (src, dst) in enumerate(zip(held, outs))
+    ]
+    for load in loads:
+        load.start()
+    for load, copy in zip(loads, copies):
+        load.wait()
+        copy.start()
+    width = sums.shape[1]
+    gain[...] = sums[0, :]
+    shift[...] = sums[1, :]
+    out_bias[...] = sums[9, :]
+    down_bias[...] = sums[9, :]
+    for row in range(3):
+        qkv_bias[row * width : (row + 1) * width] = sums[2 + row, :]
+    for row in range(groups):
+        up_bias[row * width : (row + 1) * width] = sums[5 + row, :]
+    for copy in copies:
+        copy.wait()
+
+
+def deliver(arrays, sums, groups):
+    width = sums.shape[1]
+    apart = pl.BlockSpec(memory_space=pl.ANY)
+    whole = pl.BlockSpec(memory_space=pltpu.VMEM)
+    flat = [width, width, 3 * width, width, groups * width, width]
+    return pl.pallas_call(
+        partial(deliver_kernel, len(arrays), groups),
+        out_shape=[jax.ShapeDtypeStruct(item.shape, item.dtype) for item in arrays]
+        + [jax.ShapeDtypeStruct((size,), F32) for size in flat],
+        in_specs=[apart] * len(arrays) + [whole],
+        out_specs=[apart] * len(arrays) + [whole] * 6,
+        scratch_shapes=[pltpu.VMEM(item.shape, item.dtype) for item in arrays]
+        + [pltpu.SemaphoreType.DMA((2 * len(arrays),))],
+        compiler_params=pltpu.CompilerParams(vmem_limit_bytes=60 * 2**20),
+        cost_estimate=pl.CostEstimate(flops=0, bytes_accessed=20 * 2**20, transcendentals=0),
+    )(*arrays, sums)
+
+
 def scatter_sum(parts, axis_at, place, bits):
     lead, tail = parts.shape[:axis_at], parts.shape[axis_at + 1 :]
     total = len(bits)
@@ -1827,19 +1876,44 @@
             groups,
             slot_groups,
         )
+        (
+            result,
+            input_grad,
+            qkv_weight_grad,
+            up_weight_grad,
+            out_weight_grad,
+            down_weight_grad,
+            gain_grad,
+            shift_grad,
+            qkv_bias_grad,
+            out_bias_grad,
+            up_bias_grad,
+            down_bias_grad,
+        ) = deliver(
+            (
+                result,
+                input_grad,
+                qkv_weight_grad,
+                up_weight_grad,
+                out_weight_grad,
+                down_weight_grad,
+            ),
+            sums,
+            groups,
+        )
         return (
             result[None],
             input_grad[None],
-            sums[0],
-            sums[1],
+            gain_grad,
+            shift_grad,
             qkv_weight_grad,
-            sums[2:5].reshape(-1),
+            qkv_bias_grad,
             out_weight_grad,
-            sums[9],
+            out_bias_grad,
             up_weight_grad,
-            sums[5 : 5 + groups].reshape(-1),
+            up_bias_grad,
             down_weight_grad,
-            sums[9],
+            down_bias_grad,
         )
     else:
         down_grad = contract_rows(hidden, grads).astype(BF16)

time: 563 us -> 556 us (0.988)
  local copies, waits for them, and re-layouts: 14.6 us -> 0 us
  Pallas kernels: 537 us -> 544 us
    unnamed x19 -> x0, local copies, waits for them, and re-layouts: 11.5 us -> none
    pallas_call x0 -> x1, Pallas kernels: none -> 7.78 us  [deliver(): pl.pallas_call(partial(deliver_kernel, len(arrays), groups), out_shape=[j...]
where the time goes in v7:
time: 556 us; the launch traced here: 545 us
  Pallas kernels  544 us (98%)
    pallas_call x1, Pallas kernels, middle(): pl.pallas_call(partial(middle_kernel, items, heads), out_shape=[shape((it...  198 us
    pallas_call x1, Pallas kernels, finish(): pl.pallas_call(partial(finish_kernel, items, pairs, slot_groups), out_sha...  177 us
    pallas_call x1, Pallas kernels, begin_layer(): pl.pallas_call(partial(start_kernel, shards, groups, pairs, slot_groups,...  162 us

profile of v7, /device:TPU:0, one launch (start us, length us, event | category | flops | bytes accessed | tf_op | source)
XLA Modules:
  0.0 545.4 jit_solution(4582188657084142741)
XLA Ops:
  0.6 162.3 %shard_map.229 = (bf16[1024,2048]{1,0:T(8,128)(2,1)}, bf16[1024,2048]{1,0:T(8,128)(2,1)}, bf16[2048,1536]{1,0:T(8,128)(2,1)}, bf16[2048,2048]{1,0:T(8,128)(2,1)}...) custom-call(bf16[256,2048]{1,0:T(8,128)(2,1)} %bitcast.13, ...), custom_call_target="tpu_custom_call" | custom-call | flops 25769803776 | bytes 62914560 | tf_op jit(solution)/shard_map/pallas_call | solution.py:480
  163.0 197.6 %shard_map.230 = (bf16[2,8,4,2,128,128]{5,4,3,2,1,0:T(8,128)(2,1)}, bf16[2,256,2048]{2,1,0:T(8,128)(2,1)}, bf16[256,2048]{1,0:T(8,128)(2,1)}, bf16[4,2,64,2048]{3,2,1,0:T(8,128)(2,1)}) custom-call(bf16[2,8,3,2,128,128]{5,4,3,2,1,0:T(8,128)(2,1)} %bitcast.27, bf16[8,2,2,128,128]{4,3,2,1,0:T(8,128)(2,1)} %bitcast.28, ...), custom_call_target="tpu_custom_call" | custom-call | flops 58518929408 | bytes 41943040 | tf_op jit(solution)/shard_map/pallas_call | solution.py:1044
  360.6 176.6 %shard_map.231 = (bf16[256,2048]{1,0:T(8,128)(2,1)}, bf16[256,2048]{1,0:T(8,128)(2,1)}, f32[64,6144]{1,0:T(8,128)}, f32[64,8192]{1,0:T(8,128)}, f32[64,2048]{1,0...) custom-call(bf16[2,8,4,256,128]{4,3,2,1,0:T(8,128)(2,1)} %bitcast.26, ...), custom_call_target="tpu_custom_call" | custom-call | flops 34359738368 | bytes 62914560 | tf_op jit(solution)/shard_map/pallas_call | solution.py:1623
  537.2 7.8 %shard_map.232 = (bf16[256,2048]{1,0:T(8,128)(2,1)}, bf16[256,2048]{1,0:T(8,128)(2,1)}, f32[64,6144]{1,0:T(8,128)}, f32[64,8192]{1,0:T(8,128)}, f32[64,2048]{1,0...) custom-call(bf16[256,2048]{1,0:T(8,128)(2,1)} %get-tuple-element.55., ...), custom_call_target="tpu_custom_call" | custom-call | bytes 20971520 | tf_op jit(solution)/shard_map/pallas_call | solution.py:1720
